TPU v7x, 32 devices: a whole 2x2x4 slice. The times are simulated.
32 devices in a mesh: seq: 8 (over z, y), ch: 4 (over x, core).
Axes of the slice: x: 2, y: 2, z: 4, core: 2. Of those that a mesh axis runs over, the one named last changes fastest.
Arguments:
- hidden: bfloat16 [3, 8192, 1536], P(None, 'seq'), may hold values from -6 to 6
- gain_in: float32 [1536], replicated, may hold values from 0.5 to 1.5
- in_weight: bfloat16 [1536, 3, 1536], P(None, None, 'ch'), may hold values from -0.15625 to 0.15625
- conv_weight: bfloat16 [3, 1536], P(None, 'ch'), may hold values from -3 to 3
- out_weight: bfloat16 [1536, 1536], P(None, 'ch'), may hold values from -0.15625 to 0.15625
- gain_mid: float32 [1536], replicated, may hold values from 0.5 to 1.5
- gate_up_weight: bfloat16 [1536, 2, 6912], P(None, None, 'ch'), may hold values from -0.15625 to 0.15625
- down_weight: bfloat16 [1536, 6912], P(None, 'ch'), may hold values from -0.078125 to 0.078125
- cotangent: bfloat16 [3, 8192, 1536], P(None, 'seq'), may hold values from -6 to 6
Outputs:
- block_out: bfloat16 [3, 8192, 1536], P(None, ('seq', 'ch'))
- input_grad: bfloat16 [3, 8192, 1536], P(None, ('seq', 'ch'))
- gain_in_grad: float32 [1536], replicated
- in_weight_grad: float32 [1536, 3, 1536], P('seq', None, 'ch')
- conv_weight_grad: float32 [3, 1536], replicated
- out_weight_grad: float32 [1536, 1536], P('seq', 'ch')
- gain_mid_grad: float32 [1536], replicated
- gate_up_grad: float32 [1536, 2, 6912], P('seq', None, 'ch')
- down_grad: float32 [1536, 6912], P('seq', 'ch')
All inputs are finite; a program needn't handle non-finite values.
Results may differ from a plain program's by a relative error of at most 0.017.
Values may be sent and summed in bfloat16 or wider, within the bound.
No kernel may reach another device: no remote copies, remote signals or barrier semaphores. Data moves between devices by JAX's collectives and lax.ppermute only.
A program may use at most 320 MiB of HBM per device.

v0:
```python
import jax
import jax.numpy as jnp
from jax import lax
from jax.sharding import PartitionSpec as P

EPS = 1e-05


def shifted(value, axis, steps):
    count = lax.axis_size(axis)
    first, last = (max(0, -steps), min(count, count - steps))
    return lax.ppermute(value, axis, [(source, source + steps) for source in range(first, last)])


def norm_scale(rows):
    return lax.rsqrt(jnp.mean(rows * rows, axis=-1, keepdims=True) + EPS)


def norm_back(rows, scale, gain, grad):
    weighted = grad * gain
    inner = jnp.mean(weighted * rows, axis=-1, keepdims=True)
    d_rows = scale * weighted - rows * (scale * scale * scale) * inner
    d_gain = jnp.sum(grad * rows * scale, axis=0)
    return (d_rows, d_gain)


def per_device(
    hidden,
    gain_in,
    in_weight,
    conv_weight,
    out_weight,
    gain_mid,
    gate_up_weight,
    down_weight,
    cotangent,
):
    seqs, length, width = hidden.shape
    parts = lax.axis_size("ch")
    share = length // parts
    first = lax.axis_index("ch") * share
    taps = conv_weight.shape[0]
    chans = conv_weight.shape[1]
    conv_taps = conv_weight.astype(jnp.float32)
    zero_grads = (
        jnp.zeros(in_weight.shape, jnp.float32),
        jnp.zeros(out_weight.shape, jnp.float32),
        jnp.zeros(gate_up_weight.shape, jnp.float32),
        jnp.zeros(down_weight.shape, jnp.float32),
    )
    totals = zero_grads
    pieces = None
    gain_in_acc = jnp.zeros((width,), jnp.float32)
    gain_mid_acc = jnp.zeros((width,), jnp.float32)
    conv_acc = jnp.zeros((taps, chans), jnp.float32)
    outs_rows = []
    outs_grads = []
    for seq_index in range(seqs):
        rows = hidden[seq_index].astype(jnp.float32)
        scale_in = norm_scale(rows)
        normed = (rows * scale_in * gain_in).astype(jnp.bfloat16)
        proj = jnp.einsum("td,dkc->tkc", normed, in_weight, preferred_element_type=jnp.float32)
        b_gate = proj[:, 0]
        c_gate = proj[:, 1]
        x_val = proj[:, 2]
        gated = (b_gate * x_val).astype(jnp.bfloat16)
        before = shifted(gated[length - (taps - 1) :], "seq", 1)
        padded = jnp.concatenate([before, gated], axis=0).astype(jnp.float32)
        conv = jnp.zeros((length, chans), jnp.float32)
        for tap in range(taps):
            conv = conv + conv_taps[tap] * padded[tap : tap + length]
        mixed = (c_gate * conv).astype(jnp.bfloat16)
        mix_part = lax.dot_general(
            mixed, out_weight, (((1,), (1,)), ((), ())), preferred_element_type=jnp.float32
        )
        own_rows = lax.dynamic_slice_in_dim(rows, first, share, 0)
        own_scale = lax.dynamic_slice_in_dim(scale_in, first, share, 0)
        mix_share = lax.psum_scatter(mix_part, "ch", scatter_dimension=0, tiled=True)
        resid = own_rows + mix_share
        scale_mid = norm_scale(resid)
        normed_share = (resid * scale_mid * gain_mid).astype(jnp.bfloat16)
        normed2 = lax.all_gather(normed_share, "ch", axis=0, tiled=True)
        gate_up = jnp.einsum(
            "td,dkf->tkf", normed2, gate_up_weight, preferred_element_type=jnp.float32
        )
        gate_val = gate_up[:, 0]
        up_val = gate_up[:, 1]
        sigm = jax.nn.sigmoid(gate_val)
        silu_val = gate_val * sigm
        act = (silu_val * up_val).astype(jnp.bfloat16)
        ffn_part = lax.dot_general(
            act, down_weight, (((1,), (1,)), ((), ())), preferred_element_type=jnp.float32
        )
        ffn_share = lax.psum_scatter(
            ffn_part.astype(jnp.bfloat16), "ch", scatter_dimension=0, tiled=True
        ).astype(jnp.float32)
        outs_rows.append((resid + ffn_share).astype(jnp.bfloat16))
        grad_out = cotangent[seq_index]
        d_down = jnp.einsum("td,tf->df", grad_out, act, preferred_element_type=jnp.float32)
        d_act = jnp.dot(grad_out, down_weight, preferred_element_type=jnp.float32)
        d_gate = d_act * up_val * sigm * (1.0 + gate_val * (1.0 - sigm))
        d_up = d_act * silu_val
        d_gu = jnp.stack([d_gate, d_up], axis=1).astype(jnp.bfloat16)
        d_gate_up = jnp.einsum("td,tkf->dkf", normed2, d_gu, preferred_element_type=jnp.float32)
        d_mid_part = jnp.einsum(
            "tkf,dkf->td", d_gu, gate_up_weight, preferred_element_type=jnp.float32
        )
        d_mid = lax.psum_scatter(
            d_mid_part.astype(jnp.bfloat16), "ch", scatter_dimension=0, tiled=True
        ).astype(jnp.float32)
        d_resid_norm, gain_mid_term = norm_back(resid, scale_mid, gain_mid, d_mid)
        d_resid = (
            lax.dynamic_slice_in_dim(grad_out, first, share, 0).astype(jnp.float32) + d_resid_norm
        )
        d_mix = lax.all_gather(d_resid.astype(jnp.bfloat16), "ch", axis=0, tiled=True)
        d_out_w = jnp.einsum("te,tc->ec", d_mix, mixed, preferred_element_type=jnp.float32)
        d_mixed = jnp.dot(d_mix, out_weight, preferred_element_type=jnp.float32)
        d_c = d_mixed * conv
        d_conv = d_mixed * c_gate
        d_padded = jnp.zeros((length + taps - 1, chans), jnp.float32)
        conv_terms = []
        for tap in range(taps):
            conv_terms.append(jnp.sum(d_conv * padded[tap : tap + length], axis=0))
            d_padded = d_padded + jnp.pad(conv_taps[tap] * d_conv, ((tap, taps - 1 - tap), (0, 0)))
        conv_acc = conv_acc + jnp.stack(conv_terms, axis=0)
        after = shifted(d_padded[: taps - 1], "seq", -1)
        d_gated = d_padded[taps - 1 :] + jnp.pad(after, ((length - (taps - 1), 0), (0, 0)))
        d_gated_low = d_gated.astype(jnp.bfloat16).astype(jnp.float32)
        d_proj = jnp.stack([d_gated_low * x_val, d_c, d_gated_low * b_gate], axis=1).astype(
            jnp.bfloat16
        )
        d_in_w = jnp.einsum("td,tkc->dkc", normed, d_proj, preferred_element_type=jnp.float32)
        d_in_part = jnp.einsum("tkc,dkc->td", d_proj, in_weight, preferred_element_type=jnp.float32)
        d_in = lax.psum_scatter(
            d_in_part.astype(jnp.bfloat16), "ch", scatter_dimension=0, tiled=True
        ).astype(jnp.float32)
        d_rows_norm, gain_in_term = norm_back(own_rows, own_scale, gain_in, d_in)
        outs_grads.append((d_resid + d_rows_norm).astype(jnp.bfloat16))
        gain_in_acc = gain_in_acc + gain_in_term
        gain_mid_acc = gain_mid_acc + gain_mid_term
        totals = (
            totals[0] + d_in_w,
            totals[1] + d_out_w,
            totals[2] + d_gate_up,
            totals[3] + d_down,
        )
    pieces = (
        lax.psum_scatter(
            totals[0].astype(jnp.bfloat16), "seq", scatter_dimension=0, tiled=True
        ).astype(jnp.float32),
        lax.psum_scatter(
            totals[1].astype(jnp.bfloat16), "seq", scatter_dimension=0, tiled=True
        ).astype(jnp.float32),
        lax.psum_scatter(
            totals[2].astype(jnp.bfloat16), "seq", scatter_dimension=0, tiled=True
        ).astype(jnp.float32),
        lax.psum_scatter(
            totals[3].astype(jnp.bfloat16), "seq", scatter_dimension=0, tiled=True
        ).astype(jnp.float32),
    )
    conv_full = lax.dynamic_update_slice_in_dim(
        jnp.zeros((taps, width), jnp.float32), conv_acc, lax.axis_index("ch") * chans, 1
    )
    conv_grad, gain_in_grad, gain_mid_grad = lax.psum(
        (conv_full, gain_in_acc, gain_mid_acc), ("seq", "ch")
    )
    block_out = jnp.stack(outs_rows, axis=0)
    input_grad = jnp.stack(outs_grads, axis=0)
    return (
        block_out,
        input_grad,
        gain_in_grad,
        pieces[0],
        conv_grad,
        pieces[1],
        gain_mid_grad,
        pieces[2],
        pieces[3],
    )


def solution(mesh):
    placed = (
        P(None, "seq", None),
        P(),
        P(None, None, "ch"),
        P(None, "ch"),
        P(None, "ch"),
        P(),
        P(None, None, "ch"),
        P(None, "ch"),
        P(None, "seq", None),
    )
    return jax.shard_map(
        per_device,
        mesh=mesh,
        in_specs=placed,
        out_specs=(
            P(None, ("seq", "ch"), None),
            P(None, ("seq", "ch"), None),
            P(),
            P("seq", None, "ch"),
            P(),
            P("seq", "ch"),
            P(),
            P("seq", None, "ch"),
            P("seq", "ch"),
        ),
        check_vma=False,
    )
```

profile of v0, /device:TPU:0, one launch (start us, length us, event | category | flops | bytes accessed | tf_op | source)
XLA Modules:
  0.0 1378.1 jit_solution(6991222645832877539)
XLA Ops:
  7.3 5.5 fusion.31
  14.7 4.3 fusion.159
  19.2 4.9 collective-permute-start
  28.2 4.5 fusion.200
  32.8 10.1 slice_convert_fusion.2
  42.8 50.4 %reduce-scatter.19.cloned.1.call-done = f32[256,1536]{1,0:T(8,128)} async-done(((f32[1024,1536]{1,0:T(8,128)}), f32[256,1536]{1,0:T(8,128)}) %reduce-scatter.19.cloned.1.call-update) | async-done | bytes 1572880 | tf_op jit(solution)/shard_map/reduce_scatter | solution.py:78
  98.0 28.4 %all-gather.7.cloned.1.call-done = bf16[1024,1536]{1,0:T(8,128)(2,1)} async-done(((bf16[256,1536]{1,0:T(8,128)(2,1)}), bf16[1024,1536]{1,0:T(8,128)(2,1)}) %all-gather.7.cloned.1.call-update) | async-done | bytes 3145744 | tf_op jit(solution)/shard_map/all_gather | solution.py:82
  126.4 18.0 %fusion.72 = f32[1024,2,1728]{0,2,1:T(8,128)} fusion(bf16[1536,2,1728]{0,2,1:T(8,128)(2,1)} %param.15, bf16[1024,1536]{1,0:T(8,128)(2,1)} %all-gather.7.cloned.1.call-done), kind=kOutput, calls=%fused_computation.111 | convolution fusion | flops 10871635968 | bytes 27918336 | tf_op jit(solution)/shard_map/td,dkf->tkf/dot_general | solution.py:83
  144.4 16.0 %fusion.50 = (bf16[1024,1,1728]{0,2,1:T(8,128)(2,1)S(1)}, bf16[1024,1,1728]{0,2,1:T(8,128)(2,1)}) fusion(f32[1024,2,1728]{0,2,1:T(8,128)} %fusion.72, bf16[1536,1728]{0,1:T(8,128)(2,1)} %param.16, bf16[3,1024,1536]{2,1,0:T(8,128)(2,1)} %param.17), kind=kOutput, calls=%fused_computation.89 | convolution fusion | flops 5458821120 | bytes 29687808 | tf_op jit(solution)/shard_map/dot_general | solution.py:100
  162.2 15.0 %bitcast_convert_fusion.5 = bf16[1024,1536]{1,0:T(8,128)(2,1)} fusion(bf16[1536,2,1728]{0,2,1:T(8,128)(2,1)S(1)} %bitcast.457, bf16[1024,1,1728]{0,2,1:T(8,128)(2,1)} %get-tuple-element.82, bf16[1024,1,1728]{0,2,1:T(8,128)(2,1)S(1)} %get-tuple-element.81), kind=kOutput, calls=%fused_computation.57 | convolution fusion | flops 10876747776 | bytes 20840448 | tf_op jit(solution)/shard_map/tkf,dkf->td/dot_general | solution.py:105
  177.3 6.7 fusion.193
  184.1 31.3 %reduce-scatter.31.cloned.1.call-done = bf16[256,1536]{1,0:T(8,128)(2,1)} async-done(((bf16[1024,1536]{1,0:T(8,128)(2,1)}), bf16[256,1536]{1,0:T(8,128)(2,1)}) %reduce-scatter.31.cloned.1.call-update) | async-done | bytes 786448 | tf_op jit(solution)/shard_map/reduce_scatter | solution.py:108
  222.9 6.2 fusion.156
  232.9 6.2 fusion.153
  250.3 4.1 fusion.203
  257.4 4.2 broadcast_multiply_fusion.8
  263.2 3.9 collective-permute-done.3
  268.6 5.8 bitcast_convert_fusion.4
  274.5 6.0 fusion.201
  280.6 6.1 fusion.202
  286.9 12.1 convolution_convert_fusion.2
  301.1 11.5 reduce-scatter.33.cloned.1.call-done
  315.8 57.7 %reduce-scatter.23.cloned.1.call-done = f32[256,1536]{1,0:T(8,128)} async-done(((f32[1024,1536]{1,0:T(8,128)}), f32[256,1536]{1,0:T(8,128)}) %reduce-scatter.23.cloned.1.call-update) | async-done | bytes 1572880 | tf_op jit(solution)/shard_map/reduce_scatter | solution.py:78
  377.2 57.2 %reduce-scatter.27.cloned.1.call-done = f32[256,1536]{1,0:T(8,128)} async-done(((f32[1024,1536]{1,0:T(8,128)}), f32[256,1536]{1,0:T(8,128)}) %reduce-scatter.27.cloned.1.call-update) | async-done | bytes 1572880 | tf_op jit(solution)/shard_map/reduce_scatter | solution.py:78
  438.2 36.9 %reduce-scatter.21.cloned.1.call-done = bf16[256,1536]{1,0:T(8,128)(2,1)} async-done(((bf16[1024,1536]{1,0:T(8,128)(2,1)}), bf16[256,1536]{1,0:T(8,128)(2,1)}) %reduce-scatter.21.cloned.1.call-update) | async-done | bytes 786448 | tf_op jit(solution)/shard_map/reduce_scatter | solution.py:94
  475.1 5.6 fusion.149
  480.7 28.6 %all-gather.9.cloned.1.call-done = bf16[1024,1536]{1,0:T(8,128)(2,1)} async-done(((bf16[256,1536]{1,0:T(8,128)(2,1)}), bf16[1024,1536]{1,0:T(8,128)(2,1)}) %all-gather.9.cloned.1.call-update) | async-done | bytes 3145744 | tf_op jit(solution)/shard_map/all_gather | solution.py:82
  509.4 17.9 %fusion.69 = f32[1024,2,1728]{0,2,1:T(8,128)} fusion(bf16[1536,2,1728]{0,2,1:T(8,128)(2,1)} %param.15, bf16[1024,1536]{1,0:T(8,128)(2,1)} %all-gather.9.cloned.1.call-done), kind=kOutput, calls=%fused_computation.108 | convolution fusion | flops 10871635968 | bytes 27918336 | tf_op jit(solution)/shard_map/td,dkf->tkf/dot_general | solution.py:83
  527.3 16.1 %fusion.51 = (bf16[1024,1,1728]{0,2,1:T(8,128)(2,1)S(1)}, bf16[1024,1,1728]{0,2,1:T(8,128)(2,1)}) fusion(f32[1024,2,1728]{0,2,1:T(8,128)} %fusion.69, bf16[1536,1728]{0,1:T(8,128)(2,1)} %param.16, bf16[3,1024,1536]{2,1,0:T(8,128)(2,1)} %param.17), kind=kOutput, calls=%fused_computation.90 | convolution fusion | flops 5458821120 | bytes 29687808 | tf_op jit(solution)/shard_map/dot_general | solution.py:100
  545.3 14.9 %bitcast_convert_fusion.3 = bf16[1024,1536]{1,0:T(8,128)(2,1)} fusion(bf16[1536,2,1728]{0,2,1:T(8,128)(2,1)S(1)} %bitcast.459, bf16[1024,1,1728]{0,2,1:T(8,128)(2,1)} %get-tuple-element.84, bf16[1024,1,1728]{0,2,1:T(8,128)(2,1)S(1)} %get-tuple-element.83), kind=kOutput, calls=%fused_computation.55 | convolution fusion | flops 10876747776 | bytes 20840448 | tf_op jit(solution)/shard_map/tkf,dkf->td/dot_general | solution.py:105
  560.3 38.1 %reduce-scatter.35.cloned.1.call-done = bf16[256,1536]{1,0:T(8,128)(2,1)} async-done(((bf16[1024,1536]{1,0:T(8,128)(2,1)}), bf16[256,1536]{1,0:T(8,128)(2,1)}) %reduce-scatter.35.cloned.1.call-update) | async-done | bytes 786448 | tf_op jit(solution)/shard_map/reduce_scatter | solution.py:108
  605.2 28.1 %all-gather.15.cloned.1.call-done = bf16[1024,1536]{1,0:T(8,128)(2,1)} async-done(((bf16[256,1536]{1,0:T(8,128)(2,1)}), bf16[1024,1536]{1,0:T(8,128)(2,1)}) %all-gather.15.cloned.1.call-update) | async-done | bytes 3145744 | tf_op jit(solution)/shard_map/all_gather | solution.py:115
  633.2 4.1 fusion.204
  647.8 5.8 bitcast_convert_fusion.2
  653.7 12.4 convolution_convert_fusion.1
  666.2 17.9 %fusion.66 = f32[1024,2,1728]{0,2,1:T(8,128)} fusion(bf16[1536,2,1728]{0,2,1:T(8,128)(2,1)} %param.15, bf16[1024,1536]{1,0:T(8,128)(2,1)} %all-gather.11.cloned.1.call-done), kind=kOutput, calls=%fused_computation.105 | convolution fusion | flops 10871635968 | bytes 27918336 | tf_op jit(solution)/shard_map/td,dkf->tkf/dot_general | solution.py:83
  684.2 16.1 %fusion.52 = (bf16[1024,1,1728]{0,2,1:T(8,128)(2,1)S(1)}, bf16[1024,1,1728]{0,2,1:T(8,128)(2,1)}) fusion(f32[1024,2,1728]{0,2,1:T(8,128)} %fusion.66, bf16[1536,1728]{0,1:T(8,128)(2,1)} %param.16, bf16[3,1024,1536]{2,1,0:T(8,128)(2,1)} %param.17), kind=kOutput, calls=%fused_computation.91 | convolution fusion | flops 5458821120 | bytes 29687808 | tf_op jit(solution)/shard_map/dot_general | solution.py:100
  702.0 14.8 %bitcast_convert_fusion.1 = bf16[1024,1536]{1,0:T(8,128)(2,1)} fusion(bf16[1536,2,1728]{0,2,1:T(8,128)(2,1)S(1)} %bitcast.461, bf16[1024,1,1728]{0,2,1:T(8,128)(2,1)} %get-tuple-element.86, bf16[1024,1,1728]{0,2,1:T(8,128)(2,1)S(1)} %get-tuple-element.85), kind=kOutput, calls=%fused_computation.53 | convolution fusion | flops 10876747776 | bytes 20840448 | tf_op jit(solution)/shard_map/tkf,dkf->td/dot_general | solution.py:105
  722.0 22.4 %reduce-scatter.25.cloned.1.call-done = bf16[256,1536]{1,0:T(8,128)(2,1)} async-done(((bf16[1024,1536]{1,0:T(8,128)(2,1)}), bf16[256,1536]{1,0:T(8,128)(2,1)}) %reduce-scatter.25.cloned.1.call-update) | async-done | bytes 786448 | tf_op jit(solution)/shard_map/reduce_scatter | solution.py:94
  744.4 40.5 %reduce-scatter.39.cloned.1.call-done = bf16[256,1536]{1,0:T(8,128)(2,1)} async-done(((bf16[1024,1536]{1,0:T(8,128)(2,1)}), bf16[256,1536]{1,0:T(8,128)(2,1)}) %reduce-scatter.39.cloned.1.call-update) | async-done | bytes 786448 | tf_op jit(solution)/shard_map/reduce_scatter | solution.py:108
  784.9 5.8 fusion.150
  793.9 12.2 fusion.48
  806.0 12.3 fusion.46
  818.3 16.7 %fusion.24 = bf16[1536,1728]{0,1:T(8,128)(2,1)} fusion(f32[1728,1536]{1,0:T(8,128)} %fusion.48, f32[1728,1536]{1,0:T(8,128)} %fusion.46, f32[1024,2,1728]{0,2,1:T(8,128)} %fusion.66, bf16[3,1024,1536]{2,1,0:T(8,128)(2,1)} %param.17), kind=kOutput, calls=%fused_computation.51 | convolution fusion | flops 5454397440 | bytes 43843584 | tf_op jit(solution)/shard_map/td,tf->df/dot_general | solution.py:99
  835.0 7.8 copy.54
  842.9 20.2 %fusion.37 = f32[1536,2,1728]{2,0,1:T(8,128)} fusion(bf16[1024,1,1728]{0,2,1:T(8,128)(2,1)} %get-tuple-element.82, bf16[1024,1,1728]{0,2,1:T(8,128)(2,1)} %copy-done.89, bf16[1024,1536]{1,0:T(8,128)(2,1)} %all-gather.7.cloned.1.call-done), kind=kOutput, calls=%fused_computation.76 | convolution fusion | flops 10885791744 | bytes 31457280 | tf_op jit(solution)/shard_map/td,tkf->dkf/dot_general | solution.py:104
  863.1 18.5 %fusion.35 = f32[1536,2,1728]{2,0,1:T(8,128)} fusion(bf16[1024,1,1728]{0,2,1:T(8,128)(2,1)} %get-tuple-element.84, bf16[1024,1,1728]{0,2,1:T(8,128)(2,1)} %copy-done.90, bf16[1024,1536]{1,0:T(8,128)(2,1)S(1)} %copy-done.86), kind=kOutput, calls=%fused_computation.74 | convolution fusion | flops 10885791744 | bytes 31457280 | tf_op jit(solution)/shard_map/td,tkf->dkf/dot_general | solution.py:104
  881.6 24.8 %add_convert_fusion = bf16[1536,2,1728]{2,0,1:T(8,128)(2,1)} fusion(f32[1536,2,1728]{2,0,1:T(8,128)} %fusion.37, f32[1536,2,1728]{2,0,1:T(8,128)} %fusion.35, bf16[1024,1,1728]{0,2,1:T(8,128)(2,1)} %get-tuple-element.86, bf16[1024,1,1728]{0,2,1:T(8,128)(2,1)} %copy-done.88, bf16[1024,1536]{1,0:T(8,128)(2,1)} %all-gather.11.cloned.1.call-done), kind=kOutput, calls=%fused_computation | convolution fusion | flops 10901716992 | bytes 63307776 | tf_op jit(solution)/shard_map/td,tkf->dkf/dot_general | solution.py:104
  906.4 4.2 fusion.206
  913.9 5.9 fusion.74
  919.9 4.1 fusion.205
  929.1 3.9 collective-permute-done.5
  934.5 5.7 bitcast_convert_fusion
  940.3 12.2 convolution_convert_fusion
  953.2 7.3 fusion.136
  960.6 6.7 fusion.135
  967.3 9.1 add_convert_fusion.2
  992.6 145.8 %reduce-scatter.47.cloned.1.call-done = bf16[192,2,1728]{2,0,1:T(8,128)(2,1)} async-done(((bf16[1536,2,1728]{2,0,1:T(8,128)(2,1)}), bf16[192,2,1728]{2,0,1:T(8,128)(2,1)}) %reduce-scatter.47.cloned.1.call-update) | async-done | bytes 1327120 | tf_op jit(solution)/shard_map/reduce_scatter | solution.py:154
  1138.4 4.3 copy.40
  1144.1 61.2 %reduce-scatter.45.cloned.1.call-done = bf16[192,384]{1,0:T(8,128)(2,1)} async-done(((bf16[1536,384]{1,0:T(8,128)(2,1)}), bf16[192,384]{1,0:T(8,128)(2,1)}) %reduce-scatter.45.cloned.1.call-update) | async-done | bytes 147472 | tf_op jit(solution)/shard_map/reduce_scatter | solution.py:151
  1206.9 37.9 %reduce-scatter.41.cloned.1.call-done = bf16[256,1536]{1,0:T(8,128)(2,1)} async-done(((bf16[1024,1536]{1,0:T(8,128)(2,1)}), bf16[256,1536]{1,0:T(8,128)(2,1)}) %reduce-scatter.41.cloned.1.call-update) | async-done | bytes 786448 | tf_op jit(solution)/shard_map/reduce_scatter | solution.py:134
  1248.7 40.6 %all-reduce.12 = (f32[1536]{0:T(1024)}, f32[3,1536]{1,0:T(4,128)}, f32[1536]{0:T(1024)}) all-reduce(f32[1536]{0:T(1024)} %add_add_fusion.1, f32[3,1536]{1,0:T(4,128)} %fusion.162, f32[1536]{0:T(1024)} %add_add_fusion), channel_id=1, replica_groups=mesh['seq'=8,'ch'=4] {'seq','ch'}, use_global_device_ids=true, to_apply=%region_27.28 | all-reduce | flops 7680 | bytes 61440 | tf_op jit(solution)/shard_map/psum | solution.py:164
  1290.6 3.9 fusion.151
  1298.0 70.8 %reduce-scatter.43.cloned.1.call-done = bf16[192,3,384]{2,0,1:T(8,128)(2,1)} async-done(((bf16[1536,3,384]{2,0,1:T(8,128)(2,1)}), bf16[192,3,384]{2,0,1:T(8,128)(2,1)}) %reduce-scatter.43.cloned.1.call-update) | async-done | bytes 442384 | tf_op jit(solution)/shard_map/reduce_scatter | solution.py:148
  (352 shorter events, 124.2 us)
Async XLA Ops:
  7.2 86.0 %reduce-scatter.19.cloned.1.call-start = ((), (), s32[]{:S(2)}) async-start(), calls=%async_computation.16 | async-start | bytes 7864320 | tf_op jit(solution)/shard_map/reduce_scatter | solution.py:78
  7.2 7.5 copy-start.11
  19.0 6.5 copy-start.14
  19.2 6.2 collective-permute-start
  32.7 93.7 %all-gather.7.cloned.1.call-start = ((), (), s32[]{:S(2)}) async-start(), calls=%async_computation.17 | async-start | bytes 3932160 | tf_op jit(solution)/shard_map/all_gather | solution.py:82
  42.8 53.8 %copy-start.41 = (f32[1536]{0:T(1024)S(1)}, f32[1536]{0:T(1024)}, u32[]{:S(2)}) copy-start(f32[1536]{0:T(1024)} %param.14) | copy-start | bytes 18436
  97.7 117.7 %reduce-scatter.31.cloned.1.call-start = ((), (), s32[]{:S(2)}) async-start(), calls=%async_computation.25 | async-start | bytes 3932160 | tf_op jit(solution)/shard_map/reduce_scatter | solution.py:108
  126.4 35.8 %slice-start.6 = ((s8[10616832]{0:T(1024)(128)(4,1)}), s8[4194304]{0:T(1024)(128)(4,1)S(1)}, s32[]{:S(2)}) async-start(s8[10616832]{0:T(1024)(128)(4,1)} %bitcast.456), calls=%async_computation.44 | async-start | bytes 8388608
  126.4 35.8 %slice-start.7 = ((s8[10616832]{0:T(1024)(128)(4,1)}), s8[4194304]{0:T(1024)(128)(4,1)S(1)}, s32[]{:S(2)}) async-start(s8[10616832]{0:T(1024)(128)(4,1)} %bitcast.456), calls=%async_computation.45 | async-start | bytes 8388608
  144.4 17.8 %slice-start.8 = ((s8[10616832]{0:T(1024)(128)(4,1)}), s8[2228224]{0:T(1024)(128)(4,1)S(1)}, s32[]{:S(2)}) async-start(s8[10616832]{0:T(1024)(128)(4,1)} %bitcast.456), calls=%async_computation.46 | async-start | bytes 4456448
  177.3 73.0 %all-gather.13.cloned.1.call-start = ((), (), s32[]{:S(2)}) async-start(), calls=%async_computation.26 | async-start | bytes 3932160 | tf_op jit(solution)/shard_map/all_gather | solution.py:115
  221.6 91.0 %reduce-scatter.33.cloned.1.call-start = ((), (), s32[]{:S(2)}) async-start(), calls=%async_computation.27 | async-start | bytes 3932160 | tf_op jit(solution)/shard_map/reduce_scatter | solution.py:134
  229.3 15.5 %collective-permute-start.1 = (bf16[2,384]{1,0:T(2,128)(2,1)S(1)}, bf16[2,384]{1,0:T(2,128)(2,1)S(1)}, u32[]{:S(2)}, u32[]{:S(2)}) collective-permute-start(bf16[2,384]{1,0:T(2,128)(2,1)S(1)} %slice.207), channel_id=1, source_target_pairs={{0,4},{4,8},{8,12},{12,16},{16,20},{20,24},{24,28},{1,5},{5,9},{9,... | collective-permute-start | bytes 4616 | tf_op jit(solution)/shard_map/ppermute | solution.py:12
  232.9 6.2 copy-start.75
  241.4 4.7 collective-permute-start.2
  254.5 12.6 slice-start.4
  257.4 10.1 copy-start.26
  257.4 9.7 slice-start.5
  261.6 5.5 collective-permute-start.3
  274.5 99.0 %reduce-scatter.23.cloned.1.call-start = ((), (), s32[]{:S(2)}) async-start(), calls=%async_computation.19 | async-start | bytes 7864320 | tf_op jit(solution)/shard_map/reduce_scatter | solution.py:78
  280.5 153.9 %reduce-scatter.27.cloned.1.call-start = ((), (), s32[]{:S(2)}) async-start(), calls=%async_computation.22 | async-start | bytes 7864320 | tf_op jit(solution)/shard_map/reduce_scatter | solution.py:78
  286.7 188.4 %reduce-scatter.21.cloned.1.call-start = ((), (), s32[]{:S(2)}) async-start(), calls=%async_computation.18 | async-start | bytes 3932160 | tf_op jit(solution)/shard_map/reduce_scatter | solution.py:94
  299.1 210.3 %all-gather.9.cloned.1.call-start = ((), (), s32[]{:S(2)}) async-start(), calls=%async_computation.20 | async-start | bytes 3932160 | tf_op jit(solution)/shard_map/all_gather | solution.py:82
  480.7 117.7 %reduce-scatter.35.cloned.1.call-start = ((), (), s32[]{:S(2)}) async-start(), calls=%async_computation.28 | async-start | bytes 3932160 | tf_op jit(solution)/shard_map/reduce_scatter | solution.py:108
  509.4 35.9 %slice-start.9 = ((s8[10616832]{0:T(1024)(128)(4,1)}), s8[4194304]{0:T(1024)(128)(4,1)S(1)}, s32[]{:S(2)}) async-start(s8[10616832]{0:T(1024)(128)(4,1)} %bitcast.458), calls=%async_computation.47 | async-start | bytes 8388608
  509.4 35.9 %slice-start.10 = ((s8[10616832]{0:T(1024)(128)(4,1)}), s8[4194304]{0:T(1024)(128)(4,1)S(1)}, s32[]{:S(2)}) async-start(s8[10616832]{0:T(1024)(128)(4,1)} %bitcast.458), calls=%async_computation.48 | async-start | bytes 8388608
  527.3 18.0 %slice-start.11 = ((s8[10616832]{0:T(1024)(128)(4,1)}), s8[2228224]{0:T(1024)(128)(4,1)S(1)}, s32[]{:S(2)}) async-start(s8[10616832]{0:T(1024)(128)(4,1)} %bitcast.458), calls=%async_computation.49 | async-start | bytes 4456448
  560.3 38.1 %copy-start.61 = (f32[256]{0:T(256)S(1)}, f32[256]{0:T(256)}, u32[]{:S(2)}) copy-start(f32[256]{0:T(256)} %get-tuple-element.128) | copy-start | bytes 3076
  560.3 41.4 %copy-start.66 = (f32[256]{0:T(256)S(1)}, f32[256]{0:T(256)}, u32[]{:S(2)}) copy-start(f32[256]{0:T(256)} %get-tuple-element.127) | copy-start | bytes 3076
  560.3 73.0 %all-gather.15.cloned.1.call-start = ((), (), s32[]{:S(2)}) async-start(), calls=%async_computation.29 | async-start | bytes 3932160 | tf_op jit(solution)/shard_map/all_gather | solution.py:115
  604.6 61.6 %all-gather.11.cloned.1.call-start = ((), (), s32[]{:S(2)}) async-start(), calls=%async_computation.23 | async-start | bytes 3932160 | tf_op jit(solution)/shard_map/all_gather | solution.py:82
  605.1 113.6 %reduce-scatter.37.cloned.1.call-start = ((), (), s32[]{:S(2)}) async-start(), calls=%async_computation.30 | async-start | bytes 3932160 | tf_op jit(solution)/shard_map/reduce_scatter | solution.py:134
  640.2 6.5 copy-start.29
  640.5 5.8 collective-permute-start.4
  653.7 90.7 %reduce-scatter.25.cloned.1.call-start = ((), (), s32[]{:S(2)}) async-start(), calls=%async_computation.21 | async-start | bytes 3932160 | tf_op jit(solution)/shard_map/reduce_scatter | solution.py:94
  666.1 118.8 %reduce-scatter.39.cloned.1.call-start = ((), (), s32[]{:S(2)}) async-start(), calls=%async_computation.31 | async-start | bytes 3932160 | tf_op jit(solution)/shard_map/reduce_scatter | solution.py:108
  666.2 35.8 %slice-start.12 = ((s8[10616832]{0:T(1024)(128)(4,1)}), s8[4194304]{0:T(1024)(128)(4,1)S(1)}, s32[]{:S(2)}) async-start(s8[10616832]{0:T(1024)(128)(4,1)} %bitcast.460), calls=%async_computation.50 | async-start | bytes 8388608
  666.2 35.8 %slice-start.13 = ((s8[10616832]{0:T(1024)(128)(4,1)}), s8[4194304]{0:T(1024)(128)(4,1)S(1)}, s32[]{:S(2)}) async-start(s8[10616832]{0:T(1024)(128)(4,1)} %bitcast.460), calls=%async_computation.51 | async-start | bytes 8388608
  684.2 17.8 %slice-start.14 = ((s8[10616832]{0:T(1024)(128)(4,1)}), s8[2228224]{0:T(1024)(128)(4,1)S(1)}, s32[]{:S(2)}) async-start(s8[10616832]{0:T(1024)(128)(4,1)} %bitcast.460), calls=%async_computation.52 | async-start | bytes 4456448
  716.8 197.1 %all-gather.17.cloned.1.call-start = ((), (), s32[]{:S(2)}) async-start(), calls=%async_computation.32 | async-start | bytes 3932160 | tf_op jit(solution)/shard_map/all_gather | solution.py:115
  784.9 6.3 copy-start.7
  784.9 6.3 copy-start.16
  784.9 6.3 copy-start.59
  784.9 6.3 copy-start.65
  793.8 188.8 %reduce-scatter.49.cloned.1.call-start = ((), (), s32[]{:S(2)}) async-start(), calls=%async_computation.37 | async-start | bytes 6193152
  842.8 295.6 %reduce-scatter.47.cloned.1.call-start = ((), (), s32[]{:S(2)}) async-start(), calls=%async_computation.36 | async-start | bytes 12386304 | tf_op jit(solution)/shard_map/reduce_scatter | solution.py:154
  842.9 20.2 %copy-start.86 = (bf16[1024,1536]{1,0:T(8,128)(2,1)S(1)}, bf16[1024,1536]{1,0:T(8,128)(2,1)}, u32[]{:S(2)}) copy-start(bf16[1024,1536]{1,0:T(8,128)(2,1)} %all-gather.9.cloned.1.call-done) | copy-start | bytes 9437188
  906.4 298.9 %reduce-scatter.45.cloned.1.call-start = ((), (), s32[]{:S(2)}) async-start(), calls=%async_computation.35 | async-start | bytes 1327104 | tf_op jit(solution)/shard_map/reduce_scatter | solution.py:151
  919.8 325.0 %reduce-scatter.41.cloned.1.call-start = ((), (), s32[]{:S(2)}) async-start(), calls=%async_computation.33 | async-start | bytes 3932160 | tf_op jit(solution)/shard_map/reduce_scatter | solution.py:134
  926.8 6.5 copy-start.35
  926.9 6.1 slice-start
  927.2 5.8 collective-permute-start.5
  940.2 350.3 %reduce-scatter.29.cloned.1.call-start = ((), (), s32[]{:S(2)}) async-start(), calls=%async_computation.24 | async-start | bytes 3932160 | tf_op jit(solution)/shard_map/reduce_scatter | solution.py:94
  952.5 7.9 copy-start.78
  952.5 416.3 %reduce-scatter.43.cloned.1.call-start = ((), (), s32[]{:S(2)}) async-start(), calls=%async_computation.34 | async-start | bytes 3981312 | tf_op jit(solution)/shard_map/reduce_scatter | solution.py:148
  953.2 7.3 copy-start.30
  953.2 7.3 copy-start.32
  953.2 7.3 copy-start.34
  960.5 6.7 copy-start.36
  960.5 6.7 copy-start.38
  960.5 6.7 copy-start.40
  960.5 6.7 copy-start.76
  976.4 14.9 %copy-start.58 = (f32[1536]{0:T(1024)S(1)}, f32[1536]{0:T(1024)}, u32[]{:S(2)}) copy-start(f32[1536]{0:T(1024)} %get-tuple-element.56) | copy-start | bytes 18436
  992.6 298.0 %copy-start.42 = (f32[1536]{0:T(1024)S(1)}, f32[1536]{0:T(1024)}, u32[]{:S(2)}) copy-start(f32[1536]{0:T(1024)} %param.14) | copy-start | bytes 18436
  (70 other events, 208.1 us)
Sparse Core Ops, SparseCore 0:
  32.8 60.3 reduce-scatter.18
  97.8 28.5 all-gather.6
  177.4 37.9 reduce-scatter.30
  221.7 28.5 all-gather.12
  274.6 37.9 reduce-scatter.32
  315.1 58.3 reduce-scatter.22
  376.0 58.3 reduce-scatter.26
  437.1 37.9 reduce-scatter.20
  480.8 28.5 all-gather.8
  560.4 37.9 reduce-scatter.34
  604.7 28.5 all-gather.14
  634.7 28.5 all-gather.10
  666.0 37.9 reduce-scatter.36
  706.4 37.9 reduce-scatter.24
  746.9 37.9 reduce-scatter.38
  793.9 28.5 all-gather.16
  842.9 106.3 reduce-scatter.48
  953.3 185.0 reduce-scatter.46
  1142.2 63.0 reduce-scatter.44
  1207.8 36.9 reduce-scatter.40
  1247.3 38.1 reduce-scatter.28
  1289.6 79.1 reduce-scatter.42
where the time goes:
time: 1390 us; the launch traced here: 1380 us
  waiting for transfers between devices  764 us (55%)
  matrix products  387 us (28%)
  other arithmetic  99 us (7%)
  local copies, waits for them, and re-layouts  53.4 us (4%)
  blocking collectives  40.6 us (3%)
  starting transfers between devices  17.8 us (1%)
  between operations  15.9 us (1%)
    reduce_scatter x3, waiting for transfers between devices, per_device(): lax.psum_scatter(mix_part, 'ch', scatter_dimension=0, tiled=True)  165 us
    reduce_scatter x1, waiting for transfers between devices, per_device(): lax.psum_scatter(totals[2].astype(jnp.bfloat16), 'seq', scatter_dimension...  146 us
    reduce_scatter x3, waiting for transfers between devices, per_device(): lax.psum_scatter(d_mid_part.astype(jnp.bfloat16), 'ch', scatter_dimension...  110 us
    reduce_scatter x1, waiting for transfers between devices, per_device(): lax.psum_scatter(totals[0].astype(jnp.bfloat16), 'seq', scatter_dimension...  70.8 us
    dot_general x3, matrix products, per_device(): jnp.einsum('td,tkf->dkf', normed2, d_gu, preferred_element_type=jnp.float32)  63.4 us
    reduce_scatter x1, waiting for transfers between devices, per_device(): lax.psum_scatter(totals[1].astype(jnp.bfloat16), 'seq', scatter_dimension...  61.2 us
    reduce_scatter x3, waiting for transfers between devices, per_device(): lax.psum_scatter(ffn_part.astype(jnp.bfloat16), 'ch', scatter_dimension=0...  59.3 us
    all_gather x3, waiting for transfers between devices, per_device(): normed2 = lax.all_gather(normed_share, 'ch', axis=0, tiled=True)  57.1 us
  transfers between devices with their start and end apart: 28, of which 22 were waited for; matrix products, arithmetic and copies ran while one was open for 26% of the time, Pallas kernels for 0%

commit v1 on v0

v1 whole, which is shorter than its diff:
```python
import jax
import jax.numpy as jnp
from jax import lax
from jax.sharding import PartitionSpec as P

EPS = 1e-05
LOW = jnp.bfloat16
CORES = 2


def norm_scale(rows):
    return lax.rsqrt(jnp.mean(rows * rows, axis=-1, keepdims=True) + EPS)


def norm_back(rows, scale, gain, grad):
    weighted = grad * gain
    inner = jnp.mean(weighted * rows, axis=-1, keepdims=True)
    d_rows = scale * weighted - rows * (scale * scale * scale) * inner
    d_gain = jnp.sum(grad * rows * scale, axis=0)
    return (d_rows, d_gain)


def dot(a, b, a_dim, b_dim):
    return lax.dot_general(
        a, b, (((a_dim,), (b_dim,)), ((), ())), preferred_element_type=jnp.float32
    )


def swap_cores(value):
    count = lax.axis_size("ch")
    return lax.ppermute(value, "ch", [(i, i ^ 1) for i in range(count)])


def shift_chips(value, steps):
    count = lax.axis_size("ch")
    return lax.ppermute(value, "ch", [(i, (i + CORES * steps) % count) for i in range(count)])


def shifted(value, axis, steps):
    count = lax.axis_size(axis)
    first, last = (max(0, -steps), min(count, count - steps))
    return lax.ppermute(value, axis, [(source, source + steps) for source in range(first, last)])


def pick(value, index):
    return lax.dynamic_index_in_dim(value, index, 0, keepdims=False)


def scatter_seq(grad):
    count = lax.axis_size("seq")
    index = lax.axis_index("seq")
    inner = 2 if count % 2 == 0 else 1
    outer = count // inner
    low, high = (index % inner, index // inner)
    rows = grad.shape[0] // count
    value = grad.reshape((outer, inner, rows) + grad.shape[1:])
    if inner == 2:
        keep = lax.dynamic_index_in_dim(value, low, 1, keepdims=False)
        give = lax.dynamic_index_in_dim(value, 1 - low, 1, keepdims=False)
        got = lax.ppermute(give, "seq", [(i, i ^ 1) for i in range(count)])
        value = (keep.astype(jnp.float32) + got.astype(jnp.float32)).astype(LOW)
    else:
        value = value[:, 0]
    ring = [(i, (i + inner) % count) for i in range(count)]
    moving = pick(value, (high + outer - 1) % outer)
    for step in range(outer - 1):
        got = lax.ppermute(moving, "seq", ring)
        total = got.astype(jnp.float32) + pick(value, (high + 2 * outer - 2 - step) % outer).astype(
            jnp.float32
        )
        moving = total if step == outer - 2 else total.astype(LOW)
    return moving.astype(jnp.float32)


def sum_all(value):
    for axis in ("ch", "seq"):
        count = lax.axis_size(axis)
        step = 1
        while step < count:
            value = value + lax.ppermute(value, axis, [(i, i ^ step) for i in range(count)])
            step *= 2
    return value


def per_device(
    hidden,
    gain_in,
    in_weight,
    conv_weight,
    out_weight,
    gain_mid,
    gate_up_weight,
    down_weight,
    cotangent,
):
    seqs, length, width = hidden.shape
    count = lax.axis_size("ch")
    chips = count // CORES
    me = lax.axis_index("ch")
    core, chip = (me % CORES, me // CORES)
    share = length // count
    taps, chans = conv_weight.shape
    hid = down_weight.shape[1]
    conv_taps = conv_weight.astype(jnp.float32)
    in_flat = in_weight.reshape(width, 3 * chans)
    out_pair = jnp.concatenate([out_weight, swap_cores(out_weight)], axis=1)
    gate_own, up_own = (gate_up_weight[:, 0], gate_up_weight[:, 1])
    gate_w = jnp.concatenate([gate_own, swap_cores(gate_own)], axis=1)
    up_w = jnp.concatenate([up_own, swap_cores(up_own)], axis=1)
    down_w = jnp.concatenate([down_weight, swap_cores(down_weight)], axis=1)
    in_other = swap_cores(in_flat)
    in_pair = jnp.concatenate([in_flat, in_other], axis=1)

    def blocks(value):
        return value.reshape((count, share) + value.shape[1:])

    order = [CORES * ((chip + k) % chips) + core for k in range(chips)]
    order_other = [CORES * ((chip + k) % chips) + (1 - core) for k in range(chips)]

    def take(value, places):
        split = blocks(value)
        return jnp.concatenate([pick(split, p) for p in places], axis=0)

    def give_rows(parts):
        return [shift_chips(parts[k], k) for k in range(1, chips)]

    def gather_rows(mine):
        return jnp.concatenate([mine] + [shift_chips(mine, -k) for k in range(1, chips)], axis=0)

    def natural(mine, other):
        both = jnp.stack(
            [
                mine.reshape((chips, share) + mine.shape[1:]),
                other.reshape((chips, share) + other.shape[1:]),
            ],
            axis=1,
        )
        both = jnp.where(core == 0, both, both[:, ::-1])
        both = jnp.concatenate([both, both], axis=0)
        both = lax.dynamic_slice_in_dim(both, (chips - chip) % chips, chips, 0)
        return both.reshape((length,) + mine.shape[1:])

    tail = shifted(hidden[:, length - (taps - 1) :], "seq", 1).reshape(seqs * (taps - 1), width)
    tail = tail.astype(jnp.float32)
    tail_normed = (tail * norm_scale(tail) * gain_in).astype(LOW)
    tail_proj = dot(tail_normed, in_flat, 1, 0)
    tail_gated = (tail_proj[:, :chans] * tail_proj[:, 2 * chans :]).astype(LOW)
    tail_gated = tail_gated.reshape(seqs, taps - 1, chans)

    kept = []
    for s in range(seqs):
        rows = hidden[s].astype(jnp.float32)
        scale_in = norm_scale(rows)
        normed = (rows * scale_in * gain_in).astype(LOW)
        proj = dot(normed, in_flat, 1, 0)
        b_gate, c_gate, x_val = (proj[:, :chans], proj[:, chans : 2 * chans], proj[:, 2 * chans :])
        gated = (b_gate * x_val).astype(LOW)
        padded = jnp.concatenate([tail_gated[s], gated], axis=0).astype(jnp.float32)
        conv = conv_taps[0] * padded[:length]
        for tap in range(1, taps):
            conv = conv + conv_taps[tap] * padded[tap : tap + length]
        mixed = (c_gate * conv).astype(LOW)
        got = swap_cores(take(mixed, order_other))
        mixed_rows = jnp.concatenate([take(mixed, order), got], axis=1)
        parts = [
            dot(mixed_rows[k * share : (k + 1) * share], out_pair, 1, 1) for k in range(chips)
        ]
        own_rows = pick(blocks(rows), me)
        resid = own_rows + parts[0]
        for part in give_rows([p.astype(LOW) for p in parts]):
            resid = resid + part.astype(jnp.float32)
        scale_mid = norm_scale(resid)
        normed_share = (resid * scale_mid * gain_mid).astype(LOW)
        normed2 = gather_rows(normed_share)
        kept.append(
            (normed, b_gate, c_gate, x_val, padded, conv, mixed_rows, own_rows, resid, scale_mid,
             normed2, pick(blocks(scale_in), me))
        )

    gain_mid_acc = jnp.zeros((width,), jnp.float32)
    gain_in_acc = jnp.zeros((width,), jnp.float32)
    conv_acc = jnp.zeros((taps, chans), jnp.float32)
    outs_rows, outs_grads, acts, d_gates, d_ups, grads, norms2 = ([], [], [], [], [], [], [])
    d_resids = []
    for s in range(seqs):
        resid, scale_mid, normed2 = (kept[s][8], kept[s][9], kept[s][10])
        grad_out = take(cotangent[s], order)
        gate_val = dot(normed2, gate_w, 1, 0)
        up_val = dot(normed2, up_w, 1, 0)
        sigm = jax.nn.sigmoid(gate_val)
        silu_val = gate_val * sigm
        act = (silu_val * up_val).astype(LOW)
        d_act = dot(grad_out, down_w, 1, 0)
        d_gate = (d_act * up_val * sigm * (1.0 + gate_val * (1.0 - sigm))).astype(LOW)
        d_up = (d_act * silu_val).astype(LOW)
        d_mid_part = dot(d_gate, gate_w, 1, 1) + dot(d_up, up_w, 1, 1)
        d_mid_parts = [d_mid_part[k * share : (k + 1) * share] for k in range(chips)]
        d_mid = d_mid_parts[0]
        for part in give_rows([p.astype(LOW) for p in d_mid_parts]):
            d_mid = d_mid + part.astype(jnp.float32)
        d_resid_norm, gain_term = norm_back(resid, scale_mid, gain_mid, d_mid)
        gain_mid_acc = gain_mid_acc + gain_term
        d_resid = grad_out[:share].astype(jnp.float32) + d_resid_norm
        d_resids.append(d_resid)
        ffn_part = dot(act, down_w, 1, 1)
        ffn = ffn_part[:share]
        for part in give_rows(
            [ffn_part[k * share : (k + 1) * share].astype(LOW) for k in range(chips)]
        ):
            ffn = ffn + part.astype(jnp.float32)
        outs_rows.append((resid + ffn).astype(LOW))
        acts.append(act)
        d_gates.append(d_gate)
        d_ups.append(d_up)
        grads.append(grad_out)
        norms2.append(normed2)

    def weight_grad(left, right, cols):
        other = swap_cores(dot(left, right[:, cols:], 0, 0).astype(LOW))
        return (dot(left, right[:, :cols], 0, 0) + other.astype(jnp.float32)).astype(LOW)

    act_all, d_gate_all, d_up_all = (
        jnp.concatenate(acts, axis=0),
        jnp.concatenate(d_gates, axis=0),
        jnp.concatenate(d_ups, axis=0),
    )
    norm2_all = jnp.concatenate(norms2, axis=0)
    down_grad = scatter_seq(weight_grad(jnp.concatenate(grads, axis=0), act_all, hid))
    gate_grad = scatter_seq(weight_grad(norm2_all, d_gate_all, hid))
    up_grad = scatter_seq(weight_grad(norm2_all, d_up_all, hid))

    d_mixes, d_projs = ([], [])
    for s in range(seqs):
        normed, b_gate, c_gate, x_val, padded, conv, mixed_rows, own_rows = kept[s][:8]
        d_resid = d_resids[s]
        d_mix = gather_rows(d_resid.astype(LOW))
        d_mixes.append(d_mix)
        d_mixed_own = dot(d_mix, out_pair[:, :chans], 1, 0)
        d_mixed_other = dot(d_mix, out_pair[:, chans:], 1, 0)
        d_mixed = natural(
            d_mixed_own.astype(LOW), swap_cores(d_mixed_other.astype(LOW))
        ).astype(jnp.float32)
        d_c = d_mixed * conv
        d_conv = d_mixed * c_gate
        d_padded = jnp.zeros((length + taps - 1, chans), jnp.float32)
        conv_terms = []
        for tap in range(taps):
            conv_terms.append(jnp.sum(d_conv * padded[tap : tap + length], axis=0))
            d_padded = d_padded + jnp.pad(conv_taps[tap] * d_conv, ((tap, taps - 1 - tap), (0, 0)))
        conv_acc = conv_acc + jnp.stack(conv_terms, axis=0)
        after = shifted(d_padded[: taps - 1], "seq", -1)
        d_gated = d_padded[taps - 1 :] + jnp.pad(after, ((length - (taps - 1), 0), (0, 0)))
        d_gated_low = d_gated.astype(LOW).astype(jnp.float32)
        d_proj = jnp.concatenate(
            [(d_gated_low * x_val).astype(LOW), d_c.astype(LOW), (d_gated_low * b_gate).astype(LOW)],
            axis=1,
        )
        d_projs.append(d_proj)
        got = swap_cores(take(d_proj, order_other))
        d_proj_rows = jnp.concatenate([take(d_proj, order), got], axis=1)
        d_in_part = dot(d_proj_rows, in_pair, 1, 1)
        d_in = d_in_part[:share]
        for part in give_rows(
            [d_in_part[k * share : (k + 1) * share].astype(LOW) for k in range(chips)]
        ):
            d_in = d_in + part.astype(jnp.float32)
        d_rows_norm, gain_term = norm_back(own_rows, kept[s][11], gain_in, d_in)
        gain_in_acc = gain_in_acc + gain_term
        outs_grads.append((d_resid + d_rows_norm).astype(LOW))

    out_grad = scatter_seq(
        weight_grad(
            jnp.concatenate(d_mixes, axis=0),
            jnp.concatenate([kept[s][6] for s in range(seqs)], axis=0),
            chans,
        )
    )
    in_grad = scatter_seq(
        dot(
            jnp.concatenate([kept[s][0] for s in range(seqs)], axis=0),
            jnp.concatenate(d_projs, axis=0),
            0,
            0,
        ).astype(LOW)
    )
    conv_full = lax.dynamic_update_slice_in_dim(
        jnp.zeros((taps, width), jnp.float32), conv_acc, me * chans, 1
    )
    small = sum_all(
        jnp.concatenate([conv_full, gain_in_acc[None], gain_mid_acc[None]], axis=0)
    )
    return (
        jnp.stack(outs_rows, axis=0),
        jnp.stack(outs_grads, axis=0),
        small[taps],
        in_grad.reshape(-1, 3, chans),
        small[:taps],
        out_grad,
        small[taps + 1],
        jnp.stack([gate_grad, up_grad], axis=1),
        down_grad,
    )


def solution(mesh):
    placed = (
        P(None, "seq", None),
        P(),
        P(None, None, "ch"),
        P(None, "ch"),
        P(None, "ch"),
        P(),
        P(None, None, "ch"),
        P(None, "ch"),
        P(None, "seq", None),
    )
    return jax.shard_map(
        per_device,
        mesh=mesh,
        in_specs=placed,
        out_specs=(
            P(None, ("seq", "ch"), None),
            P(None, ("seq", "ch"), None),
            P(),
            P("seq", None, "ch"),
            P(),
            P("seq", "ch"),
            P(),
            P("seq", None, "ch"),
            P("seq", "ch"),
        ),
        check_vma=False,
    )
```

time: 1390 us -> 1150 us (0.83)
  waiting for transfers between devices: 764 us -> 419 us
  local copies, waits for them, and re-layouts: 53.4 us -> 113 us
  other arithmetic: 99 us -> 150 us
  blocking collectives: 40.6 us -> 0 us
  starting transfers between devices: 17.8 us -> 54.2 us
  matrix products: 387 us -> 406 us
    reduce_scatter x15 -> x0, waiting for transfers between devices: 662 us -> none  [the longest x3 165 us: per_device(): lax.psum_scatter(mix_part, 'ch', scatter_dimension=0, tiled=True)]
    ppermute x0 -> x61, waiting for transfers between devices: none -> 410 us  [the longest x5 161 us: sum_all(): lax.ppermute(value, axis, [(i, i ^ step) for i in range(count)])]
    all_gather x6 -> x0, waiting for transfers between devices: 87.4 us -> none  [the longest x3 57.1 us: per_device(): normed2 = lax.all_gather(normed_share, 'ch', axis=0, tiled=True)]
    concatenate x0 -> x20, other arithmetic: none -> 49.3 us  [the longest x1 18.9 us: per_device(): jnp.concatenate([kept[s][6] for s in range(seqs)], axis=0)]
    ppermute x0 -> x61, starting transfers between devices: none -> 45.2 us  [the longest x18 20 us: shift_chips(): lax.ppermute(value, 'ch', [(i, (i + CORES * steps) % count) for i in rang...]
    psum x1 -> x0, blocking collectives: 40.6 us -> none  [per_device(): lax.psum((conv_full, gain_in_acc, gain_mid_acc), ('seq', 'ch'))]
    convert_element_type x0 -> x4, local copies, waits for them, and re-layouts: none -> 24.2 us  [the longest x3 24.1 us: weight_grad(): (dot(left, right[:, :cols], 0, 0) + other.astype(jnp.float32)).astype(LOW)]
    squeeze x0 -> x17, local copies, waits for them, and re-layouts: none -> 19.9 us  [the longest x1 8.68 us: per_device(): gate_own, up_own = (gate_up_weight[:, 0], gate_up_weight[:, 1])]
  transfers between devices with their start and end apart: 28 -> 65, of which waited for: 22 -> 28; matrix products, arithmetic and copies ran while one was open for 26% -> 46% of each run, Pallas kernels for 0% -> 0%
where the time goes in v1:
time: 1150 us; the launch traced here: 1140 us
  waiting for transfers between devices  419 us (36%)
  matrix products  406 us (35%)
  other arithmetic  150 us (13%)
  local copies, waits for them, and re-layouts  113 us (10%)
  starting transfers between devices  54.2 us (5%)
    dot_general x46, matrix products, dot(): lax.dot_general(a, b, (((a_dim,), (b_dim,)), ((), ())), preferred_element...  406 us
    ppermute x5, waiting for transfers between devices, sum_all(): lax.ppermute(value, axis, [(i, i ^ step) for i in range(count)])  161 us
    ppermute x15, waiting for transfers between devices, scatter_seq(): got = lax.ppermute(moving, 'seq', ring)  129 us
    ppermute x18, waiting for transfers between devices, shift_chips(): lax.ppermute(value, 'ch', [(i, (i + CORES * steps) % count) for i in rang...  111 us
    unnamed x345, local copies, waits for them, and re-layouts  41.4 us
    convert_element_type x3, local copies, waits for them, and re-layouts, weight_grad(): (dot(left, right[:, :cols], 0, 0) + other.astype(jnp.float32)).astype(LOW)  24.1 us
  transfers between devices with their start and end apart: 65, of which 28 were waited for; matrix products, arithmetic and copies ran while one was open for 46% of the time, Pallas kernels for 0%

profile of v1, /device:TPU:0, one launch (start us, length us, event | category | flops | bytes accessed | tf_op | source)
XLA Modules:
  0.0 1145.0 jit_solution(5394373650947167418)
XLA Ops:
  6.5 8.7 slice_bitcast_fusion.1
  20.7 9.1 slice_convert_fusion.1
  34.9 6.2 copy.31
  41.2 9.5 fusion.55
  50.7 6.1 fusion.58
  56.9 6.1 fusion.52
  73.9 6.9 fusion.206
  110.5 16.6 %collective-permute-done.3 = bf16[256,1536]{1,0:T(8,128)(2,1)S(1)} collective-permute-done((bf16[256,1536]{1,0:T(8,128)(2,1)S(1)}, bf16[256,1536]{1,0:T(8,128)(2,1)S(1)}, u32[]{:S(2)}, u32[]{:S(2)}) %collective-permute-start.3) | collective-permute-done | bytes 786464 | tf_op jit(solution)/shard_map/ppermute | solution.py:36
  132.8 11.2 collective-permute-done.10
  148.6 12.3 %collective-permute-done.4 = bf16[256,1536]{1,0:T(8,128)(2,1)S(1)} collective-permute-done((bf16[256,1536]{1,0:T(8,128)(2,1)S(1)}, bf16[256,1536]{1,0:T(8,128)(2,1)S(1)}, u32[]{:S(2)}, u32[]{:S(2)}) %collective-permute-start.4) | collective-permute-done | bytes 786464 | tf_op jit(solution)/shard_map/ppermute | solution.py:36
  163.3 14.4 %collective-permute-done.14 = bf16[256,1536]{1,0:T(8,128)(2,1)S(1)} collective-permute-done((bf16[256,1536]{1,0:T(8,128)(2,1)S(1)}, bf16[256,1536]{1,0:T(8,128)(2,1)S(1)}, u32[]{:S(2)}, u32[]{:S(2)}) %collective-permute-start.14) | collective-permute-done | bytes 786464 | tf_op jit(solution)/shard_map/ppermute | solution.py:36
  180.7 13.0 %collective-permute-done.11 = bf16[256,1536]{1,0:T(8,128)(2,1)S(1)} collective-permute-done((bf16[256,1536]{1,0:T(8,128)(2,1)S(1)}, bf16[256,1536]{1,0:T(8,128)(2,1)S(1)}, u32[]{:S(2)}, u32[]{:S(2)}) %collective-permute-start.11) | collective-permute-done | bytes 786464 | tf_op jit(solution)/shard_map/ppermute | solution.py:36
  196.2 18.9 %maximum_maximum_fusion = bf16[1536,768]{1,0:T(8,128)(2,1)} fusion(bf16[512,384]{1,0:T(8,128)(2,1)S(1)} %collective-permute-done.13, bf16[256,384]{1,0:T(8,128)(2,1)S(1)} %get-tuple-element.147, bf16[256,384]{1,0:T(8,128)(2,1)S(1)} %get-tuple-element.144, bf16[512,384]{1,0:T(8,128)(2,1)S(1)} %collective-permute-done.9, ...), kind=kLoop, calls=%fused_computation.140 | loop fusion | flops 21233664 | bytes 4718592 | tf_op jit(solution)/shard_map/concatenate | solution.py:274
  218.2 12.9 %fusion.157 = f32[512,3456]{1,0:T(8,128)} fusion(bf16[256,1536]{1,0:T(8,128)(2,1)S(1)} %copy-done.86, bf16[256,1536]{1,0:T(8,128)(2,1)S(1)} %copy-done.93, bf16[1536,1728]{0,1:T(8,128)(2,1)} %collective-permute-done.6, bf16[1536,1728]{0,1:T(8,128)(2,1)} %get-tuple-element.93), kind=kOutput, calls=%fused_computation.326 | convolution fusion | flops 5460197376 | bytes 19267584 | tf_op jit(solution)/shard_map/dot_general | solution.py:24
  231.1 13.0 %fusion.155 = f32[512,3456]{1,0:T(8,128)} fusion(bf16[256,1536]{1,0:T(8,128)(2,1)S(1)} %copy-done.88, bf16[256,1536]{1,0:T(8,128)(2,1)} %copy-done.95, bf16[1536,1728]{0,1:T(8,128)(2,1)} %collective-permute-done.6, bf16[1536,1728]{0,1:T(8,128)(2,1)} %get-tuple-element.93), kind=kOutput, calls=%fused_computation.324 | convolution fusion | flops 5460197376 | bytes 19267584 | tf_op jit(solution)/shard_map/dot_general | solution.py:24
  249.3 13.4 %fusion.153 = f32[512,3456]{1,0:T(8,128)} fusion(bf16[256,1536]{1,0:T(8,128)(2,1)} %copy-done.90, bf16[256,1536]{1,0:T(8,128)(2,1)} %copy-done.97, bf16[1536,1728]{0,1:T(8,128)(2,1)} %collective-permute-done.6, bf16[1536,1728]{0,1:T(8,128)(2,1)} %get-tuple-element.93), kind=kOutput, calls=%fused_computation.322 | convolution fusion | flops 5460197376 | bytes 19267584 | tf_op jit(solution)/shard_map/dot_general | solution.py:24
  262.7 12.6 %fusion.109 = f32[512,3456]{1,0:T(8,128)} fusion(bf16[1536,3456]{0,1:T(8,128)(2,1)} %constant_dynamic-update-slice_fusion.2, bf16[256,1536]{1,0:T(8,128)(2,1)S(1)} %copy-done.82, bf16[256,1536]{1,0:T(8,128)(2,1)S(1)} %copy-done.71), kind=kOutput, calls=%fused_computation.205 | convolution fusion | flops 5438963712 | bytes 19267584 | tf_op jit(solution)/shard_map/dot_general | solution.py:24
  275.3 8.3 fusion.113
  283.7 8.3 fusion.117
  292.0 16.5 %multiply_convert_fusion.5 = (bf16[512,3456]{1,0:T(8,128)(2,1)}, bf16[512,3456]{1,0:T(8,128)(2,1)}, bf16[512,3456]{1,0:T(8,128)(2,1)}) fusion(f32[512,3456]{1,0:T(8,128)} %fusion.109, f32[512,3456]{1,0:T(8,128)} %fusion.157, bf16[1536,1728]{0,1:T(8,128)(2,1)} %collective-permute-done.5, bf16[1536,1728]{0,1:T(8,128)(2,1)S(1)} %bitcast.416, ...), kind=kOutput, calls=%fused_computation.41 | convolution fusion | flops 5486739456 | bytes 36962304 | tf_op jit(solution)/shard_map/dot_general | solution.py:24
  308.5 16.9 %multiply_convert_fusion.3 = (bf16[512,3456]{1,0:T(8,128)(2,1)}, bf16[512,3456]{1,0:T(8,128)(2,1)}, bf16[512,3456]{1,0:T(8,128)(2,1)}) fusion(f32[512,3456]{1,0:T(8,128)} %fusion.113, f32[512,3456]{1,0:T(8,128)} %fusion.155, bf16[1536,1728]{0,1:T(8,128)(2,1)} %collective-permute-done.5, bf16[1536,1728]{0,1:T(8,128)(2,1)S(1)} %bitcast.416, ...), kind=kOutput, calls=%fused_computation.39 | convolution fusion | flops 5486739456 | bytes 36962304 | tf_op jit(solution)/shard_map/dot_general | solution.py:24
  325.4 15.4 %multiply_convert_fusion.1 = (bf16[512,3456]{1,0:T(8,128)(2,1)S(1)}, bf16[512,3456]{1,0:T(8,128)(2,1)}, bf16[512,3456]{1,0:T(8,128)(2,1)}) fusion(f32[512,3456]{1,0:T(8,128)} %fusion.117, f32[512,3456]{1,0:T(8,128)} %fusion.153, bf16[1536,1728]{0,1:T(8,128)(2,1)} %collective-permute-done.5, bf16[1536,1728]{0,1:T(8,128)(2,1)S(1)} %bitcast.416, ...), kind=kOutput, calls=%fused_computation.37 | convolution fusion | flops 5486739456 | bytes 36962304 | tf_op jit(solution)/shard_map/dot_general | solution.py:24
  340.8 11.5 %pad_maximum_fusion.2 = bf16[1536,3456]{1,0:T(8,128)(2,1)S(1)} fusion(bf16[512,3456]{1,0:T(8,128)(2,1)S(1)} %get-tuple-element.83, bf16[512,3456]{1,0:T(8,128)(2,1)} %get-tuple-element.86, bf16[512,3456]{1,0:T(8,128)(2,1)} %get-tuple-element.89), kind=kLoop, calls=%fused_computation.2 | loop fusion | flops 31850496 | bytes 21233664 | tf_op jit(solution)/shard_map/concatenate | solution.py:224
  352.3 17.7 %convolution_convert_fusion.2 = bf16[1536,1728]{0,1:T(8,128)(2,1)} fusion(bf16[1536,1536]{1,0:T(8,128)(2,1)} %copy-done.107, bf16[1536,3456]{1,0:T(8,128)(2,1)S(1)} %pad_maximum_fusion.2), kind=kOutput, calls=%fused_computation.17 | convolution fusion | flops 8156381184 | bytes 15532032 | tf_op jit(solution)/shard_map/dot_general | solution.py:24
  370.0 6.9 pad_maximum_fusion.3
  376.9 18.8 %convolution_convert_fusion.1 = bf16[1536,1728]{0,1:T(8,128)(2,1)} fusion(bf16[1536,1536]{1,0:T(8,128)(2,1)} %copy-done.107, bf16[1536,3456]{1,0:T(8,128)(2,1)S(1)} %pad_maximum_fusion.3), kind=kOutput, calls=%fused_computation.16 | convolution fusion | flops 8156381184 | bytes 15532032 | tf_op jit(solution)/shard_map/dot_general | solution.py:24
  395.7 9.9 fusion.205
  405.6 9.5 convolution_add_fusion.2
  415.9 9.0 fusion.209
  428.3 10.1 fusion.204
  438.4 9.5 convolution_add_fusion.1
  449.5 8.7 fusion.210
  460.9 8.7 fusion.211
  471.6 9.4 fusion.203
  481.0 8.3 convolution_add_fusion
  490.4 7.2 pad_maximum_fusion.4
  498.6 17.8 %convolution_convert_fusion = bf16[1536,1728]{0,1:T(8,128)(2,1)} fusion(bf16[1536,1536]{1,0:T(8,128)(2,1)} %copy-done.106, bf16[1536,3456]{1,0:T(8,128)(2,1)S(1)} %pad_maximum_fusion.4), kind=kOutput, calls=%fused_computation.15 | convolution fusion | flops 8156381184 | bytes 15532032 | tf_op jit(solution)/shard_map/dot_general | solution.py:24
  518.1 6.5 multiply_reduce_fusion
  529.5 15.0 %collective-permute-done.18 = bf16[256,1536]{1,0:T(8,128)(2,1)S(1)} collective-permute-done((bf16[256,1536]{1,0:T(8,128)(2,1)S(1)}, bf16[256,1536]{1,0:T(8,128)(2,1)S(1)}, u32[]{:S(2)}, u32[]{:S(2)}) %collective-permute-start.18) | collective-permute-done | bytes 786464 | tf_op jit(solution)/shard_map/ppermute | solution.py:36
  555.1 13.6 %collective-permute-done.25 = bf16[256,1536]{1,0:T(8,128)(2,1)S(1)} collective-permute-done((bf16[256,1536]{1,0:T(8,128)(2,1)S(1)}, bf16[256,1536]{1,0:T(8,128)(2,1)S(1)}, u32[]{:S(2)}, u32[]{:S(2)}) %collective-permute-start.25) | collective-permute-done | bytes 786464 | tf_op jit(solution)/shard_map/ppermute | solution.py:36
  579.2 13.6 %collective-permute-done.31 = bf16[256,1536]{1,0:T(8,128)(2,1)S(1)} collective-permute-done((bf16[256,1536]{1,0:T(8,128)(2,1)S(1)}, bf16[256,1536]{1,0:T(8,128)(2,1)S(1)}, u32[]{:S(2)}, u32[]{:S(2)}) %collective-permute-start.31) | collective-permute-done | bytes 786464 | tf_op jit(solution)/shard_map/ppermute | solution.py:36
  605.1 7.1 broadcast_multiply_fusion.6
  638.2 41.6 %fusion.6 = bf16[1536,1152]{1,0:T(8,128)(2,1)} fusion(bf16[1024,1536]{1,0:T(8,128)(2,1)} %get-tuple-element.96, bf16[1024,1536]{1,0:T(8,128)(2,1)} %get-tuple-element.95, bf16[1024,1536]{1,0:T(8,128)(2,1)} %get-tuple-element.94, bf16[1024,384]{1,0:T(8,128)(2,1)} %copy-done.62, bf16[1024,384]{1,0:T(8,128)(2,1)S(1)} %copy-done.57, ...), kind=kOutput, calls=%fused_computation.14 | convolution fusion | flops 10965417984 | bytes 20054016 | tf_op jit(solution)/shard_map/dot_general | solution.py:24
  694.0 6.2 fusion.82
  700.2 7.4 collective-permute-done.46
  709.4 6.0 fusion.70
  719.0 5.9 fusion.76
  730.2 13.9 %add_convert_fusion = bf16[1536,1728]{0,1:T(8,128)(2,1)} fusion(bf16[1536,1728]{0,1:T(8,128)(2,1)} %collective-permute-done.60, bf16[1536,1536]{1,0:T(8,128)(2,1)S(1)} %bitcast.435, bf16[1536,3456]{1,0:T(8,128)(2,1)} %copy-done.27), kind=kOutput, calls=%fused_computation.5 | convolution fusion | flops 8161689600 | bytes 20840448 | tf_op jit(solution)/shard_map/dot_general | solution.py:24
  745.1 13.6 %add_convert_fusion.2 = bf16[1536,1728]{0,1:T(8,128)(2,1)} fusion(bf16[1536,1728]{0,1:T(8,128)(2,1)} %collective-permute-done.50, bf16[1536,1536]{1,0:T(8,128)(2,1)S(1)} %bitcast.437, bf16[1536,3456]{1,0:T(8,128)(2,1)} %copy-done.26), kind=kOutput, calls=%fused_computation.7 | convolution fusion | flops 8161689600 | bytes 20840448 | tf_op jit(solution)/shard_map/dot_general | solution.py:24
  758.9 12.3 %add_convert_fusion.1 = bf16[1536,1728]{0,1:T(8,128)(2,1)} fusion(bf16[1536,1728]{0,1:T(8,128)(2,1)} %collective-permute-done.55, bf16[1536,1536]{1,0:T(8,128)(2,1)S(1)} %bitcast.437, bf16[1536,3456]{1,0:T(8,128)(2,1)S(1)} %bitcast.405), kind=kOutput, calls=%fused_computation.6 | convolution fusion | flops 8161689600 | bytes 20840448 | tf_op jit(solution)/shard_map/dot_general | solution.py:24
  771.2 7.9 copy.42
  779.1 8.1 copy.40
  787.2 8.1 copy.41
  829.3 155.0 %collective-permute-done.38 = f32[5,1536]{1,0:T(8,128)S(1)} collective-permute-done((f32[5,1536]{1,0:T(8,128)S(1)}, f32[5,1536]{1,0:T(8,128)S(1)}, u32[]{:S(2)}, u32[]{:S(2)}) %collective-permute-start.38) | collective-permute-done | bytes 30752 | tf_op jit(solution)/shard_map/ppermute | solution.py:80
  994.2 6.0 collective-permute-done.40
  1014.0 12.3 %collective-permute-done.52 = bf16[192,1728]{1,0:T(8,128)(2,1)S(1)} collective-permute-done((bf16[192,1728]{1,0:T(8,128)(2,1)S(1)}, bf16[192,1728]{1,0:T(8,128)(2,1)S(1)}, u32[]{:S(2)}, u32[]{:S(2)}) %collective-permute-start.52) | collective-permute-done | bytes 663584 | tf_op jit(solution)/shard_map/ppermute | solution.py:67
  1026.5 14.5 %collective-permute-done.57 = bf16[192,1728]{1,0:T(8,128)(2,1)S(1)} collective-permute-done((bf16[192,1728]{1,0:T(8,128)(2,1)S(1)}, bf16[192,1728]{1,0:T(8,128)(2,1)S(1)}, u32[]{:S(2)}, u32[]{:S(2)}) %collective-permute-start.57) | collective-permute-done | bytes 663584 | tf_op jit(solution)/shard_map/ppermute | solution.py:67
  1041.3 14.5 %collective-permute-done.62 = bf16[192,1728]{1,0:T(8,128)(2,1)S(1)} collective-permute-done((bf16[192,1728]{1,0:T(8,128)(2,1)S(1)}, bf16[192,1728]{1,0:T(8,128)(2,1)S(1)}, u32[]{:S(2)}, u32[]{:S(2)}) %collective-permute-start.62) | collective-permute-done | bytes 663584 | tf_op jit(solution)/shard_map/ppermute | solution.py:67
  1056.0 14.5 %collective-permute-done.53 = bf16[192,1728]{1,0:T(8,128)(2,1)S(1)} collective-permute-done((bf16[192,1728]{1,0:T(8,128)(2,1)S(1)}, bf16[192,1728]{1,0:T(8,128)(2,1)S(1)}, u32[]{:S(2)}, u32[]{:S(2)}) %collective-permute-start.53) | collective-permute-done | bytes 663584 | tf_op jit(solution)/shard_map/ppermute | solution.py:67
  1070.8 14.5 %collective-permute-done.58 = bf16[192,1728]{1,0:T(8,128)(2,1)S(1)} collective-permute-done((bf16[192,1728]{1,0:T(8,128)(2,1)S(1)}, bf16[192,1728]{1,0:T(8,128)(2,1)S(1)}, u32[]{:S(2)}, u32[]{:S(2)}) %collective-permute-start.58) | collective-permute-done | bytes 663584 | tf_op jit(solution)/shard_map/ppermute | solution.py:67
  1085.5 14.5 %collective-permute-done.63 = bf16[192,1728]{1,0:T(8,128)(2,1)S(1)} collective-permute-done((bf16[192,1728]{1,0:T(8,128)(2,1)S(1)}, bf16[192,1728]{1,0:T(8,128)(2,1)S(1)}, u32[]{:S(2)}, u32[]{:S(2)}) %collective-permute-start.63) | collective-permute-done | bytes 663584 | tf_op jit(solution)/shard_map/ppermute | solution.py:67
  1100.3 14.5 %collective-permute-done.54 = bf16[192,1728]{1,0:T(8,128)(2,1)S(1)} collective-permute-done((bf16[192,1728]{1,0:T(8,128)(2,1)S(1)}, bf16[192,1728]{1,0:T(8,128)(2,1)S(1)}, u32[]{:S(2)}, u32[]{:S(2)}) %collective-permute-start.54) | collective-permute-done | bytes 663584 | tf_op jit(solution)/shard_map/ppermute | solution.py:67
  1114.9 14.6 %collective-permute-done.59 = bf16[192,1728]{1,0:T(8,128)(2,1)S(1)} collective-permute-done((bf16[192,1728]{1,0:T(8,128)(2,1)S(1)}, bf16[192,1728]{1,0:T(8,128)(2,1)S(1)}, u32[]{:S(2)}, u32[]{:S(2)}) %collective-permute-start.59) | collective-permute-done | bytes 663584 | tf_op jit(solution)/shard_map/ppermute | solution.py:67
  1133.5 9.8 collective-permute-done.64
  (640 shorter events, 250.0 us)
Async XLA Ops:
  1.6 90.4 %collective-permute-start = (bf16[3,2,1536]{2,1,0:T(2,128)(2,1)S(1)}, bf16[3,2,1536]{2,1,0:T(2,128)(2,1)S(1)}, u32[]{:S(2)}, u32[]{:S(2)}) collective-permute-start(bf16[3,2,1536]{2,1,0:T(2,128)(2,1)S(1)} %slice.267), channel_id=1, source_target_pairs={{0,4},{4,8},{8,12},{12,16},{16,20},{20,24},{24,28},{1,5},{5,9},{9,... | collective-permute-start | bytes 55304 | tf_op jit(solution)/shard_map/ppermute | solution.py:42
  6.4 97.8 %collective-permute-start.2 = (bf16[1536,384]{1,0:T(8,128)(2,1)}, bf16[1536,384]{1,0:T(8,128)(2,1)}, u32[]{:S(2)}, u32[]{:S(2)}) collective-permute-start(bf16[1536,384]{1,0:T(8,128)(2,1)} %param.13), channel_id=1, source_target_pairs={{0,1},{1,0},{2,3},{3,2},{4,5},{5,4},{6,7},{7,6},{8,9},{9,8},{10,11... | collective-permute-start | bytes 3538952 | tf_op jit(solution)/shard_map/ppermute | solution.py:31
  15.2 203.0 %collective-permute-start.6 = (bf16[1536,1728]{0,1:T(8,128)(2,1)}, bf16[1536,1728]{0,1:T(8,128)(2,1)}, u32[]{:S(2)}, u32[]{:S(2)}) collective-permute-start(bf16[1536,1728]{0,1:T(8,128)(2,1)} %get-tuple-element.93), channel_id=1, source_target_pairs={{0,1},{1,0},{2,3},{3,2},{4,5},{5,4},{6,7},{7,6},{8,9},{9,8},{10,11... | collective-permute-start | bytes 15925256 | tf_op jit(solution)/shard_map/ppermute | solution.py:31
  15.7 228.5 %collective-permute-start.7 = (bf16[1536,1728]{0,1:T(8,128)(2,1)}, bf16[1536,1728]{0,1:T(8,128)(2,1)}, u32[]{:S(2)}, u32[]{:S(2)}) collective-permute-start(bf16[1536,1728]{0,1:T(8,128)(2,1)} %param.16), channel_id=1, source_target_pairs={{0,1},{1,0},{2,3},{3,2},{4,5},{5,4},{6,7},{7,6},{8,9},{9,8},{10,11... | collective-permute-start | bytes 15925256 | tf_op jit(solution)/shard_map/ppermute | solution.py:31
  101.9 1.9 collective-permute-start.1
  102.6 6.2 collective-permute-start.9
  103.8 5.2 collective-permute-start.13
  106.7 20.5 %collective-permute-start.3 = (bf16[256,1536]{1,0:T(8,128)(2,1)S(1)}, bf16[256,1536]{1,0:T(8,128)(2,1)S(1)}, u32[]{:S(2)}, u32[]{:S(2)}) collective-permute-start(bf16[256,1536]{1,0:T(8,128)(2,1)S(1)} %convolution_convert_fusion.6), channel_id=1, source_target_pairs={{0,2},{1,3},{2,0},{3,1},{4,6},{5,7},{6,4},{7,5},{8,10},{9,11},{10,... | collective-permute-start | bytes 2359304 | tf_op jit(solution)/shard_map/ppermute | solution.py:36
  108.9 183.2 %collective-permute-start.5 = (bf16[1536,1728]{0,1:T(8,128)(2,1)S(1)}, bf16[1536,1728]{0,1:T(8,128)(2,1)}, u32[]{:S(2)}, u32[]{:S(2)}) collective-permute-start(bf16[1536,1728]{0,1:T(8,128)(2,1)S(1)} %bitcast.416), channel_id=1, source_target_pairs={{0,1},{1,0},{2,3},{3,2},{4,5},{5,4},{6,7},{7,6},{8,9},{9,8},{10,11... | collective-permute-start | bytes 15925256 | tf_op jit(solution)/shard_map/ppermute | solution.py:31
  109.9 34.1 %collective-permute-start.10 = (bf16[256,1536]{1,0:T(8,128)(2,1)S(1)}, bf16[256,1536]{1,0:T(8,128)(2,1)S(1)}, u32[]{:S(2)}, u32[]{:S(2)}) collective-permute-start(bf16[256,1536]{1,0:T(8,128)(2,1)S(1)} %convolution_convert_fusion.5), channel_id=1, source_target_pairs={{0,2},{1,3},{2,0},{3,1},{4,6},{5,7},{6,4},{7,5},{8,10},{9,11},{10,... | collective-permute-start | bytes 2359304 | tf_op jit(solution)/shard_map/ppermute | solution.py:36
  130.4 30.4 %collective-permute-start.4 = (bf16[256,1536]{1,0:T(8,128)(2,1)S(1)}, bf16[256,1536]{1,0:T(8,128)(2,1)S(1)}, u32[]{:S(2)}, u32[]{:S(2)}) collective-permute-start(bf16[256,1536]{1,0:T(8,128)(2,1)S(1)} %get-tuple-element.64), channel_id=1, source_target_pairs={{0,2},{1,3},{2,0},{3,1},{4,6},{5,7},{6,4},{7,5},{8,10},{9,11},{10,... | collective-permute-start | bytes 2359304 | tf_op jit(solution)/shard_map/ppermute | solution.py:36
  144.0 33.7 %collective-permute-start.14 = (bf16[256,1536]{1,0:T(8,128)(2,1)S(1)}, bf16[256,1536]{1,0:T(8,128)(2,1)S(1)}, u32[]{:S(2)}, u32[]{:S(2)}) collective-permute-start(bf16[256,1536]{1,0:T(8,128)(2,1)S(1)} %convolution_convert_fusion.4), channel_id=1, source_target_pairs={{0,2},{1,3},{2,0},{3,1},{4,6},{5,7},{6,4},{7,5},{8,10},{9,11},{10,... | collective-permute-start | bytes 2359304 | tf_op jit(solution)/shard_map/ppermute | solution.py:36
  161.1 32.6 %collective-permute-start.11 = (bf16[256,1536]{1,0:T(8,128)(2,1)S(1)}, bf16[256,1536]{1,0:T(8,128)(2,1)S(1)}, u32[]{:S(2)}, u32[]{:S(2)}) collective-permute-start(bf16[256,1536]{1,0:T(8,128)(2,1)S(1)} %get-tuple-element.62), channel_id=1, source_target_pairs={{0,2},{1,3},{2,0},{3,1},{4,6},{5,7},{6,4},{7,5},{8,10},{9,11},{10,... | collective-permute-start | bytes 2359304 | tf_op jit(solution)/shard_map/ppermute | solution.py:36
  194.1 21.0 %collective-permute-start.15 = (bf16[256,1536]{1,0:T(8,128)(2,1)S(1)}, bf16[256,1536]{1,0:T(8,128)(2,1)S(1)}, u32[]{:S(2)}, u32[]{:S(2)}) collective-permute-start(bf16[256,1536]{1,0:T(8,128)(2,1)S(1)} %get-tuple-element.60), channel_id=1, source_target_pairs={{0,2},{1,3},{2,0},{3,1},{4,6},{5,7},{6,4},{7,5},{8,10},{9,11},{10,... | collective-permute-start | bytes 2359304 | tf_op jit(solution)/shard_map/ppermute | solution.py:36
  415.3 82.3 %collective-permute-start.17 = (bf16[256,1536]{1,0:T(8,128)(2,1)S(1)}, bf16[256,1536]{1,0:T(8,128)(2,1)S(1)}, u32[]{:S(2)}, u32[]{:S(2)}) collective-permute-start(bf16[256,1536]{1,0:T(8,128)(2,1)S(1)} %slice.600), channel_id=1, source_target_pairs={{0,2},{1,3},{2,0},{3,1},{4,6},{5,7},{6,4},{7,5},{8,10},{9,11},{10,... | collective-permute-start | bytes 2359304 | tf_op jit(solution)/shard_map/ppermute | solution.py:36
  426.8 89.7 %collective-permute-start.8 = (bf16[256,1536]{1,0:T(8,128)(2,1)}, bf16[256,1536]{1,0:T(8,128)(2,1)}, u32[]{:S(2)}, u32[]{:S(2)}) collective-permute-start(bf16[256,1536]{1,0:T(8,128)(2,1)} %slice.603), channel_id=1, source_target_pairs={{0,2},{1,3},{2,0},{3,1},{4,6},{5,7},{6,4},{7,5},{8,10},{9,11},{10,... | collective-permute-start | bytes 2359304 | tf_op jit(solution)/shard_map/ppermute | solution.py:36
  449.0 67.6 %collective-permute-start.24 = (bf16[256,1536]{1,0:T(8,128)(2,1)}, bf16[256,1536]{1,0:T(8,128)(2,1)S(1)}, u32[]{:S(2)}, u32[]{:S(2)}) collective-permute-start(bf16[256,1536]{1,0:T(8,128)(2,1)} %slice.598), channel_id=1, source_target_pairs={{0,2},{1,3},{2,0},{3,1},{4,6},{5,7},{6,4},{7,5},{8,10},{9,11},{10,... | collective-permute-start | bytes 2359304 | tf_op jit(solution)/shard_map/ppermute | solution.py:36
  459.4 57.7 %collective-permute-start.12 = (bf16[256,1536]{1,0:T(8,128)(2,1)}, bf16[256,1536]{1,0:T(8,128)(2,1)}, u32[]{:S(2)}, u32[]{:S(2)}) collective-permute-start(bf16[256,1536]{1,0:T(8,128)(2,1)} %slice.602), channel_id=1, source_target_pairs={{0,2},{1,3},{2,0},{3,1},{4,6},{5,7},{6,4},{7,5},{8,10},{9,11},{10,... | collective-permute-start | bytes 2359304 | tf_op jit(solution)/shard_map/ppermute | solution.py:36
  470.7 46.5 %collective-permute-start.16 = (bf16[256,1536]{1,0:T(8,128)(2,1)}, bf16[256,1536]{1,0:T(8,128)(2,1)}, u32[]{:S(2)}, u32[]{:S(2)}) collective-permute-start(bf16[256,1536]{1,0:T(8,128)(2,1)} %slice.601), channel_id=1, source_target_pairs={{0,2},{1,3},{2,0},{3,1},{4,6},{5,7},{6,4},{7,5},{8,10},{9,11},{10,... | collective-permute-start | bytes 2359304 | tf_op jit(solution)/shard_map/ppermute | solution.py:36
  497.6 20.4 %collective-permute-start.30 = (bf16[256,1536]{1,0:T(8,128)(2,1)}, bf16[256,1536]{1,0:T(8,128)(2,1)S(1)}, u32[]{:S(2)}, u32[]{:S(2)}) collective-permute-start(bf16[256,1536]{1,0:T(8,128)(2,1)} %slice.596), channel_id=1, source_target_pairs={{0,2},{1,3},{2,0},{3,1},{4,6},{5,7},{6,4},{7,5},{8,10},{9,11},{10,... | collective-permute-start | bytes 2359304 | tf_op jit(solution)/shard_map/ppermute | solution.py:36
  516.5 174.0 %collective-permute-start.22 = (bf16[1536,1152]{0,1:T(8,128)(2,1)S(1)}, bf16[1536,1152]{0,1:T(8,128)(2,1)}, u32[]{:S(2)}, u32[]{:S(2)}) collective-permute-start(bf16[1536,1152]{0,1:T(8,128)(2,1)S(1)} %bitcast.400), channel_id=1, source_target_pairs={{0,1},{1,0},{2,3},{3,2},{4,5},{5,4},{6,7},{7,6},{8,9},{9,8},{10,11... | collective-permute-start | bytes 10616840 | tf_op jit(solution)/shard_map/ppermute | solution.py:31
  516.6 212.6 %collective-permute-start.60 = (bf16[1536,1728]{0,1:T(8,128)(2,1)}, bf16[1536,1728]{0,1:T(8,128)(2,1)}, u32[]{:S(2)}, u32[]{:S(2)}) collective-permute-start(bf16[1536,1728]{0,1:T(8,128)(2,1)} %convolution_convert_fusion), channel_id=1, source_target_pairs={{0,1},{1,0},{2,3},{3,2},{4,5},{5,4},{6,7},{7,6},{8,9},{9,8},{10,11... | collective-permute-start | bytes 15925256 | tf_op jit(solution)/shard_map/ppermute | solution.py:31
  517.1 227.0 %collective-permute-start.50 = (bf16[1536,1728]{0,1:T(8,128)(2,1)}, bf16[1536,1728]{0,1:T(8,128)(2,1)}, u32[]{:S(2)}, u32[]{:S(2)}) collective-permute-start(bf16[1536,1728]{0,1:T(8,128)(2,1)} %convolution_convert_fusion.2), channel_id=1, source_target_pairs={{0,1},{1,0},{2,3},{3,2},{4,5},{5,4},{6,7},{7,6},{8,9},{9,8},{10,11... | collective-permute-start | bytes 15925256 | tf_op jit(solution)/shard_map/ppermute | solution.py:31
  526.4 18.1 %collective-permute-start.18 = (bf16[256,1536]{1,0:T(8,128)(2,1)S(1)}, bf16[256,1536]{1,0:T(8,128)(2,1)S(1)}, u32[]{:S(2)}, u32[]{:S(2)}) collective-permute-start(bf16[256,1536]{1,0:T(8,128)(2,1)S(1)} %get-tuple-element.72), channel_id=1, source_target_pairs={{0,2},{1,3},{2,0},{3,1},{4,6},{5,7},{6,4},{7,5},{8,10},{9,11},{10,... | collective-permute-start | bytes 2359304 | tf_op jit(solution)/shard_map/ppermute | solution.py:36
  546.8 4.1 collective-permute-start.19
  548.8 19.9 %collective-permute-start.25 = (bf16[256,1536]{1,0:T(8,128)(2,1)S(1)}, bf16[256,1536]{1,0:T(8,128)(2,1)S(1)}, u32[]{:S(2)}, u32[]{:S(2)}) collective-permute-start(bf16[256,1536]{1,0:T(8,128)(2,1)S(1)} %get-tuple-element.69), channel_id=1, source_target_pairs={{0,2},{1,3},{2,0},{3,1},{4,6},{5,7},{6,4},{7,5},{8,10},{9,11},{10,... | collective-permute-start | bytes 2359304 | tf_op jit(solution)/shard_map/ppermute | solution.py:36
  571.0 4.1 collective-permute-start.26
  572.9 19.9 %collective-permute-start.31 = (bf16[256,1536]{1,0:T(8,128)(2,1)S(1)}, bf16[256,1536]{1,0:T(8,128)(2,1)S(1)}, u32[]{:S(2)}, u32[]{:S(2)}) collective-permute-start(bf16[256,1536]{1,0:T(8,128)(2,1)S(1)} %get-tuple-element.66), channel_id=1, source_target_pairs={{0,2},{1,3},{2,0},{3,1},{4,6},{5,7},{6,4},{7,5},{8,10},{9,11},{10,... | collective-permute-start | bytes 2359304 | tf_op jit(solution)/shard_map/ppermute | solution.py:36
  595.1 5.3 collective-permute-start.32
  598.9 86.8 %collective-permute-start.45 = (bf16[1536,384]{1,0:T(8,128)(2,1)}, bf16[1536,384]{1,0:T(8,128)(2,1)}, u32[]{:S(2)}, u32[]{:S(2)}) collective-permute-start(bf16[1536,384]{1,0:T(8,128)(2,1)} %convolution_convert_fusion.3), channel_id=1, source_target_pairs={{0,1},{1,0},{2,3},{3,2},{4,5},{5,4},{6,7},{7,6},{8,9},{9,8},{10,11... | collective-permute-start | bytes 3538952 | tf_op jit(solution)/shard_map/ppermute | solution.py:31
  618.6 5.8 collective-permute-start.33
  624.4 5.9 collective-permute-start.20
  630.2 6.4 collective-permute-start.27
  636.6 54.5 %collective-permute-start.34 = (bf16[512,1152]{1,0:T(8,128)(2,1)}, bf16[512,1152]{1,0:T(8,128)(2,1)}, u32[]{:S(2)}, u32[]{:S(2)}) collective-permute-start(bf16[512,1152]{1,0:T(8,128)(2,1)} %pad_maximum_fusion.23), channel_id=1, source_target_pairs={{0,1},{1,0},{2,3},{3,2},{4,5},{5,4},{6,7},{7,6},{8,9},{9,8},{10,11... | collective-permute-start | bytes 3538952 | tf_op jit(solution)/shard_map/ppermute | solution.py:31
  685.7 73.0 %collective-permute-start.55 = (bf16[1536,1728]{0,1:T(8,128)(2,1)}, bf16[1536,1728]{0,1:T(8,128)(2,1)}, u32[]{:S(2)}, u32[]{:S(2)}) collective-permute-start(bf16[1536,1728]{0,1:T(8,128)(2,1)} %convolution_convert_fusion.1), channel_id=1, source_target_pairs={{0,1},{1,0},{2,3},{3,2},{4,5},{5,4},{6,7},{7,6},{8,9},{9,8},{10,11... | collective-permute-start | bytes 15925256 | tf_op jit(solution)/shard_map/ppermute | solution.py:31
  690.5 17.3 %collective-permute-start.21 = (bf16[512,1152]{1,0:T(8,128)(2,1)S(1)}, bf16[512,1152]{1,0:T(8,128)(2,1)S(1)}, u32[]{:S(2)}, u32[]{:S(2)}) collective-permute-start(bf16[512,1152]{1,0:T(8,128)(2,1)S(1)} %pad_maximum_fusion.21), channel_id=1, source_target_pairs={{0,1},{1,0},{2,3},{3,2},{4,5},{5,4},{6,7},{7,6},{8,9},{9,8},{10,11... | collective-permute-start | bytes 3538952 | tf_op jit(solution)/shard_map/ppermute | solution.py:31
  691.1 16.5 %collective-permute-start.46 = (bf16[4,192,384]{2,1,0:T(8,128)(2,1)S(1)}, bf16[4,192,384]{2,1,0:T(8,128)(2,1)S(1)}, u32[]{:S(2)}, u32[]{:S(2)}) collective-permute-start(bf16[4,192,384]{2,1,0:T(8,128)(2,1)S(1)} %dynamic-slice_bitcast_fusion.13), channel_id=1, source_target_pairs={{0,4},{4,0},{8,12},{12,8},{16,20},{20,16},{24,28},{28,24},{1,5},{5... | collective-permute-start | bytes 1769480 | tf_op jit(solution)/shard_map/ppermute | solution.py:60
  707.6 10.1 collective-permute-start.28
  707.8 8.1 collective-permute-start.47
  715.9 88.5 %collective-permute-start.41 = (bf16[4,192,1152]{2,1,0:T(8,128)(2,1)}, bf16[4,192,1152]{2,1,0:T(8,128)(2,1)}, u32[]{:S(2)}, u32[]{:S(2)}) collective-permute-start(bf16[4,192,1152]{2,1,0:T(8,128)(2,1)} %dynamic-slice_bitcast_fusion.3), channel_id=1, source_target_pairs={{0,4},{4,0},{8,12},{12,8},{16,20},{20,16},{24,28},{28,24},{1,5},{5... | collective-permute-start | bytes 5308424 | tf_op jit(solution)/shard_map/ppermute | solution.py:60
  717.7 10.3 collective-permute-start.48
  728.0 81.3 %collective-permute-start.35 = (bf16[256,1536]{1,0:T(8,128)(2,1)}, bf16[256,1536]{1,0:T(8,128)(2,1)}, u32[]{:S(2)}, u32[]{:S(2)}) collective-permute-start(bf16[256,1536]{1,0:T(8,128)(2,1)} %slice.595), channel_id=1, source_target_pairs={{0,2},{1,3},{2,0},{3,1},{4,6},{5,7},{6,4},{7,5},{8,10},{9,11},{10,... | collective-permute-start | bytes 2359304 | tf_op jit(solution)/shard_map/ppermute | solution.py:36
  729.2 80.9 %collective-permute-start.23 = (bf16[256,1536]{1,0:T(8,128)(2,1)}, bf16[256,1536]{1,0:T(8,128)(2,1)}, u32[]{:S(2)}, u32[]{:S(2)}) collective-permute-start(bf16[256,1536]{1,0:T(8,128)(2,1)} %slice.599), channel_id=1, source_target_pairs={{0,2},{1,3},{2,0},{3,1},{4,6},{5,7},{6,4},{7,5},{8,10},{9,11},{10,... | collective-permute-start | bytes 2359304 | tf_op jit(solution)/shard_map/ppermute | solution.py:36
  744.2 70.8 %collective-permute-start.29 = (bf16[256,1536]{1,0:T(8,128)(2,1)}, bf16[256,1536]{1,0:T(8,128)(2,1)}, u32[]{:S(2)}, u32[]{:S(2)}) collective-permute-start(bf16[256,1536]{1,0:T(8,128)(2,1)} %slice.597), channel_id=1, source_target_pairs={{0,2},{1,3},{2,0},{3,1},{4,6},{5,7},{6,4},{7,5},{8,10},{9,11},{10,... | collective-permute-start | bytes 2359304 | tf_op jit(solution)/shard_map/ppermute | solution.py:36
  758.7 60.3 %collective-permute-start.49 = (bf16[192,384]{1,0:T(8,128)(2,1)S(1)}, bf16[192,384]{1,0:T(8,128)(2,1)S(1)}, u32[]{:S(2)}, u32[]{:S(2)}) collective-permute-start(bf16[192,384]{1,0:T(8,128)(2,1)S(1)} %fusion.176), channel_id=1, source_target_pairs={{0,8},{4,12},{8,16},{12,20},{16,24},{20,28},{24,0},{28,4},{1,9},{5... | collective-permute-start | bytes 442376 | tf_op jit(solution)/shard_map/ppermute | solution.py:67
  804.4 205.1 %collective-permute-start.61 = (bf16[4,192,1728]{2,1,0:T(8,128)(2,1)}, bf16[4,192,1728]{2,1,0:T(8,128)(2,1)}, u32[]{:S(2)}, u32[]{:S(2)}) collective-permute-start(bf16[4,192,1728]{2,1,0:T(8,128)(2,1)} %dynamic-slice_bitcast_fusion), channel_id=1, source_target_pairs={{0,4},{4,0},{8,12},{12,8},{16,20},{20,16},{24,28},{28,24},{1,5},{5... | collective-permute-start | bytes 7962632 | tf_op jit(solution)/shard_map/ppermute | solution.py:60
  809.4 194.2 %collective-permute-start.51 = (bf16[4,192,1728]{2,1,0:T(8,128)(2,1)}, bf16[4,192,1728]{2,1,0:T(8,128)(2,1)}, u32[]{:S(2)}, u32[]{:S(2)}) collective-permute-start(bf16[4,192,1728]{2,1,0:T(8,128)(2,1)} %dynamic-slice_bitcast_fusion.2), channel_id=1, source_target_pairs={{0,4},{4,0},{8,12},{12,8},{16,20},{20,16},{24,28},{28,24},{1,5},{5... | collective-permute-start | bytes 7962632 | tf_op jit(solution)/shard_map/ppermute | solution.py:60
  810.2 196.1 %collective-permute-start.56 = (bf16[4,192,1728]{2,1,0:T(8,128)(2,1)}, bf16[4,192,1728]{2,1,0:T(8,128)(2,1)}, u32[]{:S(2)}, u32[]{:S(2)}) collective-permute-start(bf16[4,192,1728]{2,1,0:T(8,128)(2,1)} %dynamic-slice_bitcast_fusion.1), channel_id=1, source_target_pairs={{0,4},{4,0},{8,12},{12,8},{16,20},{20,16},{24,28},{28,24},{1,5},{5... | collective-permute-start | bytes 7962632 | tf_op jit(solution)/shard_map/ppermute | solution.py:60
  814.9 12.2 %collective-permute-start.42 = (bf16[192,1152]{1,0:T(8,128)(2,1)}, bf16[192,1152]{1,0:T(8,128)(2,1)}, u32[]{:S(2)}, u32[]{:S(2)}) collective-permute-start(bf16[192,1152]{1,0:T(8,128)(2,1)} %dynamic-slice_bitcast_fusion.26), channel_id=1, source_target_pairs={{0,8},{4,12},{8,16},{12,20},{16,24},{20,28},{24,0},{28,4},{1,9},{5... | collective-permute-start | bytes 1327112 | tf_op jit(solution)/shard_map/ppermute | solution.py:67
  820.9 7.4 collective-permute-start.37
  828.3 157.5 %collective-permute-start.43 = (bf16[192,1152]{1,0:T(8,128)(2,1)S(1)}, bf16[192,1152]{1,0:T(8,128)(2,1)S(1)}, u32[]{:S(2)}, u32[]{:S(2)}) collective-permute-start(bf16[192,1152]{1,0:T(8,128)(2,1)S(1)} %fusion.160), channel_id=1, source_target_pairs={{0,8},{4,12},{8,16},{12,20},{16,24},{20,28},{24,0},{28,4},{1,9},{5... | collective-permute-start | bytes 1327112 | tf_op jit(solution)/shard_map/ppermute | solution.py:67
  828.4 155.8 %collective-permute-start.38 = (f32[5,1536]{1,0:T(8,128)S(1)}, f32[5,1536]{1,0:T(8,128)S(1)}, u32[]{:S(2)}, u32[]{:S(2)}) collective-permute-start(f32[5,1536]{1,0:T(8,128)S(1)} %add.688), channel_id=1, source_target_pairs={{0,4},{4,0},{8,12},{12,8},{16,20},{20,16},{24,28},{28,24},{1,5},{5... | collective-permute-start | bytes 92168 | tf_op jit(solution)/shard_map/ppermute | solution.py:80
  984.2 6.2 collective-permute-start.39
  985.9 15.5 %collective-permute-start.44 = (bf16[192,1152]{1,0:T(8,128)(2,1)S(1)}, bf16[192,1152]{1,0:T(8,128)(2,1)}, u32[]{:S(2)}, u32[]{:S(2)}) collective-permute-start(bf16[192,1152]{1,0:T(8,128)(2,1)S(1)} %fusion.159), channel_id=1, source_target_pairs={{0,8},{4,12},{8,16},{12,20},{16,24},{20,28},{24,0},{28,4},{1,9},{5... | collective-permute-start | bytes 1327112 | tf_op jit(solution)/shard_map/ppermute | solution.py:67
  990.5 9.7 collective-permute-start.40
  1006.2 20.1 %collective-permute-start.52 = (bf16[192,1728]{1,0:T(8,128)(2,1)S(1)}, bf16[192,1728]{1,0:T(8,128)(2,1)S(1)}, u32[]{:S(2)}, u32[]{:S(2)}) collective-permute-start(bf16[192,1728]{1,0:T(8,128)(2,1)S(1)} %dynamic-slice_bitcast_fusion.12), channel_id=1, source_target_pairs={{0,8},{4,12},{8,16},{12,20},{16,24},{20,28},{24,0},{28,4},{1,9},{5... | collective-permute-start | bytes 1990664 | tf_op jit(solution)/shard_map/ppermute | solution.py:67
  1009.0 32.1 %collective-permute-start.57 = (bf16[192,1728]{1,0:T(8,128)(2,1)S(1)}, bf16[192,1728]{1,0:T(8,128)(2,1)S(1)}, u32[]{:S(2)}, u32[]{:S(2)}) collective-permute-start(bf16[192,1728]{1,0:T(8,128)(2,1)S(1)} %dynamic-slice_bitcast_fusion.11), channel_id=1, source_target_pairs={{0,8},{4,12},{8,16},{12,20},{16,24},{20,28},{24,0},{28,4},{1,9},{5... | collective-permute-start | bytes 1990664 | tf_op jit(solution)/shard_map/ppermute | solution.py:67
  1012.1 43.7 %collective-permute-start.62 = (bf16[192,1728]{1,0:T(8,128)(2,1)S(1)}, bf16[192,1728]{1,0:T(8,128)(2,1)S(1)}, u32[]{:S(2)}, u32[]{:S(2)}) collective-permute-start(bf16[192,1728]{1,0:T(8,128)(2,1)S(1)} %dynamic-slice_bitcast_fusion.10), channel_id=1, source_target_pairs={{0,8},{4,12},{8,16},{12,20},{16,24},{20,28},{24,0},{28,4},{1,9},{5... | collective-permute-start | bytes 1990664 | tf_op jit(solution)/shard_map/ppermute | solution.py:67
  1026.5 44.1 %collective-permute-start.53 = (bf16[192,1728]{1,0:T(8,128)(2,1)S(1)}, bf16[192,1728]{1,0:T(8,128)(2,1)S(1)}, u32[]{:S(2)}, u32[]{:S(2)}) collective-permute-start(bf16[192,1728]{1,0:T(8,128)(2,1)S(1)} %fusion.149), channel_id=1, source_target_pairs={{0,8},{4,12},{8,16},{12,20},{16,24},{20,28},{24,0},{28,4},{1,9},{5... | collective-permute-start | bytes 1990664 | tf_op jit(solution)/shard_map/ppermute | solution.py:67
  1041.2 44.1 %collective-permute-start.58 = (bf16[192,1728]{1,0:T(8,128)(2,1)S(1)}, bf16[192,1728]{1,0:T(8,128)(2,1)S(1)}, u32[]{:S(2)}, u32[]{:S(2)}) collective-permute-start(bf16[192,1728]{1,0:T(8,128)(2,1)S(1)} %fusion.146), channel_id=1, source_target_pairs={{0,8},{4,12},{8,16},{12,20},{16,24},{20,28},{24,0},{28,4},{1,9},{5... | collective-permute-start | bytes 1990664 | tf_op jit(solution)/shard_map/ppermute | solution.py:67
  1056.0 44.1 %collective-permute-start.63 = (bf16[192,1728]{1,0:T(8,128)(2,1)S(1)}, bf16[192,1728]{1,0:T(8,128)(2,1)S(1)}, u32[]{:S(2)}, u32[]{:S(2)}) collective-permute-start(bf16[192,1728]{1,0:T(8,128)(2,1)S(1)} %fusion.143), channel_id=1, source_target_pairs={{0,8},{4,12},{8,16},{12,20},{16,24},{20,28},{24,0},{28,4},{1,9},{5... | collective-permute-start | bytes 1990664 | tf_op jit(solution)/shard_map/ppermute | solution.py:67
  1070.7 44.1 %collective-permute-start.54 = (bf16[192,1728]{1,0:T(8,128)(2,1)S(1)}, bf16[192,1728]{1,0:T(8,128)(2,1)S(1)}, u32[]{:S(2)}, u32[]{:S(2)}) collective-permute-start(bf16[192,1728]{1,0:T(8,128)(2,1)S(1)} %fusion.148), channel_id=1, source_target_pairs={{0,8},{4,12},{8,16},{12,20},{16,24},{20,28},{24,0},{28,4},{1,9},{5... | collective-permute-start | bytes 1990664 | tf_op jit(solution)/shard_map/ppermute | solution.py:67
  1085.5 44.1 %collective-permute-start.59 = (bf16[192,1728]{1,0:T(8,128)(2,1)S(1)}, bf16[192,1728]{1,0:T(8,128)(2,1)S(1)}, u32[]{:S(2)}, u32[]{:S(2)}) collective-permute-start(bf16[192,1728]{1,0:T(8,128)(2,1)S(1)} %fusion.145), channel_id=1, source_target_pairs={{0,8},{4,12},{8,16},{12,20},{16,24},{20,28},{24,0},{28,4},{1,9},{5... | collective-permute-start | bytes 1990664 | tf_op jit(solution)/shard_map/ppermute | solution.py:67
  1100.2 43.1 %collective-permute-start.64 = (bf16[192,1728]{1,0:T(8,128)(2,1)S(1)}, bf16[192,1728]{1,0:T(8,128)(2,1)S(1)}, u32[]{:S(2)}, u32[]{:S(2)}) collective-permute-start(bf16[192,1728]{1,0:T(8,128)(2,1)S(1)} %fusion.142), channel_id=1, source_target_pairs={{0,8},{4,12},{8,16},{12,20},{16,24},{20,28},{24,0},{28,4},{1,9},{5... | collective-permute-start | bytes 1990664 | tf_op jit(solution)/shard_map/ppermute | solution.py:67
  (167 other events, 2478.7 us)

commit v2 on v0

v2 whole, which is shorter than its diff:
```python
import functools

import jax
import jax.numpy as jnp
from jax import lax
from jax.experimental import pallas as pl
from jax.experimental.pallas import tpu as pltpu
from jax.sharding import PartitionSpec as P

EPS = 1e-05
LOW = jnp.bfloat16
FULL = jnp.float32
CORES = 2
HALO = 16
HIDDEN_TILE = 512
LANES = 128
ROOM = 56 << 20


def norm_scale(rows):
    return lax.rsqrt(jnp.mean(rows * rows, axis=-1, keepdims=True) + EPS)


def norm_back(rows, scale, gain, grad):
    weighted = grad * gain
    inner = jnp.mean(weighted * rows, axis=-1, keepdims=True)
    d_rows = scale * weighted - rows * (scale * scale * scale) * inner
    d_gain = jnp.sum(grad * rows * scale, axis=0)
    return (d_rows, d_gain)


def dot(a, b, a_dim, b_dim):
    return lax.dot_general(
        a, b, (((a_dim,), (b_dim,)), ((), ())), preferred_element_type=jnp.float32
    )


def swap_cores(value):
    count = lax.axis_size("ch")
    return lax.ppermute(value, "ch", [(i, i ^ 1) for i in range(count)])


def shift_chips(value, steps):
    count = lax.axis_size("ch")
    return lax.ppermute(value, "ch", [(i, (i + CORES * steps) % count) for i in range(count)])


def shifted(value, axis, steps):
    count = lax.axis_size(axis)
    first, last = (max(0, -steps), min(count, count - steps))
    return lax.ppermute(value, axis, [(source, source + steps) for source in range(first, last)])


def tie(value, *before):
    return lax.optimization_barrier((value, before))[0]


def pick(value, index):
    return lax.dynamic_index_in_dim(value, index, 0, keepdims=False)


ANY = pl.BlockSpec(memory_space=pl.ANY)


def call(kernel, name, grid, scalars, operands, outputs, scratch, carry=(), after=(), flops=0):
    extra = len(carry) + len(after)

    def body(*refs):
        place = 1 + len(operands)
        return kernel(*refs[:place], *refs[place + extra :])

    moved = sum(a.size * a.dtype.itemsize for a, _, _ in operands)
    return pl.pallas_call(
        body,
        name=name,
        grid_spec=pltpu.PrefetchScalarGridSpec(
            num_scalar_prefetch=1,
            grid=grid,
            in_specs=[pl.BlockSpec(b, m) for _, b, m in operands] + [ANY] * extra,
            out_specs=[pl.BlockSpec(b, m) for _, _, b, m in outputs],
            scratch_shapes=scratch,
        ),
        out_shape=[jax.ShapeDtypeStruct(s, d) for s, d, _, _ in outputs],
        input_output_aliases={1 + len(operands) + i: i for i in range(len(carry))},
        compiler_params=pltpu.CompilerParams(
            vmem_limit_bytes=ROOM, dimension_semantics=("arbitrary",) * len(grid)
        ),
        cost_estimate=pl.CostEstimate(flops=flops, bytes_accessed=moved, transcendentals=0),
    )(scalars, *[a for a, _, _ in operands], *carry, *after)


def conv_forward(s, scalars, hidden, tail, gain, weight, taps, carry, after):
    seqs, length, width = hidden.shape
    chans = weight.shape[2]
    kinds = weight.shape[0]
    count = lax.axis_size("ch")
    chips = count // CORES
    share = length // count
    steps = taps.shape[0]
    wide = chans % 128 == 0

    def kernel(
        at, rows_ref, halo_ref, tail_ref, gain_ref, w_ref, taps_ref,
        flip_ref, proj_ref, conv_ref, mine_ref, theirs_ref, own_ref, flat
    ):
        i = pl.program_id(0)
        if wide:
            @pl.when(i == 0)
            def _():
                for k in range(kinds):
                    flat[:, k * chans : (k + 1) * chans] = w_ref[k]

        halo = jnp.where(i == 0, tail_ref[0].astype(FULL), halo_ref[0].astype(FULL))
        rows = jnp.concatenate([halo, rows_ref[0].astype(FULL)], axis=0)
        normed = (rows * norm_scale(rows) * gain_ref[...]).astype(LOW)
        flip_ref[...] = normed[HALO:].T
        if wide:
            proj = dot(normed, flat[...], 1, 0)
            b_gate, c_gate, x_val = [proj[:, k * chans : (k + 1) * chans] for k in range(kinds)]
        else:
            b_gate, c_gate, x_val = [dot(normed, w_ref[k], 1, 0) for k in range(kinds)]
        gated = (b_gate * x_val).astype(LOW).astype(FULL)
        conv = jnp.zeros((share, chans), FULL)
        for tap in range(steps):
            back = steps - 1 - tap
            conv = conv + taps_ref[tap : tap + 1] * gated[HALO - back : HALO - back + share]
        mixed = (c_gate[HALO:] * conv).astype(LOW)
        proj_ref[0] = b_gate[HALO:].astype(LOW)
        proj_ref[1] = c_gate[HALO:].astype(LOW)
        proj_ref[2] = x_val[HALO:].astype(LOW)
        conv_ref[...] = conv.astype(LOW)

        @pl.when(i == CORES * at[0] + at[1])
        def _():
            own_ref[...] = rows_ref[0]

        @pl.when(i % CORES == at[1])
        def _():
            mine_ref[0] = mixed

        @pl.when(i % CORES != at[1])
        def _():
            theirs_ref[0] = mixed

    away = lambda i, at: ((i // CORES + chips - at[0]) % chips, 0, 0)
    return call(
        kernel,
        "conv_forward",
        (count,),
        scalars,
        [
            (hidden, (1, share, width), lambda i, at: (s, i, 0)),
            (
                hidden,
                (1, HALO, width),
                lambda i, at: (s, jnp.maximum(i * (share // HALO) - 1, 0), 0),
            ),
            (tail, (1, HALO, width), lambda i, at: (s, 0, 0)),
            (gain, (1, width), lambda i, at: (0, 0)),
            (weight, weight.shape, lambda i, at: (0, 0, 0)),
            (taps, taps.shape, lambda i, at: (0, 0)),
        ],
        [
            ((width, seqs * length), LOW, (width, share), lambda i, at: (0, s * count + i)),
            ((kinds, length, chans), LOW, (kinds, share, chans), lambda i, at: (0, i, 0)),
            ((length, chans), LOW, (share, chans), lambda i, at: (i, 0)),
            ((chips, share, chans), LOW, (1, share, chans), away),
            ((chips, share, chans), LOW, (1, share, chans), away),
            ((share, width), LOW, (share, width), lambda i, at: (0, 0)),
        ],
        [pltpu.VMEM((width, kinds * chans) if wide else (HALO, 128), LOW)],
        carry,
        after,
        2 * length * width * kinds * chans,
    )


def act_back(scalars, cotangent, downs, after):
    seqs, length, width = cotangent.shape
    hid = downs[0].shape[0]
    count = lax.axis_size("ch")
    chips = count // CORES
    share = length // count
    many = seqs * chips * share
    cols = -(-hid // LANES) * LANES
    tile = min(HIDDEN_TILE, cols)
    steps = -(-hid // tile)
    last = hid - (steps - 1) * tile
    places = [(s, k) for s in range(seqs) for k in range(chips)]

    def kernel(at, *refs):
        grad_refs, refs = refs[: len(places)], refs[len(places) :]
        down0, down1, flip, out0, out1, own, grad = refs
        i = pl.program_id(0)

        @pl.when(i == 0)
        def _():
            for n, (s, k) in enumerate(places):
                value = grad_refs[n][0]
                if k == 0:
                    own[s] = value
                grad[n * share : (n + 1) * share] = value
                flip[:, n * share : (n + 1) * share] = value.T

        def units(size):
            for down, out in ((down0, out0), (down1, out1)):
                out[:, :size] = dot(grad[...], down[:size], 1, 1).astype(LOW)

        if last == tile:
            units(tile)
        else:
            pl.when(i < steps - 1)(lambda: units(tile))
            pl.when(i == steps - 1)(lambda: units(last))

    def place(s, k):
        return lambda i, at: (s, CORES * ((at[0] + k) % chips) + at[1], 0)

    operands = [(cotangent, (1, share, width), place(s, k)) for s, k in places]
    operands += [(d, (tile, width), lambda i, at: (i, 0)) for d in downs]
    return call(
        kernel,
        "act_back",
        (steps,),
        scalars,
        operands,
        [((width, many), LOW, (width, many), lambda i, at: (0, 0))]
        + [((many, cols), LOW, (many, tile), lambda i, at: (0, i))] * 2
        + [((seqs, share, width), LOW, (seqs, share, width), lambda i, at: (0, 0, 0))],
        [pltpu.VMEM((many, width), LOW)],
        (),
        after,
        4 * many * width * hid,
    )


def ffn(s, seqs, scalars, norms, d_acts, weights, carry, after):
    chips = len(norms)
    share, width = norms[0].shape
    hid = weights[0].shape[1]
    rows = chips * share
    tile = min(HIDDEN_TILE, -(-hid // LANES) * LANES)
    steps = -(-hid // tile)
    last = hid - (steps - 1) * tile

    def kernel(at, *refs):
        norm_refs, refs = refs[:chips], refs[chips:]
        back_refs, w_refs, refs = refs[:2], refs[2:4], refs[4:]
        acts, grads, flip_n, refs = refs[:2], refs[2:4], refs[4], refs[5:]
        mid_keep, mid_give, normed, mid = refs
        i = pl.program_id(0)

        @pl.when(i == 0)
        def _():
            for k in range(chips):
                normed[k * share : (k + 1) * share] = norm_refs[k][...]
                flip_n[:, k * share : (k + 1) * share] = norm_refs[k][...].T
            mid[...] = jnp.zeros_like(mid)

        def units(size):
            for half in range(2):
                gate_w, up_w = (w_refs[half][0, :size], w_refs[half][1, :size])
                gate = dot(normed[...], gate_w, 1, 1)
                up = dot(normed[...], up_w, 1, 1)
                d_act = back_refs[half][:, :size].astype(FULL)
                sigm = jax.nn.sigmoid(gate)
                silu = gate * sigm
                act = (silu * up).astype(LOW)
                d_gate = (d_act * up * (sigm * (1.0 + gate * (1.0 - sigm)))).astype(LOW)
                d_up = (d_act * silu).astype(LOW)
                acts[half][:, :size] = act
                grads[half][0, :, :size] = d_gate
                grads[half][1, :, :size] = d_up
                mid[...] += dot(d_gate, gate_w, 1, 0) + dot(d_up, up_w, 1, 0)
                if size < tile:
                    rest = jnp.zeros((rows, tile - size), LOW)
                    acts[half][:, size:] = rest
                    grads[half][0, :, size:] = rest
                    grads[half][1, :, size:] = rest

        if last == tile:
            units(tile)
        else:
            pl.when(i < steps - 1)(lambda: units(tile))
            pl.when(i == steps - 1)(lambda: units(last))

        @pl.when(i == steps - 1)
        def _():
            mid_keep[...] = mid[:share]
            for k in range(1, chips):
                mid_give[k - 1] = mid[k * share : (k + 1) * share].astype(LOW)

    fixed = lambda i, at: (0, 0)
    operands = [(n, (share, width), fixed) for n in norms]
    operands += [(d, (rows, tile), lambda i, at: (s, i)) for d in d_acts]
    operands += [(w, (2, tile, width), lambda i, at: (0, i, 0)) for w in weights]
    many = seqs * rows
    cols = -(-hid // LANES) * LANES
    outputs = [((many, cols), LOW, (rows, tile), lambda i, at: (s, i))] * 2
    outputs += [((2, many, cols), LOW, (2, rows, tile), lambda i, at: (0, s, i))] * 2
    outputs += [((width, many), LOW, (width, rows), lambda i, at: (0, s))]
    given = (chips - 1, share, width)
    outputs += [
        ((share, width), FULL, (share, width), fixed),
        (given, LOW, given, lambda i, at: (0, 0, 0)),
    ]
    return call(
        kernel,
        "ffn",
        (steps,),
        scalars,
        operands,
        outputs,
        [
            pltpu.VMEM((rows, width), LOW),
            pltpu.VMEM((rows, width), FULL),
        ],
        carry,
        after,
        8 * rows * width * 2 * hid,
    )


def down_product(seqs, scalars, acts, downs, after):
    many, cols = acts[0].shape
    hid, width = downs[0].shape
    rows = many // seqs
    chips = lax.axis_size("ch") // CORES
    share = rows // chips
    parts = 2
    wide = width // parts

    def kernel(at, act0, act1, down0, down1, keep, give):
        value = dot(act0[:, :hid], down0[...], 1, 0) + dot(act1[:, :hid], down1[...], 1, 0)
        keep[0] = value[:share]
        for k in range(1, chips):
            give[k - 1, 0] = value[k * share : (k + 1) * share].astype(LOW)

    act_spec = ((rows, cols), lambda i, s, at: (s, 0))
    down_spec = ((hid, wide), lambda i, s, at: (0, i))
    return call(
        kernel,
        "down_product",
        (parts, seqs),
        scalars,
        [(acts[0], *act_spec), (acts[1], *act_spec), (downs[0], *down_spec), (downs[1], *down_spec)],
        [
            ((seqs, share, width), FULL, (1, share, wide), lambda i, s, at: (s, 0, i)),
            (
                (chips - 1, seqs, share, width),
                LOW,
                (chips - 1, 1, share, wide),
                lambda i, s, at: (0, s, 0, i),
            ),
        ],
        [],
        (),
        after,
        4 * many * width * hid,
    )


def weight_grad(scalars, left, right, first, kinds, other=None, bit=None, after=()):
    width, tokens = left.shape
    cols = right.shape[2]
    count = lax.axis_size("seq")
    rows = width // count
    parts = 2
    tall = width // parts
    tops = count // (2 * parts)

    def kernel(at, left_ref, right_ref, *refs):
        value = dot(left_ref[...], right_ref[0], 1, 0)
        if bit is None:
            refs[0][0] = value.astype(LOW)
            return
        if other is not None:
            value = value + refs[0][0].astype(FULL)
        value = value.astype(LOW).reshape(tops >> bit, 2, 1 << bit, rows, cols)
        zero, one = [value[:, k].reshape(tops, rows, cols) for k in range(2)]
        keep, give = refs[-2:]

        @pl.when(at[2 + bit] == 0)
        def _():
            keep[0] = zero
            give[0] = one

        @pl.when(at[2 + bit] != 0)
        def _():
            keep[0] = one
            give[0] = zero

    operands = [
        (left, (tall, tokens), lambda k, i, at: (i, 0)),
        (right, (1, tokens, cols), lambda k, i, at: (first + k, 0, 0)),
    ]
    if other is not None:
        operands.append((other, (1, tall, cols), lambda k, i, at: (first + k, i, 0)))
    if bit is not None:
        block = (1, tops, rows, cols)
        outputs = [((kinds, count // 2, rows, cols), LOW, block, lambda k, i, at: (k, i, 0, 0))] * 2
    else:
        outputs = [((kinds, width, cols), LOW, (1, tall, cols), lambda k, i, at: (k, i, 0))]
    return call(
        kernel,
        "weight_grad",
        (kinds, parts),
        scalars,
        operands,
        outputs,
        [],
        (),
        after,
        2 * kinds * width * tokens * cols,
    )


def trade(value, bit):
    count = lax.axis_size("seq")
    return lax.ppermute(value, "seq", [(i, i ^ (1 << bit)) for i in range(count)])


def total(terms):
    value = terms[0].astype(FULL)
    for term in terms[1:]:
        value = value + term.astype(FULL)
    return value


def scatter_step(terms, bits):
    bit = bits[0]
    low = sum(1 for b in bits if b < bit)
    mine = (lax.axis_index("seq") >> bit) % 2

    def half(value, which):
        split = value.reshape((-1, 2, 1 << low) + value.shape[1:])
        part = lax.dynamic_index_in_dim(split, which, 1, keepdims=False)
        return part.reshape((-1,) + value.shape[1:])

    give = total([half(t, 1 - mine) for t in terms]).astype(LOW)
    return ([half(t, mine) for t in terms] + [trade(give, bit)], give)


def conv_backward(s, seqs, scalars, mine, other, proj, conv, taps, ahead, carry, after):
    kinds, length, chans = proj.shape
    chips, share, _ = mine.shape
    count = chips * CORES
    steps = taps.shape[0]

    def kernel(
        at, mine_ref, other_ref, proj_ref, conv_ref, taps_ref, ahead_ref,
        all_ref, keep_ref, give_ref, sums_ref, later
    ):
        i = count - 1 - pl.program_id(0)

        @pl.when(pl.program_id(0) == 0)
        def _():
            later[...] = ahead_ref[...]
            sums_ref[...] = jnp.zeros_like(sums_ref)

        own = i % CORES == at[1]
        d_mixed = jnp.where(own, mine_ref[0].astype(FULL), other_ref[0].astype(FULL))
        b_gate, c_gate, x_val = [proj_ref[k].astype(FULL) for k in range(kinds)]
        gated = (b_gate * x_val).astype(LOW).astype(FULL)
        d_c = d_mixed * conv_ref[...].astype(FULL)
        d_conv = d_mixed * c_gate
        longer = jnp.concatenate([d_conv, later[...]], axis=0)
        later[...] = d_conv[:HALO]
        d_gated = jnp.zeros((share, chans), FULL)
        for tap in range(steps):
            ahead_by = steps - 1 - tap
            term = longer[ahead_by : ahead_by + share]
            d_gated = d_gated + taps_ref[tap : tap + 1] * term
            sums_ref[tap : tap + 1] += jnp.sum(term * gated, axis=0, keepdims=True)
        d_gated = d_gated.astype(LOW).astype(FULL)
        values = [(d_gated * x_val).astype(LOW), d_c.astype(LOW), (d_gated * b_gate).astype(LOW)]
        value = jnp.concatenate(values, axis=1)
        all_ref[0] = value

        @pl.when(own)
        def _():
            keep_ref[0] = value

        @pl.when(jnp.logical_not(own))
        def _():
            give_ref[0] = value

    back = lambda i: count - 1 - i
    away = lambda i, at: ((back(i) // CORES + chips - at[0]) % chips, 0, 0)
    split = ((chips, share, kinds * chans), LOW, (1, share, kinds * chans), away)
    return call(
        kernel,
        "conv_backward",
        (count,),
        scalars,
        [
            (mine, (1, share, chans), away),
            (other, (1, share, chans), away),
            (proj, (kinds, share, chans), lambda i, at: (0, back(i), 0)),
            (conv, (share, chans), lambda i, at: (back(i), 0)),
            (taps, taps.shape, lambda i, at: (0, 0)),
            (ahead, (HALO, chans), lambda i, at: (0, 0)),
        ],
        [
            (
                (1, seqs * length, kinds * chans),
                LOW,
                (1, share, kinds * chans),
                lambda i, at: (0, s * count + back(i), 0),
            ),
            split,
            split,
            ((8, chans), FULL, (8, chans), lambda i, at: (0, 0)),
        ],
        [pltpu.VMEM((HALO, chans), FULL)],
        carry,
        after,
        40 * length * chans,
    )


def per_device(
    hidden,
    gain_in,
    in_weight,
    conv_weight,
    out_weight,
    gain_mid,
    gate_up_weight,
    down_weight,
    cotangent,
):
    seqs, length, width = hidden.shape
    count = lax.axis_size("ch")
    chips = count // CORES
    me = lax.axis_index("ch")
    core, chip = (me % CORES, me // CORES)
    places = lax.axis_size("seq").bit_length() - 1
    position = lax.axis_index("seq")
    scalars = jnp.stack([chip, core] + [(position >> b) % 2 for b in range(places)])
    scalars = scalars.astype(jnp.int32)
    share = length // count
    taps, chans = conv_weight.shape
    hid = down_weight.shape[1]
    conv_taps = conv_weight.astype(FULL)

    tail = shifted(hidden[:, length - HALO :], "seq", 1)
    out_other = swap_cores(out_weight)
    in_three = jnp.transpose(in_weight, (1, 0, 2))
    gate_up = jnp.transpose(gate_up_weight, (1, 2, 0))
    down = jnp.transpose(down_weight, (1, 0))
    gate_up_other = swap_cores(gate_up)
    down_other = swap_cores(down)
    in_other = swap_cores(in_three)
    downs = (down, down_other)
    gate_ups = (gate_up, gate_up_other)
    projs, convs, mixes, owns = ([], [], [], [])
    flips = {"in": (), "grad": ()}
    arrived = {}

    def forward(s, after):
        flip, proj, conv, mine, theirs, own = conv_forward(
            s, scalars, hidden, tail, gain_in[None], in_three, conv_taps, flips["in"], after
        )
        flips["in"] = (flip,)
        projs.append(proj)
        convs.append(conv)
        owns.append(own)
        mixes.append((mine, swap_cores(theirs)))
        return (conv,)

    def mix_part(s, k, mine, got):
        return dot(mine[k], out_weight, 1, 1) + dot(got[k], out_other, 1, 1)

    def mix_send(s, after):
        mine, got = mixes[s]
        got = tie(got, after)
        sent = [mix_part(s, k, mine, got).astype(LOW) for k in range(1, chips)]
        arrived[s] = [shift_chips(p, k + 1) for k, p in enumerate(sent)]
        return tuple(sent)

    resids, scales, normed = ([], [], [])

    def join(s, after):
        mine, got = mixes[s]
        pieces = tie(arrived[s], after)
        resid = owns[s].astype(FULL) + mix_part(s, 0, mine, got)
        for piece in pieces:
            resid = resid + piece.astype(FULL)
        scale = norm_scale(resid)
        low = (resid * scale * gain_mid).astype(LOW)
        resids.append(resid)
        scales.append(scale)
        normed.append([low] + [shift_chips(low, -k) for k in range(1, chips)])
        return (low,)

    def back(after):
        flips["grad"], own, other, state["cots"] = act_back(scalars, cotangent, downs, after)
        state["d_acts"] = (own, other)
        return (own,)

    state = {
        "ffn": (),
        "proj": (),
        "conv": jnp.zeros((taps, chans), FULL),
        "in": jnp.zeros((width,), FULL),
        "mid": jnp.zeros((width,), FULL),
    }
    results, d_resids, d_mixes = ([], [], [])

    def feed(s, after):
        out = ffn(s, seqs, scalars, normed[s], state["d_acts"], gate_ups, state["ffn"], after)
        state["ffn"] = tuple(out[:5])
        keep, give = out[5:]
        results.append((keep, [shift_chips(give[k - 1], k) for k in range(1, chips)]))
        return (give,)

    def middle(s, after):
        d_mid, pieces = results[s]
        for piece in tie(pieces, after):
            d_mid = d_mid + piece.astype(FULL)
        d_norm, gain_term = norm_back(resids[s], scales[s], gain_mid, d_mid)
        d_resid = state["cots"][s].astype(FULL) + d_norm
        low = d_resid.astype(LOW)
        state["mid"] = state["mid"] + gain_term
        d_resids.append(d_resid)
        d_mixes.append([low] + [shift_chips(low, -k) for k in range(1, chips)])
        return (low,)

    mixed_backs, d_mix_rows = ([], [])

    def mix_back(s, after):
        d_mix = jnp.concatenate(tie(d_mixes[s], after), axis=0)
        d_mix_rows.append(d_mix)
        other = dot(d_mix, out_other, 1, 0).astype(LOW)
        give = swap_cores(other).reshape(chips, share, chans)
        mine = dot(d_mix, out_weight, 1, 0).astype(LOW).reshape(chips, share, chans)
        first = (chips - chip) % chips
        head = jnp.where(core == 0, pick(mine, first)[:HALO], pick(give, first)[:HALO])
        ahead = shifted(head.astype(FULL) * projs[s][1, :HALO].astype(FULL), "seq", -1)
        mixed_backs.append((mine, give, ahead))
        return (other, mine)

    proj_parts = []

    def conv_back(s, after):
        mine, give, ahead = mixed_backs[s]
        d_proj, keep, pass_on, sums = conv_backward(
            s, seqs, scalars, mine, give, projs[s], convs[s], conv_taps, ahead, state["proj"], after
        )
        state["proj"] = (d_proj,)
        state["conv"] = state["conv"] + sums[:taps]
        proj_parts.append((keep, swap_cores(pass_on)))
        return (keep,)

    in_parts = []

    def in_part(k, keep, got):
        return dot(keep[k], in_flat, 1, 1) + dot(got[k], in_flat_other, 1, 1)

    def in_send(s, after):
        keep, got = proj_parts[s]
        got = tie(got, after)
        sent = [in_part(k, keep, got).astype(LOW) for k in range(1, chips)]
        in_parts.append([shift_chips(p, k + 1) for k, p in enumerate(sent)])
        return tuple(sent)

    outs_grads = []

    def finish(s, after):
        keep, got = proj_parts[s]
        d_in = in_part(0, keep, got)
        for piece in tie(in_parts[s], after):
            d_in = d_in + piece.astype(FULL)
        rows = owns[s].astype(FULL)
        d_norm, gain_term = norm_back(rows, norm_scale(rows), gain_in, d_in)
        state["in"] = state["in"] + gain_term
        outs_grads.append((d_resids[s] + d_norm).astype(LOW))
        return (outs_grads[-1],)

    def out_send(after):
        keep, give = down_product(seqs, scalars, state["ffn"][:2], downs, after)
        state["out"] = (keep, [shift_chips(give[k - 1], k) for k in range(1, chips)])
        return (give,)

    def out_finish(after):
        keep, pieces = state["out"]
        block = jnp.stack(resids, axis=0) + keep
        for piece in tie(pieces, after):
            block = block + piece.astype(FULL)
        state["out"] = block.astype(LOW)
        return (state["out"],)

    grads = {}

    def jobs(name):
        act_own, act_other, dgu_own, dgu_other, flip_n = state["ffn"]
        if name == "down":
            return (flips["grad"], act_own[None], act_other[None])
        return (flip_n, dgu_own, dgu_other)

    def grad_other(name, kinds, after):
        left, _, other = jobs(name)
        (part,) = weight_grad(scalars, left, other, 0, kinds, after=after)
        state[name] = swap_cores(part)
        return (part,)

    def begin(name, keep, give, bits):
        grads[name] = ([keep, trade(give, bits[0])], bits[1:])

    def grad_own(name, source, kind, bits, after):
        left, own, _ = jobs(source)
        keep, give = weight_grad(scalars, left, own, kind, 1, state[source], bits[0], after)
        begin(name, keep[0], give[0], bits)
        return (keep,)

    def in_grad(bits, after):
        keep, give = weight_grad(
            scalars, flips["in"][0], state["proj"][0], 0, 1, bit=bits[0], after=after
        )
        begin("in", keep[0], give[0], bits)
        return (give,)

    def step(name, after):
        terms, bits = grads[name]
        terms, give = scatter_step(terms[:-1] + [tie(terms[-1], after)], bits)
        grads[name] = (terms, bits[1:])
        return (give,)

    def end(name, after):
        terms, bits = grads[name]
        while len(bits) > 0:
            terms, _ = scatter_step(terms, bits)
            bits = bits[1:]
        value = total(terms[:-1] + [tie(terms[-1], after)])
        grads[name] = value.reshape(value.shape[1:])
        return (grads[name],)

    def out_other_grad(after):
        other_all = jnp.concatenate([o.reshape(chips * share, chans) for _, o in mixes], axis=0)
        rows = tie(jnp.concatenate(d_mix_rows, axis=0), after)
        part = dot(rows, other_all, 0, 0).astype(LOW)
        grads["out"] = swap_cores(part)
        return (part,)

    def out_grad(bits, after):
        mine_all = jnp.concatenate([m.reshape(chips * share, chans) for m, _ in mixes], axis=0)
        rows = tie(jnp.concatenate(d_mix_rows, axis=0), after)
        value = (dot(rows, mine_all, 0, 0) + grads["out"].astype(FULL)).astype(LOW)
        value = value.reshape((lax.axis_size("seq"), -1, chans))
        terms, give = scatter_step([value], bits)
        grads["out"] = (terms, bits[1:])
        return (give,)

    def small_begin(after):
        conv_full = lax.dynamic_update_slice_in_dim(
            jnp.zeros((taps, width), FULL), state["conv"], me * chans, 1
        )
        state["small"] = jnp.concatenate(
            [conv_full, state["in"][None], state["mid"][None]], axis=0
        )
        state["hops"] = [("ch", 1 << b) for b in range(count.bit_length() - 1)]
        state["hops"] += [("seq", 1 << b) for b in range(places)]
        return after

    def small_hop(after):
        axis, flip = state["hops"].pop(0)
        pairs = [(i, i ^ flip) for i in range(lax.axis_size(axis))]
        value = tie(state["small"], after)
        state["small"] = value + lax.ppermute(value, axis, pairs)
        return after

    def flat_weights(after):
        nonlocal in_flat, in_flat_other
        in_flat = jnp.concatenate([tie(in_three, after)[k] for k in range(3)], axis=1)
        in_flat_other = jnp.concatenate([tie(in_other, after)[k] for k in range(3)], axis=1)
        return (in_flat, in_flat_other)

    in_flat = in_flat_other = None
    last = ()
    last = forward(0, last)
    last = mix_send(0, last)
    last = forward(1, last)
    last = mix_send(1, last)
    last = forward(2, last)
    last = join(0, last)
    last = mix_send(2, last)
    last = back(last)
    last = join(1, last)
    last = feed(0, last)
    last = join(2, last)
    last = feed(1, last)
    last = middle(0, last)
    last = feed(2, last)
    last = middle(1, last)
    last = mix_back(0, last)
    last = grad_other("down", 1, last)
    last = conv_back(0, last)
    last = middle(2, last)
    last = mix_back(1, last)
    last = flat_weights(last)
    last = conv_back(1, last)
    last = mix_back(2, last)
    near_y = tuple(range(places))
    near_z = (1, 0) + tuple(range(2, places))
    last = grad_own("down", "down", 0, near_y, last)
    last = grad_other("gate", 2, last)
    last = in_send(0, last)
    last = conv_back(2, last)
    last = grad_own("up", "gate", 1, near_z, last)
    last = grad_own("gate", "gate", 0, near_y, last)
    last = finish(0, last)
    last = step("down", last)
    last = in_send(1, last)
    last = in_grad(near_y, last)
    last = finish(1, last)
    last = in_send(2, last)
    last = out_other_grad(last)
    last = out_send(last)
    last = finish(2, last)
    last = step("up", last)
    last = step("gate", last)
    last = out_grad(near_y, last)
    last = step("down", last)
    last = step("in", last)
    last = small_begin(last)
    last = small_hop(last)
    last = small_hop(last)
    last = step("gate", last)
    last = end("down", last)
    last = out_finish(last)
    last = small_hop(last)
    last = step("up", last)
    last = step("in", last)
    last = end("gate", last)
    last = step("out", last)
    last = small_hop(last)
    last = step("out", last)
    last = end("up", last)
    last = end("in", last)
    last = small_hop(last)
    last = end("out", last)
    while len(state["hops"]) > 0:
        last = small_hop(last)
    down_grad, gate_grad, up_grad = [grads[n][:, :hid] for n in ("down", "gate", "up")]
    small = state["small"]
    return (
        state["out"],
        jnp.stack(outs_grads, axis=0),
        small[taps],
        grads["in"].reshape(-1, 3, chans),
        small[:taps],
        grads["out"],
        small[taps + 1],
        jnp.stack([gate_grad, up_grad], axis=1),
        down_grad,
    )


def solution(mesh):
    placed = (
        P(None, "seq", None),
        P(),
        P(None, None, "ch"),
        P(None, "ch"),
        P(None, "ch"),
        P(),
        P(None, None, "ch"),
        P(None, "ch"),
        P(None, "seq", None),
    )
    return jax.shard_map(
        per_device,
        mesh=mesh,
        in_specs=placed,
        out_specs=(
            P(None, ("seq", "ch"), None),
            P(None, ("seq", "ch"), None),
            P(),
            P("seq", None, "ch"),
            P(),
            P("seq", "ch"),
            P(),
            P("seq", None, "ch"),
            P("seq", "ch"),
        ),
        check_vma=False,
    )
```

time: 1390 us -> 703 us (0.51)
  waiting for transfers between devices: 764 us -> 133 us
  matrix products: 387 us -> 66 us
  Pallas kernels: 0 us -> 315 us
  starting transfers between devices: 17.8 us -> 75.3 us
  blocking collectives: 40.6 us -> 0 us
  other arithmetic: 99 us -> 67.3 us
  local copies, waits for them, and re-layouts: 53.4 us -> 33.2 us
    reduce_scatter x15 -> x0, waiting for transfers between devices: 662 us -> none  [the longest x3 165 us: per_device(): lax.psum_scatter(mix_part, 'ch', scatter_dimension=0, tiled=True)]
    dot_general x36 -> x32, matrix products: 387 us -> 66 us  [dot(): lax.dot_general(a, b, (((a_dim,), (b_dim,)), ((), ())), preferred_element...]
    pallas_call x0 -> x17, Pallas kernels: none -> 315 us  [call(): pl.pallas_call(body, name=name, grid_spec=pltpu.PrefetchScalarGridSpec(nu...]
    ppermute x0 -> x52, waiting for transfers between devices: none -> 133 us  [the longest x15 56.5 us: trade(): return lax.ppermute(value, 'seq', [(i, i ^ 1 << bit) for i in range(count)])]
    all_gather x6 -> x0, waiting for transfers between devices: 87.4 us -> none  [the longest x3 57.1 us: per_device(): normed2 = lax.all_gather(normed_share, 'ch', axis=0, tiled=True)]
    ppermute x0 -> x52, starting transfers between devices: none -> 66.4 us  [the longest x15 40.7 us: trade(): return lax.ppermute(value, 'seq', [(i, i ^ 1 << bit) for i in range(count)])]
    psum x1 -> x0, blocking collectives: 40.6 us -> none  [per_device(): lax.psum((conv_full, gain_in_acc, gain_mid_acc), ('seq', 'ch'))]
    another operation x8 -> x2, other arithmetic: 19.7 us -> 1.84 us  [the longest x1 1.66 us: per_device(): jnp.stack(outs_grads, axis=0)]
  transfers between devices with their start and end apart: 28 -> 56, of which waited for: 22 -> 12; matrix products, arithmetic and copies ran while one was open for 26% -> 22% of each run, Pallas kernels for 0% -> 40%
where the time goes in v2:
time: 703 us; the launch traced here: 693 us
  Pallas kernels  315 us (45%)
  waiting for transfers between devices  133 us (19%)
  starting transfers between devices  75.3 us (11%)
  other arithmetic  67.3 us (10%)
  matrix products  66 us (9%)
  local copies, waits for them, and re-layouts  33.2 us (5%)
    pallas_call x17, Pallas kernels, call(): pl.pallas_call(body, name=name, grid_spec=pltpu.PrefetchScalarGridSpec(nu...  315 us
    dot_general x32, matrix products, dot(): lax.dot_general(a, b, (((a_dim,), (b_dim,)), ((), ())), preferred_element...  66 us
    ppermute x15, waiting for transfers between devices, trade(): return lax.ppermute(value, 'seq', [(i, i ^ 1 << bit) for i in range(count)])  56.5 us
    ppermute x5, waiting for transfers between devices, small_hop(): state['small'] = value + lax.ppermute(value, axis, pairs)  54.8 us
    ppermute x15, starting transfers between devices, trade(): return lax.ppermute(value, 'seq', [(i, i ^ 1 << bit) for i in range(count)])  40.7 us
    unnamed x231, local copies, waits for them, and re-layouts  18.9 us
    ppermute x16, starting transfers between devices, shift_chips(): lax.ppermute(value, 'ch', [(i, (i + CORES * steps) % count) for i in rang...  18.6 us
    convert_element_type x10, other arithmetic, scatter_step(): give = total([half(t, 1 - mine) for t in terms]).astype(LOW)  18.4 us
  transfers between devices with their start and end apart: 56, of which 12 were waited for; matrix products, arithmetic and copies ran while one was open for 22% of the time, Pallas kernels for 40%

profile of v2, /device:TPU:0, one launch (start us, length us, event | category | flops | bytes accessed | tf_op | source)
XLA Modules:
  0.0 692.8 jit_solution(14786048755845539311)
XLA Ops:
  2.2 4.9 collective-permute-start
  11.0 11.8 %conv_forward.3 = (bf16[1536,3072]{1,0:T(8,128)(2,1)}, bf16[3,1024,384]{2,1,0:T(8,128)(2,1)}, bf16[1024,384]{1,0:T(8,128)(2,1)}, bf16[2,256,384]{2,1,0:T(8,128)(...) custom-call(s32[5]{0:T(128)} %stack.56.refs_0_, bf16[3,1024,1536]{2,1,0:T(8,128)(2,1)} %refs_2_.6, ...), custom_call_target="tpu_custom_call" | custom-call | flops 3623878656 | bytes 22571520 | tf_op jit(solution)/shard_map/conv_forward/pallas_call | solution.py:73
  23.4 3.8 collective-permute-done.1
  29.3 12.0 %conv_forward.4 = (bf16[1536,3072]{1,0:T(8,128)(2,1)}, bf16[3,1024,384]{2,1,0:T(8,128)(2,1)}, bf16[1024,384]{1,0:T(8,128)(2,1)}, bf16[2,256,384]{2,1,0:T(8,128)(...) custom-call(s32[5]{0:T(128)} %stack.56.refs_0_, ...), custom_call_target="tpu_custom_call", output_to_operand_aliasing={{0}: (7, {})} | custom-call | flops 3623878656 | bytes 22571520 | tf_op jit(solution)/shard_map/conv_forward/pallas_call | solution.py:73
  41.7 2.6 collective-permute-start.3
  48.3 11.9 %conv_forward.5 = (bf16[1536,3072]{1,0:T(8,128)(2,1)}, bf16[3,1024,384]{2,1,0:T(8,128)(2,1)}, bf16[1024,384]{1,0:T(8,128)(2,1)}, bf16[2,256,384]{2,1,0:T(8,128)(...) custom-call(s32[5]{0:T(128)} %stack.56.refs_0_, ...), custom_call_target="tpu_custom_call", output_to_operand_aliasing={{0}: (7, {})} | custom-call | flops 3623878656 | bytes 22571520 | tf_op jit(solution)/shard_map/conv_forward/pallas_call | solution.py:73
  69.7 27.3 %act_back.1 = (bf16[1536,1536]{1,0:T(8,128)(2,1)}, bf16[1536,1792]{1,0:T(8,128)(2,1)}, bf16[1536,1792]{1,0:T(8,128)(2,1)}, bf16[3,256,1536]{2,1,0:T(8,128)(2,1)}) custom-call(s32[5]{0:T(128)} %stack.56.refs_0_, bf16[3,1024,1536]{2,1,0:T(8,128)(2,1)} %refs_6_.1, bf16[3,1024,1536]{2,1,0:T(8,128)(2,1)} %refs_6_.1, bf16[3,1024,1536]{2,1,0:T(8,128)(2,1)} %refs_6_.1, ...), custom_call_target="tpu_custom_call" | custom-call | flops 16307453952 | bytes 67239936 | tf_op jit(solution)/shard_map/act_back/pallas_call | solution.py:73
  97.0 2.4 multiply_reduce_fusion.7
  101.9 32.9 %ffn.3 = (bf16[1536,1792]{1,0:T(8,128)(2,1)}, bf16[1536,1792]{1,0:T(8,128)(2,1)}, bf16[2,1536,1792]{2,1,0:T(8,128)(2,1)}, bf16[2,1536,1792]{2,1,0:T(8,128)(2,1)}...) custom-call(s32[5]{0:T(128)} %stack.56.refs_0_, ...), custom_call_target="tpu_custom_call" | custom-call | flops 21743271936 | bytes 33816576 | tf_op jit(solution)/shard_map/ffn/pallas_call | solution.py:73
  140.5 33.1 %ffn.4 = (bf16[1536,1792]{1,0:T(8,128)(2,1)}, bf16[1536,1792]{1,0:T(8,128)(2,1)}, bf16[2,1536,1792]{2,1,0:T(8,128)(2,1)}, bf16[2,1536,1792]{2,1,0:T(8,128)(2,1)}...) custom-call(s32[5]{0:T(128)} %stack.56.refs_0_, ...), custom_call_target="tpu_custom_call", output_to_operand_aliasing={{0}: (7, {}), {1}: (8, {}), {2}: (9, {}), {3}: (10, {}), {4... | custom-call | flops 21743271936 | bytes 33816576 | tf_op jit(solution)/shard_map/ffn/pallas_call | solution.py:73
  175.2 2.8 fusion.125
  179.2 32.8 %ffn.5 = (bf16[1536,1792]{1,0:T(8,128)(2,1)}, bf16[1536,1792]{1,0:T(8,128)(2,1)}, bf16[2,1536,1792]{2,1,0:T(8,128)(2,1)}, bf16[2,1536,1792]{2,1,0:T(8,128)(2,1)}...) custom-call(s32[5]{0:T(128)} %stack.56.refs_0_, ...), custom_call_target="tpu_custom_call", output_to_operand_aliasing={{0}: (7, {}), {1}: (8, {}), {2}: (9, {}), {3}: (10, {}), {4... | custom-call | flops 21743271936 | bytes 33816576 | tf_op jit(solution)/shard_map/ffn/pallas_call | solution.py:73
  213.4 3.2 fusion.124
  223.4 2.7 convolution_convert_fusion.6
  228.2 14.6 %weight_grad.6.refs_7_ = bf16[1,1536,1792]{2,1,0:T(8,128)(2,1)} custom-call(s32[5]{0:T(128)} %stack.56.refs_0_, bf16[1536,1536]{1,0:T(8,128)(2,1)} %get-tuple-element.166.refs_1_, bf16[1,1536,1792]{2,1,0:T(8,128)(2,1)} %bitcast.364, bf16[512,384]{1,0:T(8,128)(2,1)} %convolution_convert_fusion.5.refs_3_, bf16[2,256,384]{2,1,0:T(8,128)(2,1)} %bitcast.336), custom_call_target="tpu_custom_call" | custom-call | flops 8455716864 | bytes 10223616 | tf_op jit(solution)/shard_map/weight_grad/pallas_call | solution.py:73
  243.5 7.9 %conv_backward.3 = (bf16[1,3072,1152]{2,1,0:T(8,128)(2,1)}, bf16[2,256,1152]{2,1,0:T(8,128)(2,1)}, bf16[2,256,1152]{2,1,0:T(8,128)(2,1)}, f32[8,384]{1,0:T(8,128)}) custom-call(s32[5]{0:T(128)} %stack.56.refs_0_, bf16[2,256,384]{2,1,0:T(8,128)(2,1)} %bitcast.337, bf16[2,256,384]{2,1,0:T(8,128)(2,1)} %bitcast.30.refs_2_, ...), custom_call_target="tpu_custom_call" | custom-call | flops 15728640 | bytes 3961344 | tf_op jit(solution)/shard_map/conv_backward/pallas_call | solution.py:73
  251.4 6.9 %collective-permute-done.17 = bf16[256,1536]{1,0:T(8,128)(2,1)S(1)} collective-permute-done((bf16[256,1536]{1,0:T(8,128)(2,1)}, bf16[256,1536]{1,0:T(8,128)(2,1)S(1)}, u32[]{:S(2)}, u32[]{:S(2)}) %collective-permute-start.17) | collective-permute-done | bytes 786464 | tf_op jit(solution)/shard_map/ppermute | solution.py:45
  259.6 3.2 fusion.123
  264.7 2.3 constant_dynamic-update-slice_fusion.2
  269.2 2.5 slice_bitcast_fusion.4
  275.3 3.7 pad_maximum_fusion
  280.3 7.8 %conv_backward.4 = (bf16[1,3072,1152]{2,1,0:T(8,128)(2,1)}, bf16[2,256,1152]{2,1,0:T(8,128)(2,1)}, bf16[2,256,1152]{2,1,0:T(8,128)(2,1)}, f32[8,384]{1,0:T(8,128)}) custom-call(s32[5]{0:T(128)} %stack.56.refs_0_, bf16[2,256,384]{2,1,0:T(8,128)(2,1)} %bitcast.346, bf16[2,256,384]{2,1,0:T(8,128)(2,1)} %bitcast.344, ...), custom_call_target="tpu_custom_call", output_to_operand_aliasing={{0}: (7, {})} | custom-call | flops 15728640 | bytes 3961344 | tf_op jit(solution)/shard_map/conv_backward/pallas_call | solution.py:73
  288.0 2.2 constant_dynamic-update-slice_fusion.11
  290.2 2.2 constant_dynamic-update-slice_fusion.10
  295.9 15.8 %weight_grad.7 = (bf16[1,4,192,1792]{3,2,1,0:T(8,128)(2,1)}, bf16[1,4,192,1792]{3,2,1,0:T(8,128)(2,1)}) custom-call(s32[5]{0:T(128)} %stack.56.refs_0_, bf16[1536,1536]{1,0:T(8,128)(2,1)} %get-tuple-element.166.refs_1_, bf16[1,1536,1792]{2,1,0:T(8,128)(2,1)} %bitcast.363, bf16[1,1536,1792]{2,1,0:T(8,128)(2,1)} %collective-permute-done.27.refs_3_, ...), custom_call_target="tpu_custom_call" | custom-call | flops 8455716864 | bytes 15728640 | tf_op jit(solution)/shard_map/weight_grad/pallas_call | solution.py:73
  311.6 23.4 %weight_grad.8 = bf16[2,1536,1792]{2,1,0:T(8,128)(2,1)} custom-call(s32[5]{0:T(128)} %stack.56.refs_0_, bf16[1536,1536]{1,0:T(8,128)(2,1)} %get-tuple-element.181.refs_1_, bf16[2,1536,1792]{2,1,0:T(8,128)(2,1)} %get-tuple-element.182.refs_2_, bf16[1,4,192,1792]{3,2,1,0:T(8,128)(2,1)} %get-tuple-element.183.refs_3_), custom_call_target="tpu_custom_call" | custom-call | flops 16911433728 | bytes 15728640 | tf_op jit(solution)/shard_map/weight_grad/pallas_call | solution.py:73
  338.7 9.9 %collective-permute-done.24 = bf16[512,384]{1,0:T(8,128)(2,1)S(1)} collective-permute-done((bf16[512,384]{1,0:T(8,128)(2,1)}, bf16[512,384]{1,0:T(8,128)(2,1)S(1)}, u32[]{:S(2)}, u32[]{:S(2)}) %collective-permute-start.24) | collective-permute-done | bytes 393248 | tf_op jit(solution)/shard_map/ppermute | solution.py:40
  352.7 2.9 fusion.78
  355.7 2.3 fusion.11.refs_8_
  358.6 7.9 %conv_backward.5 = (bf16[1,3072,1152]{2,1,0:T(8,128)(2,1)}, bf16[2,256,1152]{2,1,0:T(8,128)(2,1)}, bf16[2,256,1152]{2,1,0:T(8,128)(2,1)}, f32[8,384]{1,0:T(8,128)}) custom-call(s32[5]{0:T(128)} %stack.56.refs_0_, bf16[2,256,384]{2,1,0:T(8,128)(2,1)} %bitcast.340, bf16[2,256,384]{2,1,0:T(8,128)(2,1)} %bitcast.342, ...), custom_call_target="tpu_custom_call", output_to_operand_aliasing={{0}: (7, {})} | custom-call | flops 15728640 | bytes 3961344 | tf_op jit(solution)/shard_map/conv_backward/pallas_call | solution.py:73
  366.9 3.9 fusion.67
  370.8 3.4 fusion.68
  375.5 3.0 collective-permute-start.30
  378.6 2.5 fusion.66
  381.2 15.8 %weight_grad.9 = (bf16[1,4,192,1792]{3,2,1,0:T(8,128)(2,1)}, bf16[1,4,192,1792]{3,2,1,0:T(8,128)(2,1)}) custom-call(s32[5]{0:T(128)} %stack.56.refs_0_, bf16[1536,1536]{1,0:T(8,128)(2,1)} %get-tuple-element.181.refs_1_, bf16[2,1536,1792]{2,1,0:T(8,128)(2,1)} %get-tuple-element.189.refs_2_, bf16[2,1536,1792]{2,1,0:T(8,128)(2,1)} %collective-permute-done.32.refs_3_, ...), custom_call_target="tpu_custom_call" | custom-call | flops 8455716864 | bytes 26738688 | tf_op jit(solution)/shard_map/weight_grad/pallas_call | solution.py:73
  396.9 15.9 %weight_grad.10 = (bf16[1,4,192,1792]{3,2,1,0:T(8,128)(2,1)}, bf16[1,4,192,1792]{3,2,1,0:T(8,128)(2,1)}) custom-call(s32[5]{0:T(128)} %stack.56.refs_0_, bf16[1536,1536]{1,0:T(8,128)(2,1)} %get-tuple-element.181.refs_1_, bf16[2,1536,1792]{2,1,0:T(8,128)(2,1)} %get-tuple-element.189.refs_2_, bf16[2,1536,1792]{2,1,0:T(8,128)(2,1)} %collective-permute-done.32.refs_3_, ...), custom_call_target="tpu_custom_call" | custom-call | flops 8455716864 | bytes 26738688 | tf_op jit(solution)/shard_map/weight_grad/pallas_call | solution.py:73
  412.9 3.9 fusion.21
  418.2 20.3 %collective-permute-done.30 = bf16[4,192,1792]{2,1,0:T(8,128)(2,1)} collective-permute-done((bf16[4,192,1792]{2,1,0:T(8,128)(2,1)}, bf16[4,192,1792]{2,1,0:T(8,128)(2,1)}, u32[]{:S(2)}, u32[]{:S(2)}) %collective-permute-start.30) | collective-permute-done | bytes 2752544 | tf_op jit(solution)/shard_map/ppermute | solution.py:419
  438.6 2.9 fusion.38
  441.5 3.2 collective-permute-start.35
  444.7 2.3 fusion.72
  447.0 2.3 fusion.13.refs_3_
  451.0 19.3 %weight_grad.11 = (bf16[1,4,192,1152]{3,2,1,0:T(8,128)(2,1)}, bf16[1,4,192,1152]{3,2,1,0:T(8,128)(2,1)}) custom-call(s32[5]{0:T(128)} %stack.56.refs_0_, bf16[1536,3072]{1,0:T(8,128)(2,1)} %get-tuple-element.195.refs_1_, bf16[1,3072,1152]{2,1,0:T(8,128)(2,1)} %get-tuple-element.196.refs_2_, bf16[256,1536]{1,0:T(8,128)(2,1)} %fusion.13.refs_3_), custom_call_target="tpu_custom_call" | custom-call | flops 10871635968 | bytes 16515072 | tf_op jit(solution)/shard_map/weight_grad/pallas_call | solution.py:73
  471.4 3.5 fusion.29
  477.9 2.3 fusion.12
  481.5 3.7 convolution_convert_fusion.refs_5_
  485.2 24.8 %down_product.1 = (f32[3,256,1536]{2,1,0:T(8,128)}, bf16[1,3,256,1536]{3,2,1,0:T(8,128)(2,1)}) custom-call(s32[5]{0:T(128)} %stack.56.refs_0_, bf16[1536,1792]{1,0:T(8,128)(2,1)} %get-tuple-element.157.refs_1_, bf16[1536,1792]{1,0:T(8,128)(2,1)} %get-tuple-element.158.refs_2_, bf16[1728,1536]{1,0:T(8,128)(2,1)} %bitcast.311, ...), custom_call_target="tpu_custom_call" | custom-call | flops 16307453952 | bytes 21626880 | tf_op jit(solution)/shard_map/down_product/pallas_call | solution.py:73
  510.2 3.3 fusion.37
  515.5 18.1 %collective-permute-done.37 = bf16[4,192,1792]{2,1,0:T(8,128)(2,1)} collective-permute-done((bf16[4,192,1792]{2,1,0:T(8,128)(2,1)}, bf16[4,192,1792]{2,1,0:T(8,128)(2,1)}, u32[]{:S(2)}, u32[]{:S(2)}) %collective-permute-start.37) | collective-permute-done | bytes 2752544 | tf_op jit(solution)/shard_map/ppermute | solution.py:419
  534.4 2.9 fusion.39
  537.3 2.9 fusion.40
  542.0 5.0 add_convert_fusion.3
  547.2 2.9 fusion.47
  550.0 2.6 collective-permute-start.40
  552.6 2.3 fusion.63
  561.3 25.5 %collective-permute-done.44 = f32[5,1536]{1,0:T(8,128)S(1)} collective-permute-done((f32[5,1536]{1,0:T(8,128)S(1)}, f32[5,1536]{1,0:T(8,128)S(1)}, u32[]{:S(2)}, u32[]{:S(2)}) %collective-permute-start.44) | collective-permute-done | bytes 30752 | tf_op jit(solution)/shard_map/ppermute | solution.py:769
  590.9 2.7 collective-permute-start.47
  593.6 3.1 fusion.49
  596.7 6.1 fusion.1
  604.9 18.0 %collective-permute-done.48 = bf16[2,192,1152]{2,1,0:T(8,128)(2,1)S(1)} collective-permute-done((bf16[2,192,1152]{2,1,0:T(8,128)(2,1)}, bf16[2,192,1152]{2,1,0:T(8,128)(2,1)S(1)}, u32[]{:S(2)}, u32[]{:S(2)}) %collective-permute-start.48) | collective-permute-done | bytes 884768 | tf_op jit(solution)/shard_map/ppermute | solution.py:419
  628.8 19.6 %collective-permute-start.53 = (bf16[2,192,384]{2,1,0:T(8,128)(2,1)S(1)}, bf16[2,192,384]{2,1,0:T(8,128)(2,1)S(1)}, u32[]{:S(2)}, u32[]{:S(2)}) collective-permute-start(bf16[2,192,384]{2,1,0:T(8,128)(2,1)S(1)} %fusion.90), channel_id=1, source_target_pairs={{0,8},{4,12},{8,0},{12,4},{16,24},{20,28},{24,16},{28,20},{1,9},{5... | collective-permute-start | bytes 884744 | tf_op jit(solution)/shard_map/ppermute | solution.py:419
  648.6 25.9 %collective-permute-done.50 = f32[5,1536]{1,0:T(8,128)S(1)} collective-permute-done((f32[5,1536]{1,0:T(8,128)S(1)}, f32[5,1536]{1,0:T(8,128)S(1)}, u32[]{:S(2)}, u32[]{:S(2)}) %collective-permute-start.50) | collective-permute-done | bytes 30752 | tf_op jit(solution)/shard_map/ppermute | solution.py:769
  681.5 2.5 reshape_reshape.8
  684.1 3.7 copy.79
  (405 shorter events, 110.5 us)
Async XLA Ops:
  0.6 101.3 %collective-permute-start.10 = (bf16[2,1728,1536]{2,1,0:T(8,128)(2,1)}, bf16[2,1728,1536]{2,1,0:T(8,128)(2,1)}, u32[]{:S(2)}, u32[]{:S(2)}) collective-permute-start(bf16[2,1728,1536]{2,1,0:T(8,128)(2,1)} %bitcast.355), channel_id=1, source_target_pairs={{0,1},{1,0},{2,3},{3,2},{4,5},{5,4},{6,7},{7,6},{8,9},{9,8},{10,11... | collective-permute-start | bytes 31850504 | tf_op jit(solution)/shard_map/ppermute | solution.py:40
  1.2 26.0 %collective-permute-start.2 = (bf16[1536,384]{1,0:T(8,128)(2,1)}, bf16[1536,384]{1,0:T(8,128)(2,1)S(1)}, u32[]{:S(2)}, u32[]{:S(2)}) collective-permute-start(bf16[1536,384]{1,0:T(8,128)(2,1)} %param.13), channel_id=1, source_target_pairs={{0,1},{1,0},{2,3},{3,2},{4,5},{5,4},{6,7},{7,6},{8,9},{9,8},{10,11... | collective-permute-start | bytes 3538952 | tf_op jit(solution)/shard_map/ppermute | solution.py:40
  2.2 8.2 %collective-permute-start = (bf16[3,16,1536]{2,1,0:T(8,128)(2,1)S(1)}, bf16[3,16,1536]{2,1,0:T(8,128)(2,1)S(1)}, u32[]{:S(2)}, u32[]{:S(2)}) collective-permute-start(bf16[3,16,1536]{2,1,0:T(8,128)(2,1)S(1)} %slice.162), channel_id=1, source_target_pairs={{0,4},{4,8},{8,12},{12,16},{16,20},{20,24},{24,28},{1,5},{5,9},{9,... | collective-permute-start | bytes 442376 | tf_op jit(solution)/shard_map/ppermute | solution.py:51
  7.0 62.6 %collective-permute-start.6 = (bf16[1728,1536]{1,0:T(8,128)(2,1)}, bf16[1728,1536]{1,0:T(8,128)(2,1)}, u32[]{:S(2)}, u32[]{:S(2)}) collective-permute-start(bf16[1728,1536]{1,0:T(8,128)(2,1)} %bitcast.309), channel_id=1, source_target_pairs={{0,1},{1,0},{2,3},{3,2},{4,5},{5,4},{6,7},{7,6},{8,9},{9,8},{10,11... | collective-permute-start | bytes 15925256 | tf_op jit(solution)/shard_map/ppermute | solution.py:40
  22.9 4.3 collective-permute-start.1
  27.2 41.8 %copy-start.3 = (bf16[1536,384]{1,0:T(8,128)(2,1)}, bf16[1536,384]{1,0:T(8,128)(2,1)S(1)}, u32[]{:S(2)}) copy-start(bf16[1536,384]{1,0:T(8,128)(2,1)S(1)} %collective-permute-done.2) | copy-start | bytes 3538948
  41.3 3.7 collective-permute-start.4
  41.7 21.0 %collective-permute-start.3 = (bf16[256,1536]{1,0:T(8,128)(2,1)S(1)}, bf16[256,1536]{1,0:T(8,128)(2,1)S(1)}, u32[]{:S(2)}, u32[]{:S(2)}) collective-permute-start(bf16[256,1536]{1,0:T(8,128)(2,1)S(1)} %copy-done.45), channel_id=1, source_target_pairs={{0,2},{1,3},{2,0},{3,1},{4,6},{5,7},{6,4},{7,5},{8,10},{9,11},{10,... | collective-permute-start | bytes 2359304 | tf_op jit(solution)/shard_map/ppermute | solution.py:45
  47.6 49.4 %collective-permute-start.5 = (bf16[256,1536]{1,0:T(8,128)(2,1)}, bf16[256,1536]{1,0:T(8,128)(2,1)}, u32[]{:S(2)}, u32[]{:S(2)}) collective-permute-start(bf16[256,1536]{1,0:T(8,128)(2,1)} %fusion.9.refs_8_), channel_id=1, source_target_pairs={{0,2},{1,3},{2,0},{3,1},{4,6},{5,7},{6,4},{7,5},{8,10},{9,11},{10,... | collective-permute-start | bytes 2359304 | tf_op jit(solution)/shard_map/ppermute | solution.py:45
  60.2 7.1 %collective-permute-start.7 = (bf16[2,256,384]{2,1,0:T(8,128)(2,1)}, bf16[2,256,384]{2,1,0:T(8,128)(2,1)S(1)}, u32[]{:S(2)}, u32[]{:S(2)}) collective-permute-start(bf16[2,256,384]{2,1,0:T(8,128)(2,1)} %get-tuple-element.135), channel_id=1, source_target_pairs={{0,1},{1,0},{2,3},{3,2},{4,5},{5,4},{6,7},{7,6},{8,9},{9,8},{10,11... | collective-permute-start | bytes 1179656 | tf_op jit(solution)/shard_map/ppermute | solution.py:40
  63.5 111.6 %copy-start.6 = (f32[256,1536]{1,0:T(8,128)}, f32[256,1536]{1,0:T(8,128)S(1)}, u32[]{:S(2)}) copy-start(f32[256,1536]{1,0:T(8,128)S(1)} %get-tuple-element.293) | copy-start | bytes 4718596
  65.2 36.7 %collective-permute-start.9 = (bf16[256,1536]{1,0:T(8,128)(2,1)}, bf16[256,1536]{1,0:T(8,128)(2,1)}, u32[]{:S(2)}, u32[]{:S(2)}) collective-permute-start(bf16[256,1536]{1,0:T(8,128)(2,1)} %multiply_convert_fusion.2.refs_1_), channel_id=1, source_target_pairs={{0,2},{1,3},{2,0},{3,1},{4,6},{5,7},{6,4},{7,5},{8,10},{9,11},{10,... | collective-permute-start | bytes 2359304 | tf_op jit(solution)/shard_map/ppermute | solution.py:45
  68.5 66.4 %collective-permute-start.8 = (bf16[256,1536]{1,0:T(8,128)(2,1)S(1)}, bf16[256,1536]{1,0:T(8,128)(2,1)}, u32[]{:S(2)}, u32[]{:S(2)}) collective-permute-start(bf16[256,1536]{1,0:T(8,128)(2,1)S(1)} %fusion.10.refs_9_), channel_id=1, source_target_pairs={{0,2},{1,3},{2,0},{3,1},{4,6},{5,7},{6,4},{7,5},{8,10},{9,11},{10,... | collective-permute-start | bytes 2359304 | tf_op jit(solution)/shard_map/ppermute | solution.py:45
  99.5 113.9 %copy-start.8 = (f32[256,1536]{1,0:T(8,128)}, f32[256,1536]{1,0:T(8,128)S(1)}, u32[]{:S(2)}) copy-start(f32[256,1536]{1,0:T(8,128)S(1)} %get-tuple-element.295) | copy-start | bytes 4718596
  100.1 34.7 %copy-start.88 = (f32[256]{0:T(256)}, f32[256]{0:T(256)S(1)}, u32[]{:S(2)}) copy-start(f32[256]{0:T(256)S(1)} %get-tuple-element.289) | copy-start | bytes 3076
  100.3 40.2 %collective-permute-start.12 = (bf16[256,1536]{1,0:T(8,128)(2,1)S(1)}, bf16[256,1536]{1,0:T(8,128)(2,1)}, u32[]{:S(2)}, u32[]{:S(2)}) collective-permute-start(bf16[256,1536]{1,0:T(8,128)(2,1)S(1)} %multiply_convert_fusion.1.refs_7_.refs_1_), channel_id=1, source_target_pairs={{0,2},{1,3},{2,0},{3,1},{4,6},{5,7},{6,4},{7,5},{8,10},{9,11},{10,... | collective-permute-start | bytes 2359304 | tf_op jit(solution)/shard_map/ppermute | solution.py:45
  134.9 39.6 %collective-permute-start.13 = (bf16[256,1536]{1,0:T(8,128)(2,1)}, bf16[256,1536]{1,0:T(8,128)(2,1)S(1)}, u32[]{:S(2)}, u32[]{:S(2)}) collective-permute-start(bf16[256,1536]{1,0:T(8,128)(2,1)} %bitcast.362), channel_id=1, source_target_pairs={{0,2},{1,3},{2,0},{3,1},{4,6},{5,7},{6,4},{7,5},{8,10},{9,11},{10,... | collective-permute-start | bytes 2359304 | tf_op jit(solution)/shard_map/ppermute | solution.py:45
  138.4 35.2 %copy-start.86 = (f32[256]{0:T(256)}, f32[256]{0:T(256)S(1)}, u32[]{:S(2)}) copy-start(f32[256]{0:T(256)S(1)} %get-tuple-element.287) | copy-start | bytes 3076
  139.2 40.0 %collective-permute-start.11 = (bf16[256,1536]{1,0:T(8,128)(2,1)S(1)}, bf16[256,1536]{1,0:T(8,128)(2,1)}, u32[]{:S(2)}, u32[]{:S(2)}) collective-permute-start(bf16[256,1536]{1,0:T(8,128)(2,1)S(1)} %multiply_convert_fusion.refs_12_.refs_1_), channel_id=1, source_target_pairs={{0,2},{1,3},{2,0},{3,1},{4,6},{5,7},{6,4},{7,5},{8,10},{9,11},{10,... | collective-permute-start | bytes 2359304 | tf_op jit(solution)/shard_map/ppermute | solution.py:45
  140.5 34.0 %copy-start.91 = (f32[256]{0:T(256)S(1)}, f32[256]{0:T(256)}, u32[]{:S(2)}) copy-start(f32[256]{0:T(256)} %copy-done.90) | copy-start | bytes 3076
  173.6 38.5 %collective-permute-start.15 = (bf16[256,1536]{1,0:T(8,128)(2,1)}, bf16[256,1536]{1,0:T(8,128)(2,1)S(1)}, u32[]{:S(2)}, u32[]{:S(2)}) collective-permute-start(bf16[256,1536]{1,0:T(8,128)(2,1)} %bitcast.361), channel_id=1, source_target_pairs={{0,2},{1,3},{2,0},{3,1},{4,6},{5,7},{6,4},{7,5},{8,10},{9,11},{10,... | collective-permute-start | bytes 2359304 | tf_op jit(solution)/shard_map/ppermute | solution.py:45
  178.0 38.5 %collective-permute-start.14 = (bf16[256,1536]{1,0:T(8,128)(2,1)S(1)}, bf16[256,1536]{1,0:T(8,128)(2,1)S(1)}, u32[]{:S(2)}, u32[]{:S(2)}) collective-permute-start(bf16[256,1536]{1,0:T(8,128)(2,1)S(1)} %get-tuple-element.162.refs_12_), channel_id=1, source_target_pairs={{0,2},{1,3},{2,0},{3,1},{4,6},{5,7},{6,4},{7,5},{8,10},{9,11},{10,... | collective-permute-start | bytes 2359304 | tf_op jit(solution)/shard_map/ppermute | solution.py:45
  220.2 5.9 collective-permute-start.18
  221.3 47.9 %collective-permute-start.23 = (bf16[3,1536,384]{2,1,0:T(8,128)(2,1)S(1)}, bf16[3,1536,384]{2,1,0:T(8,128)(2,1)}, u32[]{:S(2)}, u32[]{:S(2)}) collective-permute-start(bf16[3,1536,384]{2,1,0:T(8,128)(2,1)S(1)} %bitcast.304), channel_id=1, source_target_pairs={{0,1},{1,0},{2,3},{3,2},{4,5},{5,4},{6,7},{7,6},{8,9},{9,8},{10,11... | collective-permute-start | bytes 10616840 | tf_op jit(solution)/shard_map/ppermute | solution.py:40
  221.3 42.3 %collective-permute-start.16 = (bf16[256,1536]{1,0:T(8,128)(2,1)}, bf16[256,1536]{1,0:T(8,128)(2,1)}, u32[]{:S(2)}, u32[]{:S(2)}) collective-permute-start(bf16[256,1536]{1,0:T(8,128)(2,1)} %get-tuple-element.169), channel_id=1, source_target_pairs={{0,2},{1,3},{2,0},{3,1},{4,6},{5,7},{6,4},{7,5},{8,10},{9,11},{10,... | collective-permute-start | bytes 2359304 | tf_op jit(solution)/shard_map/ppermute | solution.py:45
  222.2 36.1 %collective-permute-start.17 = (bf16[256,1536]{1,0:T(8,128)(2,1)}, bf16[256,1536]{1,0:T(8,128)(2,1)S(1)}, u32[]{:S(2)}, u32[]{:S(2)}) collective-permute-start(bf16[256,1536]{1,0:T(8,128)(2,1)} %bitcast.360), channel_id=1, source_target_pairs={{0,2},{1,3},{2,0},{3,1},{4,6},{5,7},{6,4},{7,5},{8,10},{9,11},{10,... | collective-permute-start | bytes 2359304 | tf_op jit(solution)/shard_map/ppermute | solution.py:45
  226.9 16.0 %collective-permute-start.19 = (f32[16,384]{1,0:T(8,128)S(1)}, f32[16,384]{1,0:T(8,128)S(1)}, u32[]{:S(2)}, u32[]{:S(2)}) collective-permute-start(f32[16,384]{1,0:T(8,128)S(1)} %multiply_bitcast_fusion.2), channel_id=1, source_target_pairs={{4,0},{8,4},{12,8},{16,12},{20,16},{24,20},{28,24},{5,1},{9,5},{13... | collective-permute-start | bytes 73736 | tf_op jit(solution)/shard_map/ppermute | solution.py:51
  242.8 53.1 %collective-permute-start.27 = (bf16[1,1536,1792]{2,1,0:T(8,128)(2,1)}, bf16[1,1536,1792]{2,1,0:T(8,128)(2,1)}, u32[]{:S(2)}, u32[]{:S(2)}) collective-permute-start(bf16[1,1536,1792]{2,1,0:T(8,128)(2,1)} %weight_grad.6.refs_7_), channel_id=1, source_target_pairs={{0,1},{1,0},{2,3},{3,2},{4,5},{5,4},{6,7},{7,6},{8,9},{9,8},{10,11... | collective-permute-start | bytes 16515080 | tf_op jit(solution)/shard_map/ppermute | solution.py:40
  262.8 25.3 %collective-permute-start.20 = (bf16[256,1536]{1,0:T(8,128)(2,1)}, bf16[256,1536]{1,0:T(8,128)(2,1)}, u32[]{:S(2)}, u32[]{:S(2)}) collective-permute-start(bf16[256,1536]{1,0:T(8,128)(2,1)} %get-tuple-element.176), channel_id=1, source_target_pairs={{0,2},{1,3},{2,0},{3,1},{4,6},{5,7},{6,4},{7,5},{8,10},{9,11},{10,... | collective-permute-start | bytes 2359304 | tf_op jit(solution)/shard_map/ppermute | solution.py:45
  267.9 4.2 collective-permute-start.21
  274.0 5.7 collective-permute-start.22
  335.1 46.1 %collective-permute-start.32 = (bf16[2,1536,1792]{2,1,0:T(8,128)(2,1)}, bf16[2,1536,1792]{2,1,0:T(8,128)(2,1)}, u32[]{:S(2)}, u32[]{:S(2)}) collective-permute-start(bf16[2,1536,1792]{2,1,0:T(8,128)(2,1)} %weight_grad.8), channel_id=1, source_target_pairs={{0,1},{1,0},{2,3},{3,2},{4,5},{5,4},{6,7},{7,6},{8,9},{9,8},{10,11... | collective-permute-start | bytes 33030152 | tf_op jit(solution)/shard_map/ppermute | solution.py:40
  335.4 16.3 %collective-permute-start.26 = (bf16[2,256,1152]{2,1,0:T(8,128)(2,1)}, bf16[2,256,1152]{2,1,0:T(8,128)(2,1)S(1)}, u32[]{:S(2)}, u32[]{:S(2)}) collective-permute-start(bf16[2,256,1152]{2,1,0:T(8,128)(2,1)} %get-tuple-element.180), channel_id=1, source_target_pairs={{0,1},{1,0},{2,3},{3,2},{4,5},{5,4},{6,7},{7,6},{8,9},{9,8},{10,11... | collective-permute-start | bytes 3538952 | tf_op jit(solution)/shard_map/ppermute | solution.py:40
  336.7 11.9 %collective-permute-start.24 = (bf16[512,384]{1,0:T(8,128)(2,1)}, bf16[512,384]{1,0:T(8,128)(2,1)S(1)}, u32[]{:S(2)}, u32[]{:S(2)}) collective-permute-start(bf16[512,384]{1,0:T(8,128)(2,1)} %convolution_convert_fusion.1.refs_4_), channel_id=1, source_target_pairs={{0,1},{1,0},{2,3},{3,2},{4,5},{5,4},{6,7},{7,6},{8,9},{9,8},{10,11... | collective-permute-start | bytes 1179656 | tf_op jit(solution)/shard_map/ppermute | solution.py:40
  338.3 171.9 %copy-start.93 = (f32[256]{0:T(256)}, f32[256]{0:T(256)S(1)}, u32[]{:S(2)}) copy-start(f32[256]{0:T(256)S(1)} %get-tuple-element.281) | copy-start | bytes 3076
  338.3 32.5 %collective-permute-start.29 = (bf16[2,256,1152]{2,1,0:T(8,128)(2,1)}, bf16[2,256,1152]{2,1,0:T(8,128)(2,1)}, u32[]{:S(2)}, u32[]{:S(2)}) collective-permute-start(bf16[2,256,1152]{2,1,0:T(8,128)(2,1)} %get-tuple-element.187), channel_id=1, source_target_pairs={{0,1},{1,0},{2,3},{3,2},{4,5},{5,4},{6,7},{7,6},{8,9},{9,8},{10,11... | collective-permute-start | bytes 3538952 | tf_op jit(solution)/shard_map/ppermute | solution.py:40
  350.2 7.8 %collective-permute-start.25 = (f32[16,384]{1,0:T(8,128)S(1)}, f32[16,384]{1,0:T(8,128)S(1)}, u32[]{:S(2)}, u32[]{:S(2)}) collective-permute-start(f32[16,384]{1,0:T(8,128)S(1)} %multiply_bitcast_fusion), channel_id=1, source_target_pairs={{4,0},{8,4},{12,8},{16,12},{20,16},{24,20},{28,24},{5,1},{9,5},{13... | collective-permute-start | bytes 73736 | tf_op jit(solution)/shard_map/ppermute | solution.py:51
  366.4 12.2 %collective-permute-start.28 = (bf16[2,256,1152]{2,1,0:T(8,128)(2,1)}, bf16[2,256,1152]{2,1,0:T(8,128)(2,1)S(1)}, u32[]{:S(2)}, u32[]{:S(2)}) collective-permute-start(bf16[2,256,1152]{2,1,0:T(8,128)(2,1)} %get-tuple-element.186), channel_id=1, source_target_pairs={{0,1},{1,0},{2,3},{3,2},{4,5},{5,4},{6,7},{7,6},{8,9},{9,8},{10,11... | collective-permute-start | bytes 3538952 | tf_op jit(solution)/shard_map/ppermute | solution.py:40
  374.2 38.6 %collective-permute-start.31 = (bf16[256,1536]{1,0:T(8,128)(2,1)}, bf16[256,1536]{1,0:T(8,128)(2,1)}, u32[]{:S(2)}, u32[]{:S(2)}) collective-permute-start(bf16[256,1536]{1,0:T(8,128)(2,1)} %fusion.11.refs_8_), channel_id=1, source_target_pairs={{0,2},{1,3},{2,0},{3,1},{4,6},{5,7},{6,4},{7,5},{8,10},{9,11},{10,... | collective-permute-start | bytes 2359304 | tf_op jit(solution)/shard_map/ppermute | solution.py:45
  375.5 63.0 %collective-permute-start.30 = (bf16[4,192,1792]{2,1,0:T(8,128)(2,1)}, bf16[4,192,1792]{2,1,0:T(8,128)(2,1)}, u32[]{:S(2)}, u32[]{:S(2)}) collective-permute-start(bf16[4,192,1792]{2,1,0:T(8,128)(2,1)} %bitcast.53), channel_id=1, source_target_pairs={{0,4},{4,0},{8,12},{12,8},{16,20},{20,16},{24,28},{28,24},{1,5},{5... | collective-permute-start | bytes 8257544 | tf_op jit(solution)/shard_map/ppermute | solution.py:419
  441.5 105.7 %collective-permute-start.35 = (bf16[2,192,1792]{2,1,0:T(8,128)(2,1)}, bf16[2,192,1792]{2,1,0:T(8,128)(2,1)}, u32[]{:S(2)}, u32[]{:S(2)}) collective-permute-start(bf16[2,192,1792]{2,1,0:T(8,128)(2,1)} %fusion.38), channel_id=1, source_target_pairs={{0,8},{4,12},{8,0},{12,4},{16,24},{20,28},{24,16},{28,20},{1,9},{5... | collective-permute-start | bytes 4128776 | tf_op jit(solution)/shard_map/ppermute | solution.py:419
  449.2 22.2 %collective-permute-start.33 = (bf16[256,1536]{1,0:T(8,128)(2,1)}, bf16[256,1536]{1,0:T(8,128)(2,1)}, u32[]{:S(2)}, u32[]{:S(2)}) collective-permute-start(bf16[256,1536]{1,0:T(8,128)(2,1)} %fusion.13.refs_3_), channel_id=1, source_target_pairs={{0,2},{1,3},{2,0},{3,1},{4,6},{5,7},{6,4},{7,5},{8,10},{9,11},{10,... | collective-permute-start | bytes 2359304 | tf_op jit(solution)/shard_map/ppermute | solution.py:45
  450.0 83.7 %collective-permute-start.37 = (bf16[4,192,1792]{2,1,0:T(8,128)(2,1)}, bf16[4,192,1792]{2,1,0:T(8,128)(2,1)}, u32[]{:S(2)}, u32[]{:S(2)}) collective-permute-start(bf16[4,192,1792]{2,1,0:T(8,128)(2,1)} %bitcast.70), channel_id=1, source_target_pairs={{0,8},{4,12},{8,0},{12,4},{16,24},{20,28},{24,16},{28,20},{1,9},{5... | collective-permute-start | bytes 8257544 | tf_op jit(solution)/shard_map/ppermute | solution.py:419
  450.1 87.2 %collective-permute-start.36 = (bf16[4,192,1792]{2,1,0:T(8,128)(2,1)}, bf16[4,192,1792]{2,1,0:T(8,128)(2,1)}, u32[]{:S(2)}, u32[]{:S(2)}) collective-permute-start(bf16[4,192,1792]{2,1,0:T(8,128)(2,1)} %bitcast.68), channel_id=1, source_target_pairs={{0,4},{4,0},{8,12},{12,8},{16,20},{20,16},{24,28},{28,24},{1,5},{5... | collective-permute-start | bytes 8257544 | tf_op jit(solution)/shard_map/ppermute | solution.py:419
  470.3 82.3 %collective-permute-start.42 = (bf16[4,192,1152]{2,1,0:T(8,128)(2,1)}, bf16[4,192,1152]{2,1,0:T(8,128)(2,1)}, u32[]{:S(2)}, u32[]{:S(2)}) collective-permute-start(bf16[4,192,1152]{2,1,0:T(8,128)(2,1)} %bitcast.359), channel_id=1, source_target_pairs={{0,4},{4,0},{8,12},{12,8},{16,20},{20,16},{24,28},{28,24},{1,5},{5... | collective-permute-start | bytes 5308424 | tf_op jit(solution)/shard_map/ppermute | solution.py:419
  480.2 29.9 %collective-permute-start.38 = (bf16[256,1536]{1,0:T(8,128)(2,1)}, bf16[256,1536]{1,0:T(8,128)(2,1)}, u32[]{:S(2)}, u32[]{:S(2)}) collective-permute-start(bf16[256,1536]{1,0:T(8,128)(2,1)} %fusion.12), channel_id=1, source_target_pairs={{0,2},{1,3},{2,0},{3,1},{4,6},{5,7},{6,4},{7,5},{8,10},{9,11},{10,... | collective-permute-start | bytes 2359304 | tf_op jit(solution)/shard_map/ppermute | solution.py:45
  510.1 31.9 %collective-permute-start.39 = (bf16[1536,384]{1,0:T(8,128)(2,1)}, bf16[1536,384]{1,0:T(8,128)(2,1)S(1)}, u32[]{:S(2)}, u32[]{:S(2)}) collective-permute-start(bf16[1536,384]{1,0:T(8,128)(2,1)} %convolution_convert_fusion.refs_5_), channel_id=1, source_target_pairs={{0,1},{1,0},{2,3},{3,2},{4,5},{5,4},{6,7},{7,6},{8,9},{9,8},{10,11... | collective-permute-start | bytes 3538952 | tf_op jit(solution)/shard_map/ppermute | solution.py:40
  533.6 63.1 %collective-permute-start.34 = (bf16[3,256,1536]{2,1,0:T(8,128)(2,1)}, bf16[3,256,1536]{2,1,0:T(8,128)(2,1)}, u32[]{:S(2)}, u32[]{:S(2)}) collective-permute-start(bf16[3,256,1536]{2,1,0:T(8,128)(2,1)} %bitcast.63), channel_id=1, source_target_pairs={{0,2},{1,3},{2,0},{3,1},{4,6},{5,7},{6,4},{7,5},{8,10},{9,11},{10,... | collective-permute-start | bytes 7077896 | tf_op jit(solution)/shard_map/ppermute | solution.py:45
  540.2 48.0 %collective-permute-start.41 = (bf16[2,192,1792]{2,1,0:T(8,128)(2,1)}, bf16[2,192,1792]{2,1,0:T(8,128)(2,1)}, u32[]{:S(2)}, u32[]{:S(2)}) collective-permute-start(bf16[2,192,1792]{2,1,0:T(8,128)(2,1)} %fusion.40), channel_id=1, source_target_pairs={{0,8},{4,12},{8,0},{12,4},{16,24},{20,28},{24,16},{28,20},{1,9},{5... | collective-permute-start | bytes 4128776 | tf_op jit(solution)/shard_map/ppermute | solution.py:419
  547.1 127.4 %copy-start.51 = (bf16[4,1,1,192,384]{4,3,1,0,2:T(8,128)(2,1)}, bf16[4,1,1,192,384]{4,3,1,0,2:T(8,128)(2,1)S(1)}, u32[]{:S(2)}) copy-start(bf16[4,1,1,192,384]{4,3,1,0,2:T(8,128)(2,1)S(1)} %get-tuple-element.266) | copy-start | bytes 1769476
  550.0 40.9 %collective-permute-start.40 = (bf16[1,192,1792]{2,1,0:T(8,128)(2,1)}, bf16[1,192,1792]{2,1,0:T(8,128)(2,1)}, u32[]{:S(2)}, u32[]{:S(2)}) collective-permute-start(bf16[1,192,1792]{2,1,0:T(8,128)(2,1)} %fusion.47), channel_id=1, source_target_pairs={{0,16},{4,20},{8,24},{12,28},{16,0},{20,4},{24,8},{28,12},{1,17},{... | collective-permute-start | bytes 2064392 | tf_op jit(solution)/shard_map/ppermute | solution.py:419
  554.9 1.6 collective-permute-start.43
  557.3 29.4 %collective-permute-start.44 = (f32[5,1536]{1,0:T(8,128)S(1)}, f32[5,1536]{1,0:T(8,128)S(1)}, u32[]{:S(2)}, u32[]{:S(2)}) collective-permute-start(f32[5,1536]{1,0:T(8,128)S(1)} %add.748), channel_id=1, source_target_pairs={{0,2},{1,3},{2,0},{3,1},{4,6},{5,7},{6,4},{7,5},{8,10},{9,11},{10,... | collective-permute-start | bytes 92168 | tf_op jit(solution)/shard_map/ppermute | solution.py:769
  560.4 42.4 %collective-permute-start.49 = (bf16[2,192,1792]{2,1,0:T(8,128)(2,1)S(1)}, bf16[2,192,1792]{2,1,0:T(8,128)(2,1)S(1)}, u32[]{:S(2)}, u32[]{:S(2)}) collective-permute-start(bf16[2,192,1792]{2,1,0:T(8,128)(2,1)S(1)} %copy-done.54), channel_id=1, source_target_pairs={{0,4},{4,0},{8,12},{12,8},{16,20},{20,16},{24,28},{28,24},{1,5},{5... | collective-permute-start | bytes 4128776 | tf_op jit(solution)/shard_map/ppermute | solution.py:419
  586.8 36.2 %collective-permute-start.48 = (bf16[2,192,1152]{2,1,0:T(8,128)(2,1)}, bf16[2,192,1152]{2,1,0:T(8,128)(2,1)S(1)}, u32[]{:S(2)}, u32[]{:S(2)}) collective-permute-start(bf16[2,192,1152]{2,1,0:T(8,128)(2,1)} %fusion.63), channel_id=1, source_target_pairs={{0,8},{4,12},{8,0},{12,4},{16,24},{20,28},{24,16},{28,20},{1,9},{5... | collective-permute-start | bytes 2654216 | tf_op jit(solution)/shard_map/ppermute | solution.py:419
  588.2 40.5 %collective-permute-start.46 = (bf16[4,192,384]{2,1,0:T(8,128)(2,1)S(1)}, bf16[4,192,384]{2,1,0:T(8,128)(2,1)S(1)}, u32[]{:S(2)}, u32[]{:S(2)}) collective-permute-start(bf16[4,192,384]{2,1,0:T(8,128)(2,1)S(1)} %get-tuple-element.267), channel_id=1, source_target_pairs={{0,4},{4,0},{8,12},{12,8},{16,20},{20,16},{24,28},{28,24},{1,5},{5... | collective-permute-start | bytes 1769480 | tf_op jit(solution)/shard_map/ppermute | solution.py:419
  590.9 36.1 %collective-permute-start.47 = (bf16[1,192,1792]{2,1,0:T(8,128)(2,1)S(1)}, bf16[1,192,1792]{2,1,0:T(8,128)(2,1)S(1)}, u32[]{:S(2)}, u32[]{:S(2)}) collective-permute-start(bf16[1,192,1792]{2,1,0:T(8,128)(2,1)S(1)} %fusion.46), channel_id=1, source_target_pairs={{0,16},{4,20},{8,24},{12,28},{16,0},{20,4},{24,8},{28,12},{1,17},{... | collective-permute-start | bytes 2064392 | tf_op jit(solution)/shard_map/ppermute | solution.py:419
  604.3 71.7 %collective-permute-start.52 = (bf16[1,192,1792]{2,1,0:T(8,128)(2,1)S(1)}, bf16[1,192,1792]{2,1,0:T(8,128)(2,1)S(1)}, u32[]{:S(2)}, u32[]{:S(2)}) collective-permute-start(bf16[1,192,1792]{2,1,0:T(8,128)(2,1)S(1)} %fusion.43), channel_id=1, source_target_pairs={{0,16},{4,20},{8,24},{12,28},{16,0},{20,4},{24,8},{28,12},{1,17},{... | collective-permute-start | bytes 2064392 | tf_op jit(solution)/shard_map/ppermute | solution.py:419
  622.9 4.1 collective-permute-start.45
  624.9 52.8 %collective-permute-start.51 = (bf16[1,192,1152]{2,1,0:T(8,128)(2,1)S(1)}, bf16[1,192,1152]{2,1,0:T(8,128)(2,1)S(1)}, u32[]{:S(2)}, u32[]{:S(2)}) collective-permute-start(bf16[1,192,1152]{2,1,0:T(8,128)(2,1)S(1)} %fusion.65), channel_id=1, source_target_pairs={{0,16},{4,20},{8,24},{12,28},{16,0},{20,4},{24,8},{28,12},{1,17},{... | collective-permute-start | bytes 1327112 | tf_op jit(solution)/shard_map/ppermute | solution.py:419
  628.8 45.7 %collective-permute-start.53 = (bf16[2,192,384]{2,1,0:T(8,128)(2,1)S(1)}, bf16[2,192,384]{2,1,0:T(8,128)(2,1)S(1)}, u32[]{:S(2)}, u32[]{:S(2)}) collective-permute-start(bf16[2,192,384]{2,1,0:T(8,128)(2,1)S(1)} %fusion.90), channel_id=1, source_target_pairs={{0,8},{4,12},{8,0},{12,4},{16,24},{20,28},{24,16},{28,20},{1,9},{5... | collective-permute-start | bytes 884744 | tf_op jit(solution)/shard_map/ppermute | solution.py:419
  648.4 26.1 %collective-permute-start.50 = (f32[5,1536]{1,0:T(8,128)S(1)}, f32[5,1536]{1,0:T(8,128)S(1)}, u32[]{:S(2)}, u32[]{:S(2)}) collective-permute-start(f32[5,1536]{1,0:T(8,128)S(1)} %add.750), channel_id=1, source_target_pairs={{0,8},{4,12},{8,0},{12,4},{16,24},{20,28},{24,16},{28,20},{1,9},{5... | collective-permute-start | bytes 92168 | tf_op jit(solution)/shard_map/ppermute | solution.py:769
  674.6 16.1 %collective-permute-start.55 = (bf16[1,192,384]{2,1,0:T(8,128)(2,1)S(1)}, bf16[1,192,384]{2,1,0:T(8,128)(2,1)}, u32[]{:S(2)}, u32[]{:S(2)}) collective-permute-start(bf16[1,192,384]{2,1,0:T(8,128)(2,1)S(1)} %fusion.93), channel_id=1, source_target_pairs={{0,16},{4,20},{8,24},{12,28},{16,0},{20,4},{24,8},{28,12},{1,17},{... | collective-permute-start | bytes 442376 | tf_op jit(solution)/shard_map/ppermute | solution.py:419
  679.8 8.9 %collective-permute-start.54 = (f32[5,1536]{1,0:T(8,128)S(1)}, f32[5,1536]{1,0:T(8,128)}, u32[]{:S(2)}, u32[]{:S(2)}) collective-permute-start(f32[5,1536]{1,0:T(8,128)S(1)} %add.763), channel_id=1, source_target_pairs={{0,16},{4,20},{8,24},{12,28},{16,0},{20,4},{24,8},{28,12},{1,17},{... | collective-permute-start | bytes 92168 | tf_op jit(solution)/shard_map/ppermute | solution.py:769
  (105 other events, 816.4 us)

commit v3 on v2

--- a/solution.py
+++ b/solution.py
@@ -14,6 +14,8 @@
 HALO = 16
 HIDDEN_TILE = 512
 LANES = 128
+COLUMN_TILE = 256
+HINT = 0.5 * 1.153e9
 ROOM = 56 << 20
 
 
@@ -62,14 +64,14 @@
 ANY = pl.BlockSpec(memory_space=pl.ANY)
 
 
-def call(kernel, name, grid, scalars, operands, outputs, scratch, carry=(), after=(), flops=0):
+def call(kernel, name, grid, scalars, operands, outputs, scratch, carry=(), after=(), micros=0):
     extra = len(carry) + len(after)
 
     def body(*refs):
         place = 1 + len(operands)
         return kernel(*refs[:place], *refs[place + extra :])
 
-    moved = sum(a.size * a.dtype.itemsize for a, _, _ in operands)
+    hint = int(micros * HINT)
     return pl.pallas_call(
         body,
         name=name,
@@ -85,7 +87,7 @@
         compiler_params=pltpu.CompilerParams(
             vmem_limit_bytes=ROOM, dimension_semantics=("arbitrary",) * len(grid)
         ),
-        cost_estimate=pl.CostEstimate(flops=flops, bytes_accessed=moved, transcendentals=0),
+        cost_estimate=pl.CostEstimate(flops=hint, bytes_accessed=1, transcendentals=0),
     )(scalars, *[a for a, _, _ in operands], *carry, *after)
 
 
@@ -101,7 +103,7 @@
 
     def kernel(
         at, rows_ref, halo_ref, tail_ref, gain_ref, w_ref, taps_ref,
-        flip_ref, proj_ref, conv_ref, mine_ref, theirs_ref, own_ref, flat
+        flip_ref, proj_ref, conv_ref, mine_ref, theirs_ref, own_ref, edge_ref, edge_proj, flat
     ):
         i = pl.program_id(0)
         if wide:
@@ -129,6 +131,12 @@
         proj_ref[1] = c_gate[HALO:].astype(LOW)
         proj_ref[2] = x_val[HALO:].astype(LOW)
         conv_ref[...] = conv.astype(LOW)
+
+        @pl.when(i == 0)
+        def _():
+            edge_ref[...] = normed[:HALO]
+            for k, value in enumerate((b_gate, c_gate, x_val)):
+                edge_proj[k] = value[:HALO].astype(LOW)
 
         @pl.when(i == CORES * at[0] + at[1])
         def _():
@@ -167,11 +175,13 @@
             ((chips, share, chans), LOW, (1, share, chans), away),
             ((chips, share, chans), LOW, (1, share, chans), away),
             ((share, width), LOW, (share, width), lambda i, at: (0, 0)),
+            ((HALO, width), LOW, (HALO, width), lambda i, at: (0, 0)),
+            ((kinds, HALO, chans), LOW, (kinds, HALO, chans), lambda i, at: (0, 0, 0)),
         ],
         [pltpu.VMEM((width, kinds * chans) if wide else (HALO, 128), LOW)],
         carry,
         after,
-        2 * length * width * kinds * chans,
+        12,
     )
 
 
@@ -190,7 +200,8 @@
 
     def kernel(at, *refs):
         grad_refs, refs = refs[: len(places)], refs[len(places) :]
-        down0, down1, flip, out0, out1, own, grad = refs
+        other_refs, refs = refs[: len(places)], refs[len(places) :]
+        down0, down1, flip, flip_other, out0, out1, own, grad = refs
         i = pl.program_id(0)
 
         @pl.when(i == 0)
@@ -201,6 +212,7 @@
                     own[s] = value
                 grad[n * share : (n + 1) * share] = value
                 flip[:, n * share : (n + 1) * share] = value.T
+                flip_other[:, n * share : (n + 1) * share] = other_refs[n][0].T
 
         def units(size):
             for down, out in ((down0, out0), (down1, out1)):
@@ -212,10 +224,12 @@
             pl.when(i < steps - 1)(lambda: units(tile))
             pl.when(i == steps - 1)(lambda: units(last))
 
-    def place(s, k):
-        return lambda i, at: (s, CORES * ((at[0] + k) % chips) + at[1], 0)
-
-    operands = [(cotangent, (1, share, width), place(s, k)) for s, k in places]
+    def place(s, k, far):
+        return lambda i, at: (s, CORES * ((at[0] + k) % chips) + (at[1] + far) % CORES, 0)
+
+    operands = [
+        (cotangent, (1, share, width), place(s, k, far)) for far in range(CORES) for s, k in places
+    ]
     operands += [(d, (tile, width), lambda i, at: (i, 0)) for d in downs]
     return call(
         kernel,
@@ -223,13 +237,13 @@
         (steps,),
         scalars,
         operands,
-        [((width, many), LOW, (width, many), lambda i, at: (0, 0))]
+        [((width, many), LOW, (width, many), lambda i, at: (0, 0))] * 2
         + [((many, cols), LOW, (many, tile), lambda i, at: (0, i))] * 2
         + [((seqs, share, width), LOW, (seqs, share, width), lambda i, at: (0, 0, 0))],
         [pltpu.VMEM((many, width), LOW)],
         (),
         after,
-        4 * many * width * hid,
+        32,
     )
 
 
@@ -245,15 +259,20 @@
     def kernel(at, *refs):
         norm_refs, refs = refs[:chips], refs[chips:]
         back_refs, w_refs, refs = refs[:2], refs[2:4], refs[4:]
-        acts, grads, flip_n, refs = refs[:2], refs[2:4], refs[4], refs[5:]
+        act_own, gate_own, up_own, flip_n, act_far, grad_far, flip_far, refs = refs[:7] + (refs[7:],)
         mid_keep, mid_give, normed, mid = refs
+        acts = (act_own, act_far)
+        gates = (gate_own, grad_far.at[0])
+        ups = (up_own, grad_far.at[1])
         i = pl.program_id(0)
 
         @pl.when(i == 0)
         def _():
             for k in range(chips):
                 normed[k * share : (k + 1) * share] = norm_refs[k][...]
-                flip_n[:, k * share : (k + 1) * share] = norm_refs[k][...].T
+                turned = norm_refs[k][...].T
+                flip_n[:, k * share : (k + 1) * share] = turned
+                flip_far[:, k * share : (k + 1) * share] = turned
             mid[...] = jnp.zeros_like(mid)
 
         def units(size):
@@ -268,14 +287,14 @@
                 d_gate = (d_act * up * (sigm * (1.0 + gate * (1.0 - sigm)))).astype(LOW)
                 d_up = (d_act * silu).astype(LOW)
                 acts[half][:, :size] = act
-                grads[half][0, :, :size] = d_gate
-                grads[half][1, :, :size] = d_up
+                gates[half][:, :size] = d_gate
+                ups[half][:, :size] = d_up
                 mid[...] += dot(d_gate, gate_w, 1, 0) + dot(d_up, up_w, 1, 0)
                 if size < tile:
                     rest = jnp.zeros((rows, tile - size), LOW)
                     acts[half][:, size:] = rest
-                    grads[half][0, :, size:] = rest
-                    grads[half][1, :, size:] = rest
+                    gates[half][:, size:] = rest
+                    ups[half][:, size:] = rest
 
         if last == tile:
             units(tile)
@@ -295,9 +314,11 @@
     operands += [(w, (2, tile, width), lambda i, at: (0, i, 0)) for w in weights]
     many = seqs * rows
     cols = -(-hid // LANES) * LANES
-    outputs = [((many, cols), LOW, (rows, tile), lambda i, at: (s, i))] * 2
-    outputs += [((2, many, cols), LOW, (2, rows, tile), lambda i, at: (0, s, i))] * 2
+    outputs = [((many, cols), LOW, (rows, tile), lambda i, at: (s, i))] * 3
     outputs += [((width, many), LOW, (width, rows), lambda i, at: (0, s))]
+    outputs += [((rows, cols), LOW, (rows, tile), lambda i, at: (0, i))]
+    outputs += [((2, rows, cols), LOW, (2, rows, tile), lambda i, at: (0, 0, i))]
+    outputs += [((width, rows), LOW, (width, rows), fixed)]
     given = (chips - 1, share, width)
     outputs += [
         ((share, width), FULL, (share, width), fixed),
@@ -316,33 +337,40 @@
         ],
         carry,
         after,
-        8 * rows * width * 2 * hid,
+        42,
     )
 
 
-def down_product(seqs, scalars, acts, downs, after):
-    many, cols = acts[0].shape
+def down_product(scalars, act, fars, downs, after):
+    rows, cols = fars[0].shape
+    seqs = len(fars)
     hid, width = downs[0].shape
-    rows = many // seqs
     chips = lax.axis_size("ch") // CORES
     share = rows // chips
     parts = 2
     wide = width // parts
 
-    def kernel(at, act0, act1, down0, down1, keep, give):
-        value = dot(act0[:, :hid], down0[...], 1, 0) + dot(act1[:, :hid], down1[...], 1, 0)
-        keep[0] = value[:share]
-        for k in range(1, chips):
-            give[k - 1, 0] = value[k * share : (k + 1) * share].astype(LOW)
-
-    act_spec = ((rows, cols), lambda i, s, at: (s, 0))
+    def kernel(at, act0, *refs):
+        far, (down0, down1, keep, give) = refs[:seqs], refs[seqs:]
+        s = pl.program_id(1)
+        for n in range(seqs):
+
+            @pl.when(s == n)
+            def _():
+                value = dot(act0[:, :hid], down0[...], 1, 0) + dot(far[n][:, :hid], down1[...], 1, 0)
+                keep[0] = value[:share]
+                for k in range(1, chips):
+                    give[k - 1, 0] = value[k * share : (k + 1) * share].astype(LOW)
+
     down_spec = ((hid, wide), lambda i, s, at: (0, i))
     return call(
         kernel,
         "down_product",
         (parts, seqs),
         scalars,
-        [(acts[0], *act_spec), (acts[1], *act_spec), (downs[0], *down_spec), (downs[1], *down_spec)],
+        [(act, (rows, cols), lambda i, s, at: (s, 0))]
+        + [(f, (rows, cols), lambda i, s, at: (0, 0)) for f in fars]
+        + [(downs[0], *down_spec), (downs[1], *down_spec)],
         [
             ((seqs, share, width), FULL, (1, share, wide), lambda i, s, at: (s, 0, i)),
             (
@@ -355,62 +383,69 @@
         [],
         (),
         after,
-        4 * many * width * hid,
+        25,
     )
 
 
-def weight_grad(scalars, left, right, first, kinds, other=None, bit=None, after=()):
-    width, tokens = left.shape
-    cols = right.shape[2]
+def weight_grad(scalars, pairs, cuts, after):
+    width = pairs[0][0].shape[0]
+    cols = pairs[0][2].shape[-1]
     count = lax.axis_size("seq")
     rows = width // count
-    parts = 2
-    tall = width // parts
-    tops = count // (2 * parts)
-
-    def kernel(at, left_ref, right_ref, *refs):
-        value = dot(left_ref[...], right_ref[0], 1, 0)
-        if bit is None:
-            refs[0][0] = value.astype(LOW)
-            return
-        if other is not None:
-            value = value + refs[0][0].astype(FULL)
-        value = value.astype(LOW).reshape(tops >> bit, 2, 1 << bit, rows, cols)
-        zero, one = [value[:, k].reshape(tops, rows, cols) for k in range(2)]
-        keep, give = refs[-2:]
-
-        @pl.when(at[2 + bit] == 0)
-        def _():
-            keep[0] = zero
-            give[0] = one
-
-        @pl.when(at[2 + bit] != 0)
-        def _():
-            keep[0] = one
-            give[0] = zero
-
-    operands = [
-        (left, (tall, tokens), lambda k, i, at: (i, 0)),
-        (right, (1, tokens, cols), lambda k, i, at: (first + k, 0, 0)),
-    ]
-    if other is not None:
-        operands.append((other, (1, tall, cols), lambda k, i, at: (first + k, i, 0)))
-    if bit is not None:
-        block = (1, tops, rows, cols)
-        outputs = [((kinds, count // 2, rows, cols), LOW, block, lambda k, i, at: (k, i, 0, 0))] * 2
-    else:
-        outputs = [((kinds, width, cols), LOW, (1, tall, cols), lambda k, i, at: (k, i, 0))]
+    half = count // 2
+
+    def kernel(at, *refs):
+        i = pl.program_id(0)
+        value = None
+        for n, (_, _, _, kind) in enumerate(pairs):
+            right = refs[2 * n + 1][...] if kind is None else refs[2 * n + 1][0]
+            term = dot(refs[2 * n][...], right, 1, 0)
+            value = term if value is None else value + term
+        value = value.astype(LOW)
+        outs = refs[2 * len(pairs) :]
+        for n, (bit, first, last) in enumerate(cuts):
+            split = value.reshape(half >> bit, 2, 1 << bit, rows, COLUMN_TILE)
+            zero, one = [split[:, k].reshape(half, rows, COLUMN_TILE) for k in range(2)]
+            keep, give = outs[2 * n : 2 * n + 2]
+            here = jnp.logical_and(i >= first, i < last)
+
+            @pl.when(jnp.logical_and(here, at[2 + bit] == 0))
+            def _():
+                keep[...] = zero
+                give[...] = one
+
+            @pl.when(jnp.logical_and(here, at[2 + bit] != 0))
+            def _():
+                keep[...] = one
+                give[...] = zero
+
+    operands, outputs = ([], [])
+    for left, n, right, kind in pairs:
+        tokens = right.shape[-2]
+        operands.append((left, (width, tokens), lambda i, at, n=n: (0, n)))
+        if kind is None:
+            operands.append((right, (tokens, COLUMN_TILE), lambda i, at: (0, i)))
+        else:
+            operands.append((right, (1, tokens, COLUMN_TILE), lambda i, at, k=kind: (k, 0, i)))
+
+    def tile(first, last):
+        return lambda i, at: (0, 0, jnp.clip(i, first, last - 1) - first)
+
+    for _, first, last in cuts:
+        wide = min(last * COLUMN_TILE, cols) - first * COLUMN_TILE
+        whole = (half, rows, wide)
+        outputs += [(whole, LOW, (half, rows, COLUMN_TILE), tile(first, last))] * 2
     return call(
         kernel,
         "weight_grad",
-        (kinds, parts),
+        (-(-cols // COLUMN_TILE),),
         scalars,
         operands,
         outputs,
         [],
         (),
         after,
-        2 * kinds * width * tokens * cols,
+        22 if len(pairs) > 1 else 19,
     )
 
 
@@ -440,21 +475,21 @@
     return ([half(t, mine) for t in terms] + [trade(give, bit)], give)
 
 
-def conv_backward(s, seqs, scalars, mine, other, proj, conv, taps, ahead, carry, after):
+def conv_backward(s, seqs, scalars, mine, other, proj, conv, taps, edge, carry, after):
     kinds, length, chans = proj.shape
     chips, share, _ = mine.shape
     count = chips * CORES
     steps = taps.shape[0]
 
     def kernel(
-        at, mine_ref, other_ref, proj_ref, conv_ref, taps_ref, ahead_ref,
-        all_ref, keep_ref, give_ref, sums_ref, later
+        at, mine_ref, other_ref, proj_ref, conv_ref, taps_ref, edge_ref,
+        all_ref, keep_ref, give_ref, sums_ref, before_ref, later
     ):
         i = count - 1 - pl.program_id(0)
 
         @pl.when(pl.program_id(0) == 0)
         def _():
-            later[...] = ahead_ref[...]
+            later[...] = jnp.zeros_like(later)
             sums_ref[...] = jnp.zeros_like(sums_ref)
 
         own = i % CORES == at[1]
@@ -465,16 +500,31 @@
         d_conv = d_mixed * c_gate
         longer = jnp.concatenate([d_conv, later[...]], axis=0)
         later[...] = d_conv[:HALO]
-        d_gated = jnp.zeros((share, chans), FULL)
-        for tap in range(steps):
-            ahead_by = steps - 1 - tap
-            term = longer[ahead_by : ahead_by + share]
-            d_gated = d_gated + taps_ref[tap : tap + 1] * term
-            sums_ref[tap : tap + 1] += jnp.sum(term * gated, axis=0, keepdims=True)
-        d_gated = d_gated.astype(LOW).astype(FULL)
+
+        def spread(longer, gated):
+            size = gated.shape[0]
+            d_gated = jnp.zeros((size, chans), FULL)
+            for tap in range(steps):
+                ahead_by = steps - 1 - tap
+                term = longer[ahead_by : ahead_by + size]
+                d_gated = d_gated + taps_ref[tap : tap + 1] * term
+                sums_ref[tap : tap + 1] += jnp.sum(term * gated, axis=0, keepdims=True)
+            return d_gated.astype(LOW).astype(FULL)
+
+        @pl.when(i == 0)
+        def _():
+            b_edge, x_edge = (edge_ref[0].astype(FULL), edge_ref[2].astype(FULL))
+            rows = jnp.concatenate([jnp.zeros((HALO, chans), FULL), d_conv[:HALO]], axis=0)
+            d_edge = spread(rows, (b_edge * x_edge).astype(LOW).astype(FULL))
+            none = jnp.zeros((HALO, chans), FULL)
+            before_ref[...] = jnp.concatenate(
+                [d_edge * x_edge, none, d_edge * b_edge], axis=1
+            ).astype(LOW)
+
+        d_gated = spread(longer, gated)
         values = [(d_gated * x_val).astype(LOW), d_c.astype(LOW), (d_gated * b_gate).astype(LOW)]
         value = jnp.concatenate(values, axis=1)
-        all_ref[0] = value
+        all_ref[...] = value
 
         @pl.when(own)
         def _():
@@ -498,23 +548,24 @@
             (proj, (kinds, share, chans), lambda i, at: (0, back(i), 0)),
             (conv, (share, chans), lambda i, at: (back(i), 0)),
             (taps, taps.shape, lambda i, at: (0, 0)),
-            (ahead, (HALO, chans), lambda i, at: (0, 0)),
+            (edge, edge.shape, lambda i, at: (0, 0, 0)),
         ],
         [
             (
-                (1, seqs * length, kinds * chans),
+                (seqs * length, kinds * chans),
                 LOW,
-                (1, share, kinds * chans),
-                lambda i, at: (0, s * count + back(i), 0),
+                (share, kinds * chans),
+                lambda i, at: (s * count + back(i), 0),
             ),
             split,
             split,
             ((8, chans), FULL, (8, chans), lambda i, at: (0, 0)),
+            ((HALO, kinds * chans), LOW, (HALO, kinds * chans), lambda i, at: (0, 0)),
         ],
         [pltpu.VMEM((HALO, chans), FULL)],
         carry,
         after,
-        40 * length * chans,
+        8,
     )
 
 
@@ -553,18 +604,19 @@
     in_other = swap_cores(in_three)
     downs = (down, down_other)
     gate_ups = (gate_up, gate_up_other)
-    projs, convs, mixes, owns = ([], [], [], [])
+    projs, convs, mixes, owns, edges = ([], [], [], [], [])
     flips = {"in": (), "grad": ()}
     arrived = {}
 
     def forward(s, after):
-        flip, proj, conv, mine, theirs, own = conv_forward(
+        flip, proj, conv, mine, theirs, own, edge, edge_proj = conv_forward(
             s, scalars, hidden, tail, gain_in[None], in_three, conv_taps, flips["in"], after
         )
         flips["in"] = (flip,)
         projs.append(proj)
         convs.append(conv)
         owns.append(own)
+        edges.append((edge, edge_proj))
         mixes.append((mine, swap_cores(theirs)))
         return (conv,)
 
@@ -594,12 +646,17 @@
         return (low,)
 
     def back(after):
-        flips["grad"], own, other, state["cots"] = act_back(scalars, cotangent, downs, after)
+        out = act_back(scalars, cotangent, downs, after)
+        flips["grad"], flips["far"], own, other, state["cots"] = out
         state["d_acts"] = (own, other)
         return (own,)
 
     state = {
         "ffn": (),
+        "act_far": [],
+        "act_sent": [],
+        "grad_far": [],
+        "flip_far": [],
         "proj": (),
         "conv": jnp.zeros((taps, chans), FULL),
         "in": jnp.zeros((width,), FULL),
@@ -609,10 +666,17 @@
 
     def feed(s, after):
         out = ffn(s, seqs, scalars, normed[s], state["d_acts"], gate_ups, state["ffn"], after)
-        state["ffn"] = tuple(out[:5])
-        keep, give = out[5:]
+        state["ffn"] = tuple(out[:4])
+        act_far, grad_far, flip_far, keep, give = out[4:]
+        state["act_far"].append(swap_cores(act_far))
+        state["grad_far"].append(swap_cores(grad_far))
+        state["flip_far"].append(swap_cores(flip_far))
+        state["act_sent"].append(act_far)
         results.append((keep, [shift_chips(give[k - 1], k) for k in range(1, chips)]))
         return (give,)
+
+    def far(s):
+        return (state["act_far"][s], state["grad_far"][s], state["flip_far"][s])
 
     def middle(s, after):
         d_mid, pieces = results[s]
@@ -634,19 +698,18 @@
         other = dot(d_mix, out_other, 1, 0).astype(LOW)
         give = swap_cores(other).reshape(chips, share, chans)
         mine = dot(d_mix, out_weight, 1, 0).astype(LOW).reshape(chips, share, chans)
-        first = (chips - chip) % chips
-        head = jnp.where(core == 0, pick(mine, first)[:HALO], pick(give, first)[:HALO])
-        ahead = shifted(head.astype(FULL) * projs[s][1, :HALO].astype(FULL), "seq", -1)
-        mixed_backs.append((mine, give, ahead))
+        mixed_backs.append((mine, give))
         return (other, mine)
 
-    proj_parts = []
+    proj_parts, befores = ([], [])
 
     def conv_back(s, after):
-        mine, give, ahead = mixed_backs[s]
-        d_proj, keep, pass_on, sums = conv_backward(
-            s, seqs, scalars, mine, give, projs[s], convs[s], conv_taps, ahead, state["proj"], after
+        mine, give = mixed_backs[s]
+        d_proj, keep, pass_on, sums, before = conv_backward(
+            s, seqs, scalars, mine, give, projs[s], convs[s], conv_taps, edges[s][1],
+            state["proj"], after,
         )
+        befores.append(before)
         state["proj"] = (d_proj,)
         state["conv"] = state["conv"] + sums[:taps]
         proj_parts.append((keep, swap_cores(pass_on)))
@@ -666,11 +729,15 @@
 
     outs_grads = []
 
-    def finish(s, after):
-        keep, got = proj_parts[s]
-        d_in = in_part(0, keep, got)
+    def arrive(s, after):
+        d_in = in_part(0, *proj_parts[s])
         for piece in tie(in_parts[s], after):
             d_in = d_in + piece.astype(FULL)
+        in_parts[s] = d_in
+        return (d_in,)
+
+    def finish(s, after):
+        d_in = tie(in_parts[s], after).at[share - HALO :].add(state["edge"][s])
         rows = owns[s].astype(FULL)
         d_norm, gain_term = norm_back(rows, norm_scale(rows), gain_in, d_in)
         state["in"] = state["in"] + gain_term
@@ -678,7 +745,7 @@
         return (outs_grads[-1],)
 
     def out_send(after):
-        keep, give = down_product(seqs, scalars, state["ffn"][:2], downs, after)
+        keep, give = down_product(scalars, state["ffn"][0], state["act_sent"], downs, after)
         state["out"] = (keep, [shift_chips(give[k - 1], k) for k in range(1, chips)])
         return (give,)
 
@@ -692,33 +759,50 @@
 
     grads = {}
 
-    def jobs(name):
-        act_own, act_other, dgu_own, dgu_other, flip_n = state["ffn"]
-        if name == "down":
-            return (flips["grad"], act_own[None], act_other[None])
-        return (flip_n, dgu_own, dgu_other)
-
-    def grad_other(name, kinds, after):
-        left, _, other = jobs(name)
-        (part,) = weight_grad(scalars, left, other, 0, kinds, after=after)
-        state[name] = swap_cores(part)
-        return (part,)
-
     def begin(name, keep, give, bits):
         grads[name] = ([keep, trade(give, bits[0])], bits[1:])
 
-    def grad_own(name, source, kind, bits, after):
-        left, own, _ = jobs(source)
-        keep, give = weight_grad(scalars, left, own, kind, 1, state[source], bits[0], after)
-        begin(name, keep[0], give[0], bits)
-        return (keep,)
-
-    def in_grad(bits, after):
-        keep, give = weight_grad(
-            scalars, flips["in"][0], state["proj"][0], 0, 1, bit=bits[0], after=after
-        )
-        begin("in", keep[0], give[0], bits)
-        return (give,)
+    def own_grad(name, pairs, orders, after):
+        tiles = -(-pairs[0][2].shape[-1] // COLUMN_TILE)
+        edges = [tiles * n // len(orders) for n in range(len(orders) + 1)]
+        cuts = [(bits[0], edges[n], edges[n + 1]) for n, bits in enumerate(orders)]
+        parts = weight_grad(scalars, pairs, cuts, after)
+        for n, bits in enumerate(orders):
+            begin(name + str(n), parts[2 * n], parts[2 * n + 1], bits)
+        return (parts[0],)
+
+    def down_grad(orders, after):
+        pairs = [(flips["grad"], 0, state["ffn"][0], None)]
+        pairs += [(flips["far"], s, state["act_far"][s], None) for s in range(seqs)]
+        return own_grad("down", pairs, orders, after)
+
+    def hidden_grad(name, kind, orders, after):
+        pairs = [(state["ffn"][3], 0, state["ffn"][1 + kind], None)]
+        for s in range(seqs):
+            pairs.append((state["flip_far"][s], 0, state["grad_far"][s], kind))
+        return own_grad(name, pairs, orders, after)
+
+    def in_grad(orders, after):
+        left = jnp.concatenate([edge for edge, _ in edges], axis=0).T
+        pairs = [(flips["in"][0], 0, state["proj"][0], None)]
+        pairs.append((left, 0, jnp.concatenate(befores, axis=0), None))
+        return own_grad("in", pairs, orders, after)
+
+    def edge_send(after):
+        part = dot(tie(jnp.concatenate(befores, axis=0), after), in_flat, 1, 1)
+        state["edge"] = shifted(part.reshape(seqs, HALO, width)[:, HALO - 8 :], "seq", -1)
+        return (part,)
+
+    def edge_hop(bit, after):
+        value = tie(state["edge"], after)
+        pairs = [(i, i ^ (1 << bit)) for i in range(count)]
+        state["edge"] = value + lax.ppermute(value, "ch", pairs)
+        return after
+
+    def edge_place(after):
+        value = jnp.pad(state["edge"], ((0, 0), (HALO - 8, 0), (0, 0)))
+        state["edge"] = jnp.where(me == count - 1, value, 0.0)
+        return after
 
     def step(name, after):
         terms, bits = grads[name]
@@ -776,6 +860,8 @@
         return (in_flat, in_flat_other)
 
     in_flat = in_flat_other = None
+    near_y = tuple(range(places))
+    near_z = (1, 0) + tuple(range(2, places))
     last = ()
     last = forward(0, last)
     last = mix_send(0, last)
@@ -788,71 +874,78 @@
     last = join(1, last)
     last = feed(0, last)
     last = join(2, last)
+    last = flat_weights(last)
     last = feed(1, last)
     last = middle(0, last)
-    last = feed(2, last)
-    last = middle(1, last)
+    last = feed(2, last + far(0))
+    last = middle(1, last + far(1))
+    last = down_grad((near_y,), last)
+    last = middle(2, last)
     last = mix_back(0, last)
-    last = grad_other("down", 1, last)
+    last = hidden_grad("gate", 0, (near_z,), last)
     last = conv_back(0, last)
-    last = middle(2, last)
     last = mix_back(1, last)
-    last = flat_weights(last)
+    last = mix_back(2, last)
+    last = in_send(0, last)
+    last = hidden_grad("up", 1, (near_y,), last)
+    last = step("down0", last)
+    last = arrive(0, last)
     last = conv_back(1, last)
-    last = mix_back(2, last)
-    near_y = tuple(range(places))
-    near_z = (1, 0) + tuple(range(2, places))
-    last = grad_own("down", "down", 0, near_y, last)
-    last = grad_other("gate", 2, last)
-    last = in_send(0, last)
     last = conv_back(2, last)
-    last = grad_own("up", "gate", 1, near_z, last)
-    last = grad_own("gate", "gate", 0, near_y, last)
+    last = edge_send(last)
+    last = step("gate0", last)
+    last = in_send(1, last)
+    last = in_send(2, last)
+    last = in_grad((near_y,), last)
+    last = arrive(1, last)
+    last = step("down0", last)
+    last = arrive(2, last)
+    last = step("up0", last)
+    last = out_other_grad(last)
+    for bit in range(count.bit_length() - 1):
+        last = edge_hop(bit, last)
+    last = edge_place(last)
+    last = out_send(last)
+    last = out_grad(near_y, last)
+    last = end("down0", last)
+    last = step("gate0", last)
     last = finish(0, last)
-    last = step("down", last)
-    last = in_send(1, last)
-    last = in_grad(near_y, last)
     last = finish(1, last)
-    last = in_send(2, last)
-    last = out_other_grad(last)
-    last = out_send(last)
     last = finish(2, last)
-    last = step("up", last)
-    last = step("gate", last)
-    last = out_grad(near_y, last)
-    last = step("down", last)
-    last = step("in", last)
+    last = step("up0", last)
+    last = step("in0", last)
+    last = end("gate0", last)
     last = small_begin(last)
     last = small_hop(last)
-    last = small_hop(last)
-    last = step("gate", last)
-    last = end("down", last)
     last = out_finish(last)
     last = small_hop(last)
-    last = step("up", last)
-    last = step("in", last)
-    last = end("gate", last)
+    last = step("out", last)
+    last = end("up0", last)
+    last = step("in0", last)
+    last = small_hop(last)
     last = step("out", last)
     last = small_hop(last)
-    last = step("out", last)
-    last = end("up", last)
-    last = end("in", last)
+    last = end("in0", last)
     last = small_hop(last)
     last = end("out", last)
     while len(state["hops"]) > 0:
         last = small_hop(last)
-    down_grad, gate_grad, up_grad = [grads[n][:, :hid] for n in ("down", "gate", "up")]
+
+    def columns(name):
+        parts = [grads[n] for n in (name + "0", name + "1") if n in grads]
+        return jnp.concatenate(parts, axis=1) if len(parts) > 1 else parts[0]
+
     small = state["small"]
     return (
         state["out"],
         jnp.stack(outs_grads, axis=0),
         small[taps],
-        grads["in"].reshape(-1, 3, chans),
+        columns("in").reshape(-1, 3, chans),
         small[:taps],
         grads["out"],
         small[taps + 1],
-        jnp.stack([gate_grad, up_grad], axis=1),
-        down_grad,
+        jnp.stack([columns("gate")[:, :hid], columns("up")[:, :hid]], axis=1),
+        columns("down")[:, :hid],
     )
 
 

time: 703 us -> 621 us (0.88)
  waiting for transfers between devices: 133 us -> 76.7 us
  starting transfers between devices: 75.3 us -> 55.2 us
    ppermute x5, waiting for transfers between devices: 54.8 us -> 6.45 us  [small_hop(): state['small'] = value + lax.ppermute(value, axis, pairs)]
    ppermute x15, starting transfers between devices: 40.7 us -> 21.3 us  [trade(): return lax.ppermute(value, 'seq', [(i, i ^ 1 << bit) for i in range(count)])]
    ppermute x16 -> x23, waiting for transfers between devices: 13.8 us -> 0.06 us  [swap_cores(): return lax.ppermute(value, 'ch', [(i, i ^ 1) for i in range(count)])]
    dot_general x32 -> x33, matrix products: 66 us -> 60.7 us  [dot(): lax.dot_general(a, b, (((a_dim,), (b_dim,)), ((), ())), preferred_element...]
    unnamed x231 -> x201, local copies, waits for them, and re-layouts: 18.9 us -> 17.3 us
    pallas_call x17 -> x15, Pallas kernels: 315 us -> 314 us  [call(): pl.pallas_call(body, name=name, grid_spec=pltpu.PrefetchScalarGridSpec(nu...]
  transfers between devices with their start and end apart: 56 -> 63, of which waited for: 12 -> 12; matrix products, arithmetic and copies ran while one was open for 22% -> 25% of each run, Pallas kernels for 40% -> 52%
where the time goes in v3:
time: 621 us; the launch traced here: 610 us
  Pallas kernels  314 us (51%)
  waiting for transfers between devices  76.7 us (12%)
  other arithmetic  67 us (11%)
  matrix products  60.7 us (10%)
  starting transfers between devices  55.2 us (9%)
  local copies, waits for them, and re-layouts  33.7 us (5%)
    pallas_call x15, Pallas kernels, call(): pl.pallas_call(body, name=name, grid_spec=pltpu.PrefetchScalarGridSpec(nu...  314 us
    ppermute x15, waiting for transfers between devices, trade(): return lax.ppermute(value, 'seq', [(i, i ^ 1 << bit) for i in range(count)])  63.1 us
    dot_general x33, matrix products, dot(): lax.dot_general(a, b, (((a_dim,), (b_dim,)), ((), ())), preferred_element...  60.7 us
    ppermute x15, starting transfers between devices, trade(): return lax.ppermute(value, 'seq', [(i, i ^ 1 << bit) for i in range(count)])  21.3 us
    convert_element_type x10, other arithmetic, scatter_step(): give = total([half(t, 1 - mine) for t in terms]).astype(LOW)  21 us
    unnamed x201, local copies, waits for them, and re-layouts  17.3 us
    ppermute x16, starting transfers between devices, shift_chips(): lax.ppermute(value, 'ch', [(i, (i + CORES * steps) % count) for i in rang...  17.1 us
  transfers between devices with their start and end apart: 63, of which 12 were waited for; matrix products, arithmetic and copies ran while one was open for 25% of the time, Pallas kernels for 52%

profile of v3, /device:TPU:0, one launch (start us, length us, event | category | flops | bytes accessed | tf_op | source)
XLA Modules:
  0.0 610.1 jit_solution(9494063145426746964)
XLA Ops:
  2.1 4.5 collective-permute-start
  10.9 11.9 %conv_forward.3 = (bf16[1536,3072]{1,0:T(8,128)(2,1)}, bf16[3,1024,384]{2,1,0:T(8,128)(2,1)}, bf16[1024,384]{1,0:T(8,128)(2,1)}, bf16[2,256,384]{2,1,0:T(8,128)(...) custom-call(s32[5]{0:T(128)} %stack.56.refs_0_, ...), custom_call_target="tpu_custom_call" | custom-call | flops 6918000128 | bytes 1 | tf_op jit(solution)/shard_map/conv_forward/pallas_call | solution.py:75
  28.4 12.0 %conv_forward.4 = (bf16[1536,3072]{1,0:T(8,128)(2,1)}, bf16[3,1024,384]{2,1,0:T(8,128)(2,1)}, bf16[1024,384]{1,0:T(8,128)(2,1)}, bf16[2,256,384]{2,1,0:T(8,128)(...) custom-call(s32[5]{0:T(128)} %stack.56.refs_0_, ...), custom_call_target="tpu_custom_call", output_to_operand_aliasing={{0}: (7, {})} | custom-call | flops 6918000128 | bytes 1 | tf_op jit(solution)/shard_map/conv_forward/pallas_call | solution.py:75
  45.6 1.8 fusion.95
  47.3 12.1 %conv_forward.5 = (bf16[1536,3072]{1,0:T(8,128)(2,1)}, bf16[3,1024,384]{2,1,0:T(8,128)(2,1)}, bf16[1024,384]{1,0:T(8,128)(2,1)}, bf16[2,256,384]{2,1,0:T(8,128)(...) custom-call(s32[5]{0:T(128)} %stack.56.refs_0_, ...), custom_call_target="tpu_custom_call", output_to_operand_aliasing={{0}: (7, {})} | custom-call | flops 6918000128 | bytes 1 | tf_op jit(solution)/shard_map/conv_forward/pallas_call | solution.py:75
  60.3 1.9 multiply_reduce_fusion.8
  64.5 1.8 fusion.94
  69.9 31.5 %act_back.1 = (bf16[1536,1536]{1,0:T(8,128)(2,1)}, bf16[1536,1536]{1,0:T(8,128)(2,1)}, bf16[1536,1792]{1,0:T(8,128)(2,1)}, bf16[1536,1792]{1,0:T(8,128)(2,1)}, bf16[3,256,1536]{2,1,0:T(8,128)(2,1)}) custom-call(s32[5]{0:T(128)} %stack.56.refs_0_, bf16[3,1024,1536]{2,1,0:T(8,128)(2,1)} %refs_12_.1, bf16[3,1024,1536]{2,1,0:T(8,128)(2,1)} %refs_12_.1, ...), custom_call_target="tpu_custom_call" | custom-call | flops 18447998976 | bytes 1 | tf_op jit(solution)/shard_map/act_back/pallas_call | solution.py:75
  101.5 2.2 multiply_reduce_fusion.7
  105.9 33.7 %ffn.3 = (bf16[1536,1792]{1,0:T(8,128)(2,1)}, bf16[1536,1792]{1,0:T(8,128)(2,1)}, bf16[1536,1792]{1,0:T(8,128)(2,1)}, bf16[1536,1536]{1,0:T(8,128)(2,1)}, bf16[5...) custom-call(s32[5]{0:T(128)} %stack.56.refs_0_, ...), custom_call_target="tpu_custom_call" | custom-call | flops 24213000192 | bytes 1 | tf_op jit(solution)/shard_map/ffn/pallas_call | solution.py:75
  139.7 1.9 multiply_reduce_fusion.6
  144.0 2.3 slice_bitcast_fusion.4
  147.9 2.0 pad_maximum_fusion.1.refs_12_
  149.9 2.3 slice_bitcast_fusion.7
  152.2 1.9 pad_maximum_fusion.refs_11_
  154.2 33.4 %ffn.4 = (bf16[1536,1792]{1,0:T(8,128)(2,1)}, bf16[1536,1792]{1,0:T(8,128)(2,1)}, bf16[1536,1792]{1,0:T(8,128)(2,1)}, bf16[1536,1536]{1,0:T(8,128)(2,1)}, bf16[5...) custom-call(s32[5]{0:T(128)} %stack.56.refs_0_, ...), custom_call_target="tpu_custom_call", output_to_operand_aliasing={{0}: (7, {}), {1}: (8, {}), {2}: (9, {}), {3}: (10, {})} | custom-call | flops 24213000192 | bytes 1 | tf_op jit(solution)/shard_map/ffn/pallas_call | solution.py:75
  189.8 3.4 fusion.128
  194.8 33.5 %ffn.5 = (bf16[1536,1792]{1,0:T(8,128)(2,1)}, bf16[1536,1792]{1,0:T(8,128)(2,1)}, bf16[1536,1792]{1,0:T(8,128)(2,1)}, bf16[1536,1536]{1,0:T(8,128)(2,1)}, bf16[5...) custom-call(s32[5]{0:T(128)} %stack.56.refs_0_, ...), custom_call_target="tpu_custom_call", output_to_operand_aliasing={{0}: (7, {}), {1}: (8, {}), {2}: (9, {}), {3}: (10, {})} | custom-call | flops 24213000192 | bytes 1 | tf_op jit(solution)/shard_map/ffn/pallas_call | solution.py:75
  233.5 2.7 multiply_reduce_fusion.1
  236.6 3.1 fusion.127
  240.8 25.7 %weight_grad.4 = (bf16[4,192,1792]{2,1,0:T(8,128)(2,1)}, bf16[4,192,1792]{2,1,0:T(8,128)(2,1)}) custom-call(s32[5]{0:T(128)} %stack.56.refs_0_, bf16[1536,1536]{1,0:T(8,128)(2,1)} %get-tuple-element.223.refs_1_, bf16[1536,1792]{1,0:T(8,128)(2,1)} %get-tuple-element.218.refs_2_.refs_1_, bf16[1536,1536]{1,0:T(8,128)(2,1)} %get-tuple-element.224.refs_3_.refs_5_.refs_7_, ...), custom_call_target="tpu_custom_call" | custom-call | flops 12682999808 | bytes 1 | tf_op jit(solution)/shard_map/weight_grad/pallas_call | solution.py:75
  266.6 1.8 collective-permute-done.19
  269.0 3.2 fusion.126
  278.6 2.5 collective-permute-start.35
  281.1 25.2 %weight_grad.5 = (bf16[4,192,1792]{2,1,0:T(8,128)(2,1)}, bf16[4,192,1792]{2,1,0:T(8,128)(2,1)}) custom-call(s32[5]{0:T(128)} %stack.56.refs_0_, bf16[1536,1536]{1,0:T(8,128)(2,1)} %get-tuple-element.235.refs_1_, bf16[1536,1792]{1,0:T(8,128)(2,1)} %get-tuple-element.236.refs_2_, bf16[1536,512]{1,0:T(8,128)(2,1)} %copy-done.76, ...), custom_call_target="tpu_custom_call" | custom-call | flops 12682999808 | bytes 1 | tf_op jit(solution)/shard_map/weight_grad/pallas_call | solution.py:75
  307.0 8.3 %conv_backward.3 = (bf16[3072,1152]{1,0:T(8,128)(2,1)}, bf16[2,256,1152]{2,1,0:T(8,128)(2,1)}, bf16[2,256,1152]{2,1,0:T(8,128)(2,1)}, f32[8,384]{1,0:T(8,128)}, bf16[16,1152]{1,0:T(8,128)(2,1)}) custom-call(s32[5]{0:T(128)} %stack.56.refs_0_, bf16[2,256,384]{2,1,0:T(8,128)(2,1)} %bitcast.360, bf16[2,256,384]{2,1,0:T(8,128)(2,1)} %bitcast.356, ...), custom_call_target="tpu_custom_call" | custom-call | flops 4611999744 | bytes 1 | tf_op jit(solution)/shard_map/conv_backward/pallas_call | solution.py:75
  316.3 2.1 constant_dynamic-update-slice_fusion.2
  322.4 2.2 constant_dynamic-update-slice_fusion.11
  332.2 2.4 fusion.76
  334.6 2.3 fusion.11.refs_9_
  337.8 25.2 %weight_grad.6 = (bf16[4,192,1792]{2,1,0:T(8,128)(2,1)}, bf16[4,192,1792]{2,1,0:T(8,128)(2,1)}) custom-call(s32[5]{0:T(128)} %stack.56.refs_0_, bf16[1536,1536]{1,0:T(8,128)(2,1)} %get-tuple-element.235.refs_1_, bf16[1536,1792]{1,0:T(8,128)(2,1)} %get-tuple-element.245.refs_2_, bf16[1536,512]{1,0:T(8,128)(2,1)} %copy-done.76, ...), custom_call_target="tpu_custom_call" | custom-call | flops 12682999808 | bytes 1 | tf_op jit(solution)/shard_map/weight_grad/pallas_call | solution.py:75
  363.0 3.3 fusion.38
  368.4 3.4 fusion.5.refs_8_
  372.6 8.0 %conv_backward.4 = (bf16[3072,1152]{1,0:T(8,128)(2,1)}, bf16[2,256,1152]{2,1,0:T(8,128)(2,1)}, bf16[2,256,1152]{2,1,0:T(8,128)(2,1)}, f32[8,384]{1,0:T(8,128)}, bf16[16,1152]{1,0:T(8,128)(2,1)}) custom-call(s32[5]{0:T(128)} %stack.56.refs_0_, bf16[2,256,384]{2,1,0:T(8,128)(2,1)} %bitcast.357, ...), custom_call_target="tpu_custom_call", output_to_operand_aliasing={{0}: (7, {})} | custom-call | flops 4611999744 | bytes 1 | tf_op jit(solution)/shard_map/conv_backward/pallas_call | solution.py:75
  381.3 8.3 %conv_backward.5 = (bf16[3072,1152]{1,0:T(8,128)(2,1)}, bf16[2,256,1152]{2,1,0:T(8,128)(2,1)}, bf16[2,256,1152]{2,1,0:T(8,128)(2,1)}, f32[8,384]{1,0:T(8,128)}, bf16[16,1152]{1,0:T(8,128)(2,1)}) custom-call(s32[5]{0:T(128)} %stack.56.refs_0_, bf16[2,256,384]{2,1,0:T(8,128)(2,1)} %bitcast.358, ...), custom_call_target="tpu_custom_call", output_to_operand_aliasing={{0}: (7, {})} | custom-call | flops 4611999744 | bytes 1 | tf_op jit(solution)/shard_map/conv_backward/pallas_call | solution.py:75
  391.0 2.3 fusion.70
  394.5 2.4 fusion.66
  398.1 2.4 fusion.74
  401.8 2.9 fusion.39
  407.5 2.3 fusion.13.refs_5_
  410.6 20.3 %weight_grad.7 = (bf16[4,192,1152]{2,1,0:T(8,128)(2,1)}, bf16[4,192,1152]{2,1,0:T(8,128)(2,1)}) custom-call(s32[5]{0:T(128)} %stack.56.refs_0_, bf16[1536,3072]{1,0:T(8,128)(2,1)} %get-tuple-element.271.refs_1_, bf16[3072,1152]{1,0:T(8,128)(2,1)} %get-tuple-element.272.refs_2_, bf16[1536,48]{1,0:T(8,128)(2,1)} %bitcast.346, bf16[48,1152]{1,0:T(8,128)(2,1)} %copy-done.61, ...), custom_call_target="tpu_custom_call" | custom-call | flops 12682999808 | bytes 1 | tf_op jit(solution)/shard_map/weight_grad/pallas_call | solution.py:75
  431.9 3.1 fusion.7
  435.0 2.8 fusion.49
  437.8 5.1 collective-permute-done.39
  442.9 2.4 fusion.6
  445.4 2.9 fusion.40
  448.3 2.7 convolution_convert_fusion.refs_7_
  451.2 2.4 collective-permute-start.43
  453.9 2.5 collective-permute-start.44
  457.7 25.3 %down_product.1 = (f32[3,256,1536]{2,1,0:T(8,128)}, bf16[1,3,256,1536]{3,2,1,0:T(8,128)(2,1)}) custom-call(s32[5]{0:T(128)} %stack.56.refs_0_, bf16[1536,1792]{1,0:T(8,128)(2,1)} %get-tuple-element.218.refs_2_.refs_1_, bf16[512,1792]{1,0:T(8,128)(2,1)} %get-tuple-element.215.refs_2_, bf16[512,1792]{1,0:T(8,128)(2,1)} %get-tuple-element.219.refs_3_, ...), custom_call_target="tpu_custom_call" | custom-call | flops 14412499968 | bytes 1 | tf_op jit(solution)/shard_map/down_product/pallas_call | solution.py:75
  483.1 1.8 collective-permute-start.48
  485.8 5.6 add_convert_fusion.3
  492.4 3.1 fusion.46
  505.9 25.9 %collective-permute-done.48 = bf16[2,192,1792]{2,1,0:T(8,128)(2,1)S(1)} collective-permute-done((bf16[2,192,1792]{2,1,0:T(8,128)(2,1)}, bf16[2,192,1792]{2,1,0:T(8,128)(2,1)S(1)}, u32[]{:S(2)}, u32[]{:S(2)}) %collective-permute-start.48) | collective-permute-done | bytes 1376288 | tf_op jit(solution)/shard_map/ppermute | solution.py:454
  531.8 2.7 fusion.43
  537.6 2.4 collective-permute-start.54
  543.2 2.9 fusion.1
  547.3 20.7 %collective-permute-done.55 = bf16[1,192,1792]{2,1,0:T(8,128)(2,1)} collective-permute-done((bf16[1,192,1792]{2,1,0:T(8,128)(2,1)}, bf16[1,192,1792]{2,1,0:T(8,128)(2,1)}, u32[]{:S(2)}, u32[]{:S(2)}) %collective-permute-start.55) | collective-permute-done | bytes 688160 | tf_op jit(solution)/shard_map/ppermute | solution.py:454
  569.6 4.7 collective-permute-done.54
  578.4 1.9 collective-permute-start.57
  580.4 2.1 collective-permute-done.57
  585.1 3.9 copy.110
  590.6 10.9 %collective-permute-done.60 = bf16[1,192,1152]{2,1,0:T(8,128)(2,1)S(1)} collective-permute-done((bf16[1,192,1152]{2,1,0:T(8,128)(2,1)S(1)}, bf16[1,192,1152]{2,1,0:T(8,128)(2,1)S(1)}, u32[]{:S(2)}, u32[]{:S(2)}) %collective-permute-start.60) | collective-permute-done | bytes 442400 | tf_op jit(solution)/shard_map/ppermute | solution.py:454
  606.7 2.0 collective-permute-done.61
  (400 shorter events, 111.7 us)
Async XLA Ops:
  0.6 105.3 %collective-permute-start.10 = (bf16[2,1728,1536]{2,1,0:T(8,128)(2,1)}, bf16[2,1728,1536]{2,1,0:T(8,128)(2,1)}, u32[]{:S(2)}, u32[]{:S(2)}) collective-permute-start(bf16[2,1728,1536]{2,1,0:T(8,128)(2,1)} %bitcast.349), channel_id=1, source_target_pairs={{0,1},{1,0},{2,3},{3,2},{4,5},{5,4},{6,7},{7,6},{8,9},{9,8},{10,11... | collective-permute-start | bytes 31850504 | tf_op jit(solution)/shard_map/ppermute | solution.py:42
  2.1 8.2 %collective-permute-start = (bf16[3,16,1536]{2,1,0:T(8,128)(2,1)S(1)}, bf16[3,16,1536]{2,1,0:T(8,128)(2,1)S(1)}, u32[]{:S(2)}, u32[]{:S(2)}) collective-permute-start(bf16[3,16,1536]{2,1,0:T(8,128)(2,1)S(1)} %slice.198), channel_id=1, source_target_pairs={{0,4},{4,8},{8,12},{12,16},{16,20},{20,24},{24,28},{1,5},{5,9},{9,... | collective-permute-start | bytes 442376 | tf_op jit(solution)/shard_map/ppermute | solution.py:53
  6.5 19.0 %collective-permute-start.2 = (bf16[1536,384]{1,0:T(8,128)(2,1)}, bf16[1536,384]{1,0:T(8,128)(2,1)S(1)}, u32[]{:S(2)}, u32[]{:S(2)}) collective-permute-start(bf16[1536,384]{1,0:T(8,128)(2,1)} %param.19), channel_id=1, source_target_pairs={{0,1},{1,0},{2,3},{3,2},{4,5},{5,4},{6,7},{7,6},{8,9},{9,8},{10,11... | collective-permute-start | bytes 3538952 | tf_op jit(solution)/shard_map/ppermute | solution.py:42
  22.9 2.7 collective-permute-start.1
  23.0 121.0 %collective-permute-start.13 = (bf16[3,1536,384]{2,1,0:T(8,128)(2,1)}, bf16[3,1536,384]{2,1,0:T(8,128)(2,1)}, u32[]{:S(2)}, u32[]{:S(2)}) collective-permute-start(bf16[3,1536,384]{2,1,0:T(8,128)(2,1)} %bitcast.5.refs_5_), channel_id=1, source_target_pairs={{0,1},{1,0},{2,3},{3,2},{4,5},{5,4},{6,7},{7,6},{8,9},{9,8},{10,11... | collective-permute-start | bytes 10616840 | tf_op jit(solution)/shard_map/ppermute | solution.py:42
  23.4 45.4 %collective-permute-start.6 = (bf16[1728,1536]{1,0:T(8,128)(2,1)}, bf16[1728,1536]{1,0:T(8,128)(2,1)}, u32[]{:S(2)}, u32[]{:S(2)}) collective-permute-start(bf16[1728,1536]{1,0:T(8,128)(2,1)} %bitcast.314), channel_id=1, source_target_pairs={{0,1},{1,0},{2,3},{3,2},{4,5},{5,4},{6,7},{7,6},{8,9},{9,8},{10,11... | collective-permute-start | bytes 15925256 | tf_op jit(solution)/shard_map/ppermute | solution.py:42
  26.9 32.6 %collective-permute-start.3 = (bf16[256,1536]{1,0:T(8,128)(2,1)S(1)}, bf16[256,1536]{1,0:T(8,128)(2,1)S(1)}, u32[]{:S(2)}, u32[]{:S(2)}) collective-permute-start(bf16[256,1536]{1,0:T(8,128)(2,1)S(1)} %fusion.8.refs_8_), channel_id=1, source_target_pairs={{0,2},{1,3},{2,0},{3,1},{4,6},{5,7},{6,4},{7,5},{8,10},{9,11},{10,... | collective-permute-start | bytes 2359304 | tf_op jit(solution)/shard_map/ppermute | solution.py:47
  40.4 2.2 collective-permute-start.4
  44.4 57.0 %collective-permute-start.5 = (bf16[256,1536]{1,0:T(8,128)(2,1)S(1)}, bf16[256,1536]{1,0:T(8,128)(2,1)S(1)}, u32[]{:S(2)}, u32[]{:S(2)}) collective-permute-start(bf16[256,1536]{1,0:T(8,128)(2,1)S(1)} %fusion.9.refs_8_), channel_id=1, source_target_pairs={{0,2},{1,3},{2,0},{3,1},{4,6},{5,7},{6,4},{7,5},{8,10},{9,11},{10,... | collective-permute-start | bytes 2359304 | tf_op jit(solution)/shard_map/ppermute | solution.py:47
  59.5 4.1 collective-permute-start.7
  62.3 127.5 %copy-start.1 = (f32[256,1536]{1,0:T(8,128)}, f32[256,1536]{1,0:T(8,128)S(1)}, u32[]{:S(2)}) copy-start(f32[256,1536]{1,0:T(8,128)S(1)} %get-tuple-element.382) | copy-start | bytes 4718596
  63.6 42.4 %collective-permute-start.9 = (bf16[256,1536]{1,0:T(8,128)(2,1)}, bf16[256,1536]{1,0:T(8,128)(2,1)}, u32[]{:S(2)}, u32[]{:S(2)}) collective-permute-start(bf16[256,1536]{1,0:T(8,128)(2,1)} %multiply_convert_fusion.2.refs_1_), channel_id=1, source_target_pairs={{0,2},{1,3},{2,0},{3,1},{4,6},{5,7},{6,4},{7,5},{8,10},{9,11},{10,... | collective-permute-start | bytes 2359304 | tf_op jit(solution)/shard_map/ppermute | solution.py:47
  68.8 70.8 %collective-permute-start.8 = (bf16[256,1536]{1,0:T(8,128)(2,1)}, bf16[256,1536]{1,0:T(8,128)(2,1)}, u32[]{:S(2)}, u32[]{:S(2)}) collective-permute-start(bf16[256,1536]{1,0:T(8,128)(2,1)} %fusion.10.refs_15_), channel_id=1, source_target_pairs={{0,2},{1,3},{2,0},{3,1},{4,6},{5,7},{6,4},{7,5},{8,10},{9,11},{10,... | collective-permute-start | bytes 2359304 | tf_op jit(solution)/shard_map/ppermute | solution.py:47
  105.0 49.2 %collective-permute-start.12 = (bf16[256,1536]{1,0:T(8,128)(2,1)}, bf16[256,1536]{1,0:T(8,128)(2,1)}, u32[]{:S(2)}, u32[]{:S(2)}) collective-permute-start(bf16[256,1536]{1,0:T(8,128)(2,1)} %multiply_convert_fusion.1.refs_7_.refs_1_), channel_id=1, source_target_pairs={{0,2},{1,3},{2,0},{3,1},{4,6},{5,7},{6,4},{7,5},{8,10},{9,11},{10,... | collective-permute-start | bytes 2359304 | tf_op jit(solution)/shard_map/ppermute | solution.py:47
  142.9 50.3 %collective-permute-start.11 = (bf16[256,1536]{1,0:T(8,128)(2,1)}, bf16[256,1536]{1,0:T(8,128)(2,1)}, u32[]{:S(2)}, u32[]{:S(2)}) collective-permute-start(bf16[256,1536]{1,0:T(8,128)(2,1)} %multiply_convert_fusion.refs_1_), channel_id=1, source_target_pairs={{0,2},{1,3},{2,0},{3,1},{4,6},{5,7},{6,4},{7,5},{8,10},{9,11},{10,... | collective-permute-start | bytes 2359304 | tf_op jit(solution)/shard_map/ppermute | solution.py:47
  146.4 41.2 %collective-permute-start.14 = (bf16[256,1536]{1,0:T(8,128)(2,1)}, bf16[256,1536]{1,0:T(8,128)(2,1)}, u32[]{:S(2)}, u32[]{:S(2)}) collective-permute-start(bf16[256,1536]{1,0:T(8,128)(2,1)} %bitcast.30), channel_id=1, source_target_pairs={{0,2},{1,3},{2,0},{3,1},{4,6},{5,7},{6,4},{7,5},{8,10},{9,11},{10,... | collective-permute-start | bytes 2359304 | tf_op jit(solution)/shard_map/ppermute | solution.py:47
  147.4 47.4 %collective-permute-start.16 = (bf16[2,512,1792]{2,1,0:T(8,128)(2,1)}, bf16[2,512,1792]{2,1,0:T(8,128)(2,1)}, u32[]{:S(2)}, u32[]{:S(2)}) collective-permute-start(bf16[2,512,1792]{2,1,0:T(8,128)(2,1)} %get-tuple-element.216), channel_id=1, source_target_pairs={{0,1},{1,0},{2,3},{3,2},{4,5},{5,4},{6,7},{7,6},{8,9},{9,8},{10,11... | collective-permute-start | bytes 11010056 | tf_op jit(solution)/shard_map/ppermute | solution.py:42
  147.4 46.3 %collective-permute-start.15 = (bf16[512,1792]{1,0:T(8,128)(2,1)}, bf16[512,1792]{1,0:T(8,128)(2,1)}, u32[]{:S(2)}, u32[]{:S(2)}) collective-permute-start(bf16[512,1792]{1,0:T(8,128)(2,1)} %get-tuple-element.215.refs_2_), channel_id=1, source_target_pairs={{0,1},{1,0},{2,3},{3,2},{4,5},{5,4},{6,7},{7,6},{8,9},{9,8},{10,11... | collective-permute-start | bytes 5505032 | tf_op jit(solution)/shard_map/ppermute | solution.py:42
  154.2 39.1 %collective-permute-start.17 = (bf16[1536,512]{1,0:T(8,128)(2,1)}, bf16[1536,512]{1,0:T(8,128)(2,1)S(1)}, u32[]{:S(2)}, u32[]{:S(2)}) collective-permute-start(bf16[1536,512]{1,0:T(8,128)(2,1)} %get-tuple-element.217), channel_id=1, source_target_pairs={{0,1},{1,0},{2,3},{3,2},{4,5},{5,4},{6,7},{7,6},{8,9},{9,8},{10,11... | collective-permute-start | bytes 4718600 | tf_op jit(solution)/shard_map/ppermute | solution.py:42
  187.6 44.4 %collective-permute-start.23 = (bf16[2,512,1792]{2,1,0:T(8,128)(2,1)}, bf16[2,512,1792]{2,1,0:T(8,128)(2,1)}, u32[]{:S(2)}, u32[]{:S(2)}) collective-permute-start(bf16[2,512,1792]{2,1,0:T(8,128)(2,1)} %get-tuple-element.226), channel_id=1, source_target_pairs={{0,1},{1,0},{2,3},{3,2},{4,5},{5,4},{6,7},{7,6},{8,9},{9,8},{10,11... | collective-permute-start | bytes 11010056 | tf_op jit(solution)/shard_map/ppermute | solution.py:42
  193.2 38.8 %collective-permute-start.20 = (bf16[512,1792]{1,0:T(8,128)(2,1)}, bf16[512,1792]{1,0:T(8,128)(2,1)}, u32[]{:S(2)}, u32[]{:S(2)}) collective-permute-start(bf16[512,1792]{1,0:T(8,128)(2,1)} %get-tuple-element.219.refs_3_), channel_id=1, source_target_pairs={{0,1},{1,0},{2,3},{3,2},{4,5},{5,4},{6,7},{7,6},{8,9},{9,8},{10,11... | collective-permute-start | bytes 5505032 | tf_op jit(solution)/shard_map/ppermute | solution.py:42
  193.2 38.7 %collective-permute-start.24 = (bf16[1536,512]{1,0:T(8,128)(2,1)}, bf16[1536,512]{1,0:T(8,128)(2,1)}, u32[]{:S(2)}, u32[]{:S(2)}) collective-permute-start(bf16[1536,512]{1,0:T(8,128)(2,1)} %get-tuple-element.227), channel_id=1, source_target_pairs={{0,1},{1,0},{2,3},{3,2},{4,5},{5,4},{6,7},{7,6},{8,9},{9,8},{10,11... | collective-permute-start | bytes 4718600 | tf_op jit(solution)/shard_map/ppermute | solution.py:42
  193.7 37.2 %collective-permute-start.22 = (bf16[256,1536]{1,0:T(8,128)(2,1)}, bf16[256,1536]{1,0:T(8,128)(2,1)}, u32[]{:S(2)}, u32[]{:S(2)}) collective-permute-start(bf16[256,1536]{1,0:T(8,128)(2,1)} %bitcast.34), channel_id=1, source_target_pairs={{0,2},{1,3},{2,0},{3,1},{4,6},{5,7},{6,4},{7,5},{8,10},{9,11},{10,... | collective-permute-start | bytes 2359304 | tf_op jit(solution)/shard_map/ppermute | solution.py:47
  228.3 11.4 %collective-permute-start.21 = (bf16[512,1792]{1,0:T(8,128)(2,1)}, bf16[512,1792]{1,0:T(8,128)(2,1)}, u32[]{:S(2)}, u32[]{:S(2)}) collective-permute-start(bf16[512,1792]{1,0:T(8,128)(2,1)} %get-tuple-element.220.refs_4_), channel_id=1, source_target_pairs={{0,1},{1,0},{2,3},{3,2},{4,5},{5,4},{6,7},{7,6},{8,9},{9,8},{10,11... | collective-permute-start | bytes 5505032 | tf_op jit(solution)/shard_map/ppermute | solution.py:42
  230.9 42.4 %collective-permute-start.18 = (bf16[256,1536]{1,0:T(8,128)(2,1)}, bf16[256,1536]{1,0:T(8,128)(2,1)}, u32[]{:S(2)}, u32[]{:S(2)}) collective-permute-start(bf16[256,1536]{1,0:T(8,128)(2,1)} %get-tuple-element.231.refs_11_), channel_id=1, source_target_pairs={{0,2},{1,3},{2,0},{3,1},{4,6},{5,7},{6,4},{7,5},{8,10},{9,11},{10,... | collective-permute-start | bytes 2359304 | tf_op jit(solution)/shard_map/ppermute | solution.py:47
  232.0 36.3 %collective-permute-start.19 = (bf16[256,1536]{1,0:T(8,128)(2,1)}, bf16[256,1536]{1,0:T(8,128)(2,1)S(1)}, u32[]{:S(2)}, u32[]{:S(2)}) collective-permute-start(bf16[256,1536]{1,0:T(8,128)(2,1)} %bitcast.354), channel_id=1, source_target_pairs={{0,2},{1,3},{2,0},{3,1},{4,6},{5,7},{6,4},{7,5},{8,10},{9,11},{10,... | collective-permute-start | bytes 2359304 | tf_op jit(solution)/shard_map/ppermute | solution.py:47
  233.0 48.0 %collective-permute-start.28 = (bf16[2,512,1792]{2,1,0:T(8,128)(2,1)}, bf16[2,512,1792]{2,1,0:T(8,128)(2,1)}, u32[]{:S(2)}, u32[]{:S(2)}) collective-permute-start(bf16[2,512,1792]{2,1,0:T(8,128)(2,1)} %get-tuple-element.238), channel_id=1, source_target_pairs={{0,1},{1,0},{2,3},{3,2},{4,5},{5,4},{6,7},{7,6},{8,9},{9,8},{10,11... | collective-permute-start | bytes 11010056 | tf_op jit(solution)/shard_map/ppermute | solution.py:42
  233.0 45.6 %collective-permute-start.27 = (bf16[1536,512]{1,0:T(8,128)(2,1)}, bf16[1536,512]{1,0:T(8,128)(2,1)}, u32[]{:S(2)}, u32[]{:S(2)}) collective-permute-start(bf16[1536,512]{1,0:T(8,128)(2,1)} %get-tuple-element.237), channel_id=1, source_target_pairs={{0,1},{1,0},{2,3},{3,2},{4,5},{5,4},{6,7},{7,6},{8,9},{9,8},{10,11... | collective-permute-start | bytes 4718600 | tf_op jit(solution)/shard_map/ppermute | solution.py:42
  239.7 75.5 %collective-permute-start.25 = (bf16[256,1536]{1,0:T(8,128)(2,1)S(1)}, bf16[256,1536]{1,0:T(8,128)(2,1)}, u32[]{:S(2)}, u32[]{:S(2)}) collective-permute-start(bf16[256,1536]{1,0:T(8,128)(2,1)S(1)} %get-tuple-element.241.refs_9_), channel_id=1, source_target_pairs={{0,2},{1,3},{2,0},{3,1},{4,6},{5,7},{6,4},{7,5},{8,10},{9,11},{10,... | collective-permute-start | bytes 2359304 | tf_op jit(solution)/shard_map/ppermute | solution.py:47
  272.2 49.9 %collective-permute-start.29 = (bf16[256,1536]{1,0:T(8,128)(2,1)}, bf16[256,1536]{1,0:T(8,128)(2,1)S(1)}, u32[]{:S(2)}, u32[]{:S(2)}) collective-permute-start(bf16[256,1536]{1,0:T(8,128)(2,1)} %get-tuple-element.243), channel_id=1, source_target_pairs={{0,2},{1,3},{2,0},{3,1},{4,6},{5,7},{6,4},{7,5},{8,10},{9,11},{10,... | collective-permute-start | bytes 2359304 | tf_op jit(solution)/shard_map/ppermute | solution.py:47
  276.8 29.4 %collective-permute-start.26 = (bf16[512,384]{1,0:T(8,128)(2,1)S(1)}, bf16[512,384]{1,0:T(8,128)(2,1)S(1)}, u32[]{:S(2)}, u32[]{:S(2)}) collective-permute-start(bf16[512,384]{1,0:T(8,128)(2,1)S(1)} %convolution_convert_fusion.5.refs_9_), channel_id=1, source_target_pairs={{0,1},{1,0},{2,3},{3,2},{4,5},{5,4},{6,7},{7,6},{8,9},{9,8},{10,11... | collective-permute-start | bytes 1179656 | tf_op jit(solution)/shard_map/ppermute | solution.py:42
  278.6 84.4 %collective-permute-start.35 = (bf16[4,192,1792]{2,1,0:T(8,128)(2,1)}, bf16[4,192,1792]{2,1,0:T(8,128)(2,1)}, u32[]{:S(2)}, u32[]{:S(2)}) collective-permute-start(bf16[4,192,1792]{2,1,0:T(8,128)(2,1)} %get-tuple-element.255), channel_id=1, source_target_pairs={{0,4},{4,0},{8,12},{12,8},{16,20},{20,16},{24,28},{28,24},{1,5},{5... | collective-permute-start | bytes 8257544 | tf_op jit(solution)/shard_map/ppermute | solution.py:454
  320.2 51.7 %collective-permute-start.33 = (bf16[512,384]{1,0:T(8,128)(2,1)}, bf16[512,384]{1,0:T(8,128)(2,1)S(1)}, u32[]{:S(2)}, u32[]{:S(2)}) collective-permute-start(bf16[512,384]{1,0:T(8,128)(2,1)} %convolution_convert_fusion.4), channel_id=1, source_target_pairs={{0,1},{1,0},{2,3},{3,2},{4,5},{5,4},{6,7},{7,6},{8,9},{9,8},{10,11... | collective-permute-start | bytes 1179656 | tf_op jit(solution)/shard_map/ppermute | solution.py:42
  322.1 12.4 %collective-permute-start.30 = (bf16[2,256,1152]{2,1,0:T(8,128)(2,1)S(1)}, bf16[2,256,1152]{2,1,0:T(8,128)(2,1)S(1)}, u32[]{:S(2)}, u32[]{:S(2)}) collective-permute-start(bf16[2,256,1152]{2,1,0:T(8,128)(2,1)S(1)} %copy-done.80), channel_id=1, source_target_pairs={{0,1},{1,0},{2,3},{3,2},{4,5},{5,4},{6,7},{7,6},{8,9},{9,8},{10,11... | collective-permute-start | bytes 3538952 | tf_op jit(solution)/shard_map/ppermute | solution.py:42
  327.4 54.0 %collective-permute-start.32 = (bf16[512,384]{1,0:T(8,128)(2,1)}, bf16[512,384]{1,0:T(8,128)(2,1)}, u32[]{:S(2)}, u32[]{:S(2)}) collective-permute-start(bf16[512,384]{1,0:T(8,128)(2,1)} %convolution_convert_fusion.2), channel_id=1, source_target_pairs={{0,1},{1,0},{2,3},{3,2},{4,5},{5,4},{6,7},{7,6},{8,9},{9,8},{10,11... | collective-permute-start | bytes 1179656 | tf_op jit(solution)/shard_map/ppermute | solution.py:42
  327.6 72.9 %collective-permute-start.38 = (bf16[4,192,1792]{2,1,0:T(8,128)(2,1)}, bf16[4,192,1792]{2,1,0:T(8,128)(2,1)}, u32[]{:S(2)}, u32[]{:S(2)}) collective-permute-start(bf16[4,192,1792]{2,1,0:T(8,128)(2,1)} %get-tuple-element.263), channel_id=1, source_target_pairs={{0,8},{4,12},{8,0},{12,4},{16,24},{20,28},{24,16},{28,20},{1,9},{5... | collective-permute-start | bytes 8257544 | tf_op jit(solution)/shard_map/ppermute | solution.py:454
  336.9 30.0 %collective-permute-start.34 = (bf16[256,1536]{1,0:T(8,128)(2,1)}, bf16[256,1536]{1,0:T(8,128)(2,1)}, u32[]{:S(2)}, u32[]{:S(2)}) collective-permute-start(bf16[256,1536]{1,0:T(8,128)(2,1)} %fusion.11.refs_9_), channel_id=1, source_target_pairs={{0,2},{1,3},{2,0},{3,1},{4,6},{5,7},{6,4},{7,5},{8,10},{9,11},{10,... | collective-permute-start | bytes 2359304 | tf_op jit(solution)/shard_map/ppermute | solution.py:47
  366.3 68.7 %collective-permute-start.40 = (bf16[2,192,1792]{2,1,0:T(8,128)(2,1)}, bf16[2,192,1792]{2,1,0:T(8,128)(2,1)}, u32[]{:S(2)}, u32[]{:S(2)}) collective-permute-start(bf16[2,192,1792]{2,1,0:T(8,128)(2,1)} %fusion.38), channel_id=1, source_target_pairs={{0,8},{4,12},{8,0},{12,4},{16,24},{20,28},{24,16},{28,20},{1,9},{5... | collective-permute-start | bytes 4128776 | tf_op jit(solution)/shard_map/ppermute | solution.py:454
  366.9 78.4 %collective-permute-start.31 = (bf16[4,192,1792]{2,1,0:T(8,128)(2,1)}, bf16[4,192,1792]{2,1,0:T(8,128)(2,1)}, u32[]{:S(2)}, u32[]{:S(2)}) collective-permute-start(bf16[4,192,1792]{2,1,0:T(8,128)(2,1)} %get-tuple-element.249), channel_id=1, source_target_pairs={{0,4},{4,0},{8,12},{12,8},{16,20},{20,16},{24,28},{28,24},{1,5},{5... | collective-permute-start | bytes 8257544 | tf_op jit(solution)/shard_map/ppermute | solution.py:454
  390.5 14.2 %collective-permute-start.37 = (bf16[2,256,1152]{2,1,0:T(8,128)(2,1)}, bf16[2,256,1152]{2,1,0:T(8,128)(2,1)S(1)}, u32[]{:S(2)}, u32[]{:S(2)}) collective-permute-start(bf16[2,256,1152]{2,1,0:T(8,128)(2,1)} %get-tuple-element.262), channel_id=1, source_target_pairs={{0,1},{1,0},{2,3},{3,2},{4,5},{5,4},{6,7},{7,6},{8,9},{9,8},{10,11... | collective-permute-start | bytes 3538952 | tf_op jit(solution)/shard_map/ppermute | solution.py:42
  390.5 17.0 %collective-permute-start.36 = (bf16[2,256,1152]{2,1,0:T(8,128)(2,1)}, bf16[2,256,1152]{2,1,0:T(8,128)(2,1)S(1)}, u32[]{:S(2)}, u32[]{:S(2)}) collective-permute-start(bf16[2,256,1152]{2,1,0:T(8,128)(2,1)} %get-tuple-element.261), channel_id=1, source_target_pairs={{0,1},{1,0},{2,3},{3,2},{4,5},{5,4},{6,7},{7,6},{8,9},{9,8},{10,11... | collective-permute-start | bytes 3538952 | tf_op jit(solution)/shard_map/ppermute | solution.py:42
  400.5 50.5 %collective-permute-start.49 = (f32[3,8,1536]{2,1,0:T(8,128)S(1)}, f32[3,8,1536]{2,1,0:T(8,128)S(1)}, u32[]{:S(2)}, u32[]{:S(2)}) collective-permute-start(f32[3,8,1536]{2,1,0:T(8,128)S(1)} %slice.254), channel_id=1, source_target_pairs={{4,0},{8,4},{12,8},{16,12},{20,16},{24,20},{28,24},{5,1},{9,5},{13... | collective-permute-start | bytes 442376 | tf_op jit(solution)/shard_map/ppermute | solution.py:53
  406.3 24.7 %collective-permute-start.41 = (bf16[256,1536]{1,0:T(8,128)(2,1)S(1)}, bf16[256,1536]{1,0:T(8,128)(2,1)S(1)}, u32[]{:S(2)}, u32[]{:S(2)}) collective-permute-start(bf16[256,1536]{1,0:T(8,128)(2,1)S(1)} %fusion.12), channel_id=1, source_target_pairs={{0,2},{1,3},{2,0},{3,1},{4,6},{5,7},{6,4},{7,5},{8,10},{9,11},{10,... | collective-permute-start | bytes 2359304 | tf_op jit(solution)/shard_map/ppermute | solution.py:47
  409.7 33.2 %collective-permute-start.39 = (bf16[256,1536]{1,0:T(8,128)(2,1)}, bf16[256,1536]{1,0:T(8,128)(2,1)}, u32[]{:S(2)}, u32[]{:S(2)}) collective-permute-start(bf16[256,1536]{1,0:T(8,128)(2,1)} %fusion.13.refs_5_), channel_id=1, source_target_pairs={{0,2},{1,3},{2,0},{3,1},{4,6},{5,7},{6,4},{7,5},{8,10},{9,11},{10,... | collective-permute-start | bytes 2359304 | tf_op jit(solution)/shard_map/ppermute | solution.py:47
  451.1 5.4 collective-permute-start.50
  451.2 44.2 %collective-permute-start.43 = (bf16[2,192,1792]{2,1,0:T(8,128)(2,1)}, bf16[2,192,1792]{2,1,0:T(8,128)(2,1)}, u32[]{:S(2)}, u32[]{:S(2)}) collective-permute-start(bf16[2,192,1792]{2,1,0:T(8,128)(2,1)} %fusion.39), channel_id=1, source_target_pairs={{0,4},{4,0},{8,12},{12,8},{16,20},{20,16},{24,28},{28,24},{1,5},{5... | collective-permute-start | bytes 4128776 | tf_op jit(solution)/shard_map/ppermute | solution.py:454
  453.6 82.6 %collective-permute-start.47 = (bf16[4,192,1152]{2,1,0:T(8,128)(2,1)}, bf16[4,192,1152]{2,1,0:T(8,128)(2,1)}, u32[]{:S(2)}, u32[]{:S(2)}) collective-permute-start(bf16[4,192,1152]{2,1,0:T(8,128)(2,1)} %get-tuple-element.287), channel_id=1, source_target_pairs={{0,4},{4,0},{8,12},{12,8},{16,20},{20,16},{24,28},{28,24},{1,5},{5... | collective-permute-start | bytes 5308424 | tf_op jit(solution)/shard_map/ppermute | solution.py:454
  453.7 31.2 %collective-permute-start.45 = (bf16[1536,384]{1,0:T(8,128)(2,1)S(1)}, bf16[1536,384]{1,0:T(8,128)(2,1)}, u32[]{:S(2)}, u32[]{:S(2)}) collective-permute-start(bf16[1536,384]{1,0:T(8,128)(2,1)S(1)} %convolution_convert_fusion.refs_7_), channel_id=1, source_target_pairs={{0,1},{1,0},{2,3},{3,2},{4,5},{5,4},{6,7},{7,6},{8,9},{9,8},{10,11... | collective-permute-start | bytes 3538952 | tf_op jit(solution)/shard_map/ppermute | solution.py:42
  453.9 38.5 %collective-permute-start.44 = (bf16[1,192,1792]{2,1,0:T(8,128)(2,1)}, bf16[1,192,1792]{2,1,0:T(8,128)(2,1)S(1)}, u32[]{:S(2)}, u32[]{:S(2)}) collective-permute-start(bf16[1,192,1792]{2,1,0:T(8,128)(2,1)} %fusion.49), channel_id=1, source_target_pairs={{0,16},{4,20},{8,24},{12,28},{16,0},{20,4},{24,8},{28,12},{1,17},{... | collective-permute-start | bytes 2064392 | tf_op jit(solution)/shard_map/ppermute | solution.py:454
  456.5 26.6 %collective-permute-start.51 = (f32[3,8,1536]{2,1,0:T(8,128)S(1)}, f32[3,8,1536]{2,1,0:T(8,128)S(1)}, u32[]{:S(2)}, u32[]{:S(2)}) collective-permute-start(f32[3,8,1536]{2,1,0:T(8,128)S(1)} %add.753), channel_id=1, source_target_pairs={{0,2},{1,3},{2,0},{3,1},{4,6},{5,7},{6,4},{7,5},{8,10},{9,11},{10,... | collective-permute-start | bytes 442376 | tf_op jit(solution)/shard_map/ppermute | solution.py:799
  483.1 48.7 %collective-permute-start.48 = (bf16[2,192,1792]{2,1,0:T(8,128)(2,1)}, bf16[2,192,1792]{2,1,0:T(8,128)(2,1)S(1)}, u32[]{:S(2)}, u32[]{:S(2)}) collective-permute-start(bf16[2,192,1792]{2,1,0:T(8,128)(2,1)} %fusion.40), channel_id=1, source_target_pairs={{0,8},{4,12},{8,0},{12,4},{16,24},{20,28},{24,16},{28,20},{1,9},{5... | collective-permute-start | bytes 4128776 | tf_op jit(solution)/shard_map/ppermute | solution.py:454
  484.9 58.2 %collective-permute-start.42 = (bf16[3,256,1536]{2,1,0:T(8,128)(2,1)}, bf16[3,256,1536]{2,1,0:T(8,128)(2,1)S(1)}, u32[]{:S(2)}, u32[]{:S(2)}) collective-permute-start(bf16[3,256,1536]{2,1,0:T(8,128)(2,1)} %bitcast.353), channel_id=1, source_target_pairs={{0,2},{1,3},{2,0},{3,1},{4,6},{5,7},{6,4},{7,5},{8,10},{9,11},{10,... | collective-permute-start | bytes 7077896 | tf_op jit(solution)/shard_map/ppermute | solution.py:47
  497.2 42.8 %collective-permute-start.46 = (bf16[1,192,1792]{2,1,0:T(8,128)(2,1)S(1)}, bf16[1,192,1792]{2,1,0:T(8,128)(2,1)S(1)}, u32[]{:S(2)}, u32[]{:S(2)}) collective-permute-start(bf16[1,192,1792]{2,1,0:T(8,128)(2,1)S(1)} %fusion.44), channel_id=1, source_target_pairs={{0,16},{4,20},{8,24},{12,28},{16,0},{20,4},{24,8},{28,12},{1,17},{... | collective-permute-start | bytes 2064392 | tf_op jit(solution)/shard_map/ppermute | solution.py:454
  497.6 48.5 %collective-permute-start.56 = (bf16[4,192,384]{2,1,0:T(8,128)(2,1)}, bf16[4,192,384]{2,1,0:T(8,128)(2,1)}, u32[]{:S(2)}, u32[]{:S(2)}) collective-permute-start(bf16[4,192,384]{2,1,0:T(8,128)(2,1)} %get-tuple-element.356), channel_id=1, source_target_pairs={{0,4},{4,0},{8,12},{12,8},{16,20},{20,16},{24,28},{28,24},{1,5},{5... | collective-permute-start | bytes 1769480 | tf_op jit(solution)/shard_map/ppermute | solution.py:454
  534.5 33.5 %collective-permute-start.55 = (bf16[1,192,1792]{2,1,0:T(8,128)(2,1)}, bf16[1,192,1792]{2,1,0:T(8,128)(2,1)}, u32[]{:S(2)}, u32[]{:S(2)}) collective-permute-start(bf16[1,192,1792]{2,1,0:T(8,128)(2,1)} %fusion.43), channel_id=1, source_target_pairs={{0,16},{4,20},{8,24},{12,28},{16,0},{20,4},{24,8},{28,12},{1,17},{... | collective-permute-start | bytes 2064392 | tf_op jit(solution)/shard_map/ppermute | solution.py:454
  537.6 36.7 %collective-permute-start.54 = (bf16[2,192,1152]{2,1,0:T(8,128)(2,1)S(1)}, bf16[2,192,1152]{2,1,0:T(8,128)(2,1)S(1)}, u32[]{:S(2)}, u32[]{:S(2)}) collective-permute-start(bf16[2,192,1152]{2,1,0:T(8,128)(2,1)S(1)} %fusion.63), channel_id=1, source_target_pairs={{0,8},{4,12},{8,0},{12,4},{16,24},{20,28},{24,16},{28,20},{1,9},{5... | collective-permute-start | bytes 2654216 | tf_op jit(solution)/shard_map/ppermute | solution.py:454
  541.8 1.3 collective-permute-start.52
  547.2 35.3 %collective-permute-start.58 = (bf16[2,192,384]{2,1,0:T(8,128)(2,1)S(1)}, bf16[2,192,384]{2,1,0:T(8,128)(2,1)S(1)}, u32[]{:S(2)}, u32[]{:S(2)}) collective-permute-start(bf16[2,192,384]{2,1,0:T(8,128)(2,1)S(1)} %fusion.90), channel_id=1, source_target_pairs={{0,8},{4,12},{8,0},{12,4},{16,24},{20,28},{24,16},{28,20},{1,9},{5... | collective-permute-start | bytes 884744 | tf_op jit(solution)/shard_map/ppermute | solution.py:454
  574.3 4.1 collective-permute-start.53
  576.6 24.9 %collective-permute-start.60 = (bf16[1,192,1152]{2,1,0:T(8,128)(2,1)S(1)}, bf16[1,192,1152]{2,1,0:T(8,128)(2,1)S(1)}, u32[]{:S(2)}, u32[]{:S(2)}) collective-permute-start(bf16[1,192,1152]{2,1,0:T(8,128)(2,1)S(1)} %fusion.65), channel_id=1, source_target_pairs={{0,16},{4,20},{8,24},{12,28},{16,0},{20,4},{24,8},{28,12},{1,17},{... | collective-permute-start | bytes 1327112 | tf_op jit(solution)/shard_map/ppermute | solution.py:454
  578.4 4.2 collective-permute-start.57
  583.5 7.1 %collective-permute-start.59 = (f32[5,1536]{1,0:T(8,128)S(1)}, f32[5,1536]{1,0:T(8,128)S(1)}, u32[]{:S(2)}, u32[]{:S(2)}) collective-permute-start(f32[5,1536]{1,0:T(8,128)S(1)} %add.784), channel_id=1, source_target_pairs={{0,8},{4,12},{8,0},{12,4},{16,24},{20,28},{24,16},{28,20},{1,9},{5... | collective-permute-start | bytes 92168 | tf_op jit(solution)/shard_map/ppermute | solution.py:853
  588.9 14.7 %collective-permute-start.62 = (bf16[1,192,384]{2,1,0:T(8,128)(2,1)S(1)}, bf16[1,192,384]{2,1,0:T(8,128)(2,1)S(1)}, u32[]{:S(2)}, u32[]{:S(2)}) collective-permute-start(bf16[1,192,384]{2,1,0:T(8,128)(2,1)S(1)} %fusion.93), channel_id=1, source_target_pairs={{0,16},{4,20},{8,24},{12,28},{16,0},{20,4},{24,8},{28,12},{1,17},{... | collective-permute-start | bytes 442376 | tf_op jit(solution)/shard_map/ppermute | solution.py:454
  603.7 5.0 collective-permute-start.61
  (96 other events, 859.2 us)
